TPU v7x, 32 devices: a whole 2x2x4 slice. The times are simulated.
32 devices in a mesh: rep: 8 (over y, x, core), shard: 4 (over z).
Axes of the slice: x: 2, y: 2, z: 4, core: 2. Of those that a mesh axis runs over, the one named last changes fastest.
Arguments:
- tokens: bfloat16 [16, 2048, 768], P('rep', 'shard'), may hold values from -6 to 6
- cotangent: bfloat16 [16, 2048, 768], P('rep', 'shard'), may hold values from -6 to 6
- lengths: int32 [16], P('rep'), may hold values from 512 to 2048, as said below
- w_qkv: float32 [768, 2304], P('shard', 'rep'), may hold values from -0.21875 to 0.21875
- w_out: float32 [768, 768], P('shard', 'rep'), may hold values from -6 to 6
- w_gate_up: float32 [768, 6144], P('shard', 'rep'), may hold values from -0.21875 to 0.21875
- w_down: float32 [3072, 768], P('shard', 'rep'), may hold values from -0.109375 to 0.109375
- mom_qkv: float32 [768, 2304], P('shard', 'rep'), may hold values from -28 to 28
- mom_out: float32 [768, 768], P('shard', 'rep'), may hold values from -28 to 28
- mom_gate_up: float32 [768, 6144], P('shard', 'rep'), may hold values from -28 to 28
- mom_down: float32 [3072, 768], P('shard', 'rep'), may hold values from -28 to 28
- err_qkv: float32 [8, 768, 2304], P('rep', 'shard'), may hold values from -128 to 128
- err_out: float32 [8, 768, 768], P('rep', 'shard'), may hold values from -32 to 32
- err_gate_up: float32 [8, 768, 6144], P('rep', 'shard'), may hold values from -128 to 128
- err_down: float32 [8, 3072, 768], P('rep', 'shard'), may hold values from -128 to 128
- start_qkv: float32 [4, 2304, 8], P('shard'), may hold values from -6 to 6
- start_out: float32 [4, 768, 8], P('shard'), may hold values from -6 to 6
- start_gate_up: float32 [4, 6144, 8], P('shard'), may hold values from -6 to 6
- start_down: float32 [4, 768, 8], P('shard'), may hold values from -6 to 6
- layer_norm_gains: float32 [2, 768], replicated, may hold values from 0.5 to 1.5
- layer_norm_biases: float32 [2, 768], replicated, may hold values from -4 to 4
- norm_moments: float32 [4, 768], replicated, may hold values from -80 to 80
Outputs:
- mixed_out: bfloat16 [16, 2048, 768], P('rep', 'shard')
- input_grad: float32 [16, 2048, 768], P('rep', 'shard')
- new_qkv: float32 [768, 2304], P('shard', 'rep')
- new_out: float32 [768, 768], P('shard', 'rep')
- new_gate_up: float32 [768, 6144], P('shard', 'rep')
- new_down: float32 [3072, 768], P('shard', 'rep')
- moment_qkv: float32 [768, 2304], P('shard', 'rep')
- moment_out: float32 [768, 768], P('shard', 'rep')
- moment_gate_up: float32 [768, 6144], P('shard', 'rep')
- moment_down: float32 [3072, 768], P('shard', 'rep')
- error_qkv: float32 [8, 768, 2304], P('rep', 'shard')
- error_out: float32 [8, 768, 768], P('rep', 'shard')
- error_gate_up: float32 [8, 768, 6144], P('rep', 'shard')
- error_down: float32 [8, 3072, 768], P('rep', 'shard')
- basis_qkv: float32 [768, 8], P('shard')
- basis_out: float32 [768, 8], P('shard')
- basis_gate_up: float32 [768, 8], P('shard')
- basis_down: float32 [3072, 8], P('shard')
- factor_qkv: float32 [4, 2304, 8], P('shard')
- factor_out: float32 [4, 768, 8], P('shard')
- factor_gate_up: float32 [4, 6144, 8], P('shard')
- factor_down: float32 [4, 768, 8], P('shard')
- norm_moment_new: float32 [4, 768], replicated
- norm_new: float32 [4, 768], replicated
Inputs may be any that keep to these rules, and one draw needn't show every extreme that they name: `lengths`: in each group of 2 consecutive entries, one entry, which one drawn from the seed, equals 2048.
All inputs are finite; a program needn't handle non-finite values.
Results may differ from a plain program's by a relative error of at most 0.03.
Values may be sent and summed in bfloat16 or wider, within the bound.
No kernel may reach another device: no remote copies, remote signals or barrier semaphores. Data moves between devices by JAX's collectives and lax.ppermute only.
A program may use at most 320 MiB of HBM per device.

v0:
```python
import math

import jax
import jax.numpy as jnp
from jax import lax
from jax.sharding import PartitionSpec as P

H = 12
HD = 64
FF = 3072


EPS = 1e-05
ROPE_BASE = 1000.0
MOMENTUM = 0.5
LEARN_RATES = (0.002, 0.1, 0.004, 0.002)
NORM_RATE = 0.01
NEG_FILL = -1e30


def norm_components(values_in, gain, bias):
    centre = jnp.mean(values_in, axis=-1, keepdims=True)
    centred = values_in - centre
    spread = jnp.mean(centred * centred, axis=-1, keepdims=True)
    row_rstd = lax.rsqrt(spread + EPS)
    normed = centred * row_rstd
    return (normed * gain + bias, normed, row_rstd)


def norm_reverse_pass(grad_in, normed, row_rstd):
    return row_rstd * (
        grad_in
        - jnp.mean(grad_in, axis=-1, keepdims=True)
        - normed * jnp.mean(grad_in * normed, axis=-1, keepdims=True)
    )


def rotary(values_in, cosine_table, sine_table):
    half_dim = values_in.shape[-1] // 2
    leading_half = values_in[..., :half_dim]
    second_half = values_in[..., half_dim:]
    return jnp.concatenate(
        [
            leading_half * cosine_table - second_half * sine_table,
            second_half * cosine_table + leading_half * sine_table,
        ],
        axis=-1,
    )


def rotary_back(grad_in, cosine_table, sine_table):
    half_dim = grad_in.shape[-1] // 2
    leading_half = grad_in[..., :half_dim]
    second_half = grad_in[..., half_dim:]
    return jnp.concatenate(
        [
            leading_half * cosine_table + second_half * sine_table,
            second_half * cosine_table - leading_half * sine_table,
        ],
        axis=-1,
    )


def orthonormal(factor):
    columns = []
    for column in range(factor.shape[1]):
        vector = factor[:, column]
        for earlier in columns:
            vector = vector - jnp.sum(earlier * vector) * earlier
        vector = vector * lax.rsqrt(jnp.sum(vector * vector) + 1e-06)
        columns.append(vector)
    return jnp.stack(columns, axis=1)


def per_device(
    tokens,
    cotangent,
    lengths,
    w_qkv,
    w_out,
    w_gate_up,
    w_down,
    mom_qkv,
    mom_out,
    mom_gate_up,
    mom_down,
    err_qkv,
    err_out,
    err_gate_up,
    err_down,
    start_qkv,
    start_out,
    start_gate_up,
    start_down,
    layer_norm_gains,
    layer_norm_biases,
    norm_moments,
):
    single_float = jnp.float32
    bf16 = jnp.bfloat16
    wide_cols = (
        lax.all_gather(w_qkv.astype(bf16), "rep", axis=1, tiled=True),
        lax.all_gather(w_out.astype(bf16), "rep", axis=1, tiled=True),
        lax.all_gather(w_gate_up.astype(bf16), "rep", axis=1, tiled=True),
        lax.all_gather(w_down.astype(bf16), "rep", axis=1, tiled=True),
    )
    complete_query_key_value, complete_out_weight, complete_gate_up_weight, complete_down_weight = (
        lax.all_gather(wide_cols[0], "shard", axis=0, tiled=True),
        lax.all_gather(wide_cols[1], "shard", axis=0, tiled=True),
        lax.all_gather(wide_cols[2], "shard", axis=0, tiled=True),
        lax.all_gather(wide_cols[3], "shard", axis=0, tiled=True),
    )
    groups, local_len, model_width = tokens.shape
    shards = lax.axis_size("shard")
    seq_len = local_len * shards
    score_scale = HD ** (-0.5)
    offset = lax.axis_index("shard") * local_len
    position = offset + jnp.arange(local_len, dtype=jnp.int32)
    valid_rows = position[None, :] < lengths[:, None]
    key_keep = jnp.arange(seq_len, dtype=jnp.int32)[None, :] < lengths[:, None]
    inverse = jnp.exp(
        jnp.arange(HD // 2, dtype=jnp.int32).astype(single_float)
        * (-2.0 * math.log(ROPE_BASE) / HD)
    )
    angle = position.astype(single_float)[:, None] * inverse[None, :]
    cosine_table = jnp.cos(angle)[:, None, :]
    sine_table = jnp.sin(angle)[:, None, :]
    query_key_value_rows = jnp.einsum(
        "znk,kb->znb", tokens, complete_query_key_value, preferred_element_type=single_float
    )
    query_key_value_rows = query_key_value_rows.reshape(groups, local_len, 3, H, HD)
    q_half = (
        rotary(query_key_value_rows[:, :, 0], cosine_table, sine_table)
        .astype(bf16)
        .transpose(2, 0, 1, 3)
    )
    k_half = (
        rotary(query_key_value_rows[:, :, 1], cosine_table, sine_table)
        .astype(bf16)
        .transpose(2, 0, 1, 3)
    )
    v_half = query_key_value_rows[:, :, 2].astype(bf16).transpose(2, 0, 1, 3)
    key_all, value_all = (
        lax.all_gather(k_half, "shard", axis=2, tiled=True),
        lax.all_gather(v_half, "shard", axis=2, tiled=True),
    )

    def head_forward(inputs):
        query_h, key_h, value_h = inputs
        scores = (
            jnp.einsum("sqd,skd->sqk", query_h, key_h, preferred_element_type=single_float)
            * score_scale
        )
        scores = jnp.where(key_keep[:, None, :], scores, NEG_FILL)
        row_peak = jnp.max(scores, axis=-1, keepdims=True)
        exp_scores = jnp.exp(scores - row_peak)
        row_total = jnp.sum(exp_scores, axis=-1, keepdims=True)
        attn_probs = (exp_scores / row_total).astype(bf16)
        head_rows = jnp.einsum(
            "sqk,skd->sqd", attn_probs, value_h, preferred_element_type=single_float
        )
        return (head_rows, (row_peak + jnp.log(row_total))[..., 0])

    head_out, log_total = lax.map(head_forward, (q_half, key_all, value_all))
    mix_half = head_out.astype(bf16)
    mixture_rows = mix_half.transpose(1, 2, 0, 3).reshape(groups, local_len, model_width)
    attention_result = jnp.einsum(
        "znk,kb->znb", mixture_rows, complete_out_weight, preferred_element_type=single_float
    )
    attention_normed, attention_standardized, attention_inverse_deviation = norm_components(
        tokens.astype(single_float) + attention_result, layer_norm_gains[0], layer_norm_biases[0]
    )
    leading_half = attention_normed.astype(bf16)
    gate_up_output = jnp.einsum(
        "znk,kb->znb", leading_half, complete_gate_up_weight, preferred_element_type=single_float
    )
    gate_part = gate_up_output[..., :FF]
    up_part = gate_up_output[..., FF:]
    gate_sig = jax.nn.sigmoid(gate_part)
    hidden_state = (gate_part * gate_sig * up_part).astype(bf16)
    residual_branch = jnp.einsum(
        "ckh,hy->cky", hidden_state, complete_down_weight, preferred_element_type=single_float
    )
    feedforward_normed, feedforward_standardized, feedforward_inverse_deviation = norm_components(
        attention_normed + residual_branch, layer_norm_gains[1], layer_norm_biases[1]
    )
    mixed_out = feedforward_normed.astype(bf16)
    output_gradient = cotangent.astype(single_float) * valid_rows[..., None].astype(single_float)
    feedforward_gain = jnp.sum(output_gradient * feedforward_standardized, axis=(0, 1))
    bias_two = jnp.sum(output_gradient, axis=(0, 1))
    trailing_norm_gradient = norm_reverse_pass(
        output_gradient * layer_norm_gains[1],
        feedforward_standardized,
        feedforward_inverse_deviation,
    )
    branch_gradient = trailing_norm_gradient.astype(bf16)
    down_weight_gradient = jnp.einsum(
        "zxi,zxp->ip", hidden_state, branch_gradient, preferred_element_type=single_float
    )
    hidden_gradient = jnp.einsum(
        "gbz,wz->gbw", branch_gradient, complete_down_weight, preferred_element_type=single_float
    )
    grad_gate = hidden_gradient * up_part * gate_sig * (1.0 + gate_part * (1.0 - gate_sig))
    grad_up = hidden_gradient * gate_part * gate_sig
    gate_up_gradient = jnp.concatenate([grad_gate, grad_up], axis=-1).astype(bf16)
    gate_up_weight_gradient = jnp.einsum(
        "vcm,vcb->mb", leading_half, gate_up_gradient, preferred_element_type=single_float
    )
    leading_norm_gradient = (
        jnp.einsum(
            "thi,ci->thc",
            gate_up_gradient,
            complete_gate_up_weight,
            preferred_element_type=single_float,
        )
        + trailing_norm_gradient
    )
    attention_gain = jnp.sum(leading_norm_gradient * attention_standardized, axis=(0, 1))
    bias_one = jnp.sum(leading_norm_gradient, axis=(0, 1))
    attention_gradient = norm_reverse_pass(
        leading_norm_gradient * layer_norm_gains[0],
        attention_standardized,
        attention_inverse_deviation,
    )
    attention_gradient_half = attention_gradient.astype(bf16)
    out_weight_gradient = jnp.einsum(
        "vcm,vcb->mb", mixture_rows, attention_gradient_half, preferred_element_type=single_float
    )
    mixture_gradient = jnp.einsum(
        "thi,ci->thc",
        attention_gradient_half,
        complete_out_weight,
        preferred_element_type=single_float,
    )
    grad_mix_half = (
        mixture_gradient.astype(bf16).reshape(groups, local_len, H, HD).transpose(2, 0, 1, 3)
    )

    def head_back(inputs):
        query_h, key_h, value_h, grad_h, lse_h = inputs
        scores = (
            jnp.einsum("sqd,skd->sqk", query_h, key_h, preferred_element_type=single_float)
            * score_scale
        )
        scores = jnp.where(key_keep[:, None, :], scores, NEG_FILL)
        attn_probs = jnp.exp(scores - lse_h[..., None])
        grad_probs = jnp.einsum(
            "sqd,skd->sqk", grad_h, value_h, preferred_element_type=single_float
        )
        row_delta = jnp.sum(grad_probs * attn_probs, axis=-1, keepdims=True)
        grad_scores = (attn_probs * (grad_probs - row_delta)).astype(bf16)
        grad_query = (
            jnp.einsum("sqk,skd->sqd", grad_scores, key_h, preferred_element_type=single_float)
            * score_scale
        )
        grad_key = (
            jnp.einsum("sqk,sqd->skd", grad_scores, query_h, preferred_element_type=single_float)
            * score_scale
        )
        grad_value = jnp.einsum(
            "sqk,sqd->skd", attn_probs.astype(bf16), grad_h, preferred_element_type=single_float
        )
        return (grad_query, grad_key, grad_value)

    grad_q_heads, key_parts, value_parts = lax.map(
        head_back, (q_half, key_all, value_all, grad_mix_half, log_total)
    )
    grad_k_heads, grad_v_heads = (
        lax.psum_scatter(key_parts, "shard", scatter_dimension=2, tiled=True),
        lax.psum_scatter(value_parts, "shard", scatter_dimension=2, tiled=True),
    )
    grad_q_rows = rotary_back(grad_q_heads.transpose(1, 2, 0, 3), cosine_table, sine_table)
    grad_k_rows = rotary_back(grad_k_heads.transpose(1, 2, 0, 3), cosine_table, sine_table)
    grad_v_rows = grad_v_heads.transpose(1, 2, 0, 3)
    query_key_value_gradient = jnp.stack([grad_q_rows, grad_k_rows, grad_v_rows], axis=2)
    query_key_value_gradient = query_key_value_gradient.reshape(
        groups, local_len, 3 * model_width
    ).astype(bf16)
    query_key_value_weight_gradient = jnp.einsum(
        "vcm,vcb->mb", tokens, query_key_value_gradient, preferred_element_type=single_float
    )
    input_grad = (
        jnp.einsum(
            "thi,ci->thc",
            query_key_value_gradient,
            complete_query_key_value,
            preferred_element_type=single_float,
        )
        + attention_gradient
    )
    owned = (
        lax.psum_scatter(
            query_key_value_weight_gradient.astype(jnp.bfloat16),
            "shard",
            scatter_dimension=0,
            tiled=True,
        ).astype(jnp.float32),
        lax.psum_scatter(
            out_weight_gradient.astype(jnp.bfloat16), "shard", scatter_dimension=0, tiled=True
        ).astype(jnp.float32),
        lax.psum_scatter(
            gate_up_weight_gradient.astype(jnp.bfloat16), "shard", scatter_dimension=0, tiled=True
        ).astype(jnp.float32),
        lax.psum_scatter(
            down_weight_gradient.astype(jnp.bfloat16), "shard", scatter_dimension=0, tiled=True
        ).astype(jnp.float32),
    )
    replicas = lax.axis_size("rep")
    vector_parts = jnp.stack([attention_gain, bias_one, feedforward_gain, bias_two])
    norm_grad = lax.psum(vector_parts, ("rep", "shard")) / replicas
    params = jnp.stack(
        [layer_norm_gains[0], layer_norm_biases[0], layer_norm_gains[1], layer_norm_biases[1]]
    )
    norm_moment_new = MOMENTUM * norm_moments + norm_grad
    norm_new = params - NORM_RATE * norm_moment_new
    errors = (err_qkv, err_out, err_gate_up, err_down)
    starts = (start_qkv, start_out, start_gate_up, start_down)
    masters = (w_qkv, w_out, w_gate_up, w_down)
    moments = (mom_qkv, mom_out, mom_gate_up, mom_down)
    merged = tuple((part + error_set[0] for part, error_set in zip(owned, errors)))
    projected = tuple(
        (
            jnp.dot(block, start_set[0], precision=lax.Precision.HIGHEST)
            for block, start_set in zip(merged, starts)
        )
    )
    summed_left = lax.psum((projected[0], projected[1], projected[2], projected[3]), "rep")
    bases = tuple((orthonormal(part / replicas) for part in summed_left))
    pulled = tuple(
        (
            jnp.einsum("rc,rk->ck", block, basis, precision=lax.Precision.HIGHEST)
            for block, basis in zip(merged, bases)
        )
    )
    summed_right = (
        lax.psum(pulled[0].astype(jnp.bfloat16), "rep").astype(jnp.float32),
        lax.psum(pulled[1].astype(jnp.bfloat16), "rep").astype(jnp.float32),
        lax.psum(pulled[2].astype(jnp.bfloat16), "rep").astype(jnp.float32),
        lax.psum(pulled[3].astype(jnp.bfloat16), "rep").astype(jnp.float32),
    )
    factors = tuple((part / replicas for part in summed_right))
    rep_pos = lax.axis_index("rep")
    new_weights = []
    new_moments = []
    new_errors = []
    for block, basis, factor, master, moment, step_rate in zip(
        merged, bases, factors, masters, moments, LEARN_RATES
    ):
        approx = jnp.dot(basis, factor.T, precision=lax.Precision.HIGHEST)
        new_errors.append((block - approx)[None])
        col_count = master.shape[1]
        piece = lax.dynamic_slice_in_dim(approx, rep_pos * col_count, col_count, 1)
        moment_new = MOMENTUM * moment + piece
        new_moments.append(moment_new)
        new_weights.append(master - step_rate * moment_new)
    return (
        mixed_out,
        input_grad,
        new_weights[0],
        new_weights[1],
        new_weights[2],
        new_weights[3],
        new_moments[0],
        new_moments[1],
        new_moments[2],
        new_moments[3],
        new_errors[0],
        new_errors[1],
        new_errors[2],
        new_errors[3],
        bases[0],
        bases[1],
        bases[2],
        bases[3],
        factors[0][None],
        factors[1][None],
        factors[2][None],
        factors[3][None],
        norm_moment_new,
        norm_new,
    )


def solution(mesh):
    placed = (
        P("rep", "shard", None),
        P("rep", "shard", None),
        P("rep"),
        P("shard", "rep"),
        P("shard", "rep"),
        P("shard", "rep"),
        P("shard", "rep"),
        P("shard", "rep"),
        P("shard", "rep"),
        P("shard", "rep"),
        P("shard", "rep"),
        P("rep", "shard", None),
        P("rep", "shard", None),
        P("rep", "shard", None),
        P("rep", "shard", None),
        P("shard", None, None),
        P("shard", None, None),
        P("shard", None, None),
        P("shard", None, None),
        P(),
        P(),
        P(),
    )
    return jax.shard_map(
        per_device,
        mesh=mesh,
        in_specs=placed,
        out_specs=(
            P("rep", "shard", None),
            P("rep", "shard", None),
            P("shard", "rep"),
            P("shard", "rep"),
            P("shard", "rep"),
            P("shard", "rep"),
            P("shard", "rep"),
            P("shard", "rep"),
            P("shard", "rep"),
            P("shard", "rep"),
            P("rep", "shard", None),
            P("rep", "shard", None),
            P("rep", "shard", None),
            P("rep", "shard", None),
            P("shard", None),
            P("shard", None),
            P("shard", None),
            P("shard", None),
            P("shard", None, None),
            P("shard", None, None),
            P("shard", None, None),
            P("shard", None, None),
            P(),
            P(),
        ),
        check_vma=False,
    )
```

profile of v0, /device:TPU:16, one launch (start us, length us, event | category | flops | bytes accessed | tf_op | source)
XLA Modules:
  0.0 2103.5 jit_solution(1400203427132746241)
XLA Ops:
  8.4 11.6 all_gather.30
  23.4 66.9 %all-gather.9.cloned.1.call-done = bf16[768,2304]{1,0:T(8,128)(2,1)} async-done(((bf16[192,2304]{1,0:T(8,128)(2,1)}), bf16[768,2304]{1,0:T(8,128)(2,1)}) %all-gather.9.cloned.1.call-update) | async-done | bytes 3538960 | tf_op jit(solution)/shard_map/all_gather | solution.py:108
  106.8 10.3 all_gather.34
  123.8 25.0 %all-gather.21.cloned.1.call-done = bf16[768,768]{0,1:T(8,128)(2,1)} async-done(((bf16[768,96]{0,1:T(8,128)(2,1)}), bf16[768,768]{0,1:T(8,128)(2,1)}) %all-gather.21.cloned.1.call-update) | async-done | bytes 1179664 | tf_op jit(solution)/shard_map/all_gather | solution.py:105
  152.0 112.4 %all-gather.11.cloned.1.call-done = bf16[12,2,2048,64]{2,3,0,1:T(8,128)(2,1)} async-done(((bf16[12,2,512,64]{2,3,0,1:T(8,128)(2,1)}), bf16[12,2,2048,64]{2,3,0,1:T(8,128)(2,1)}) %all-gather.11.cloned.1.call-update) | async-done | bytes 6291472 | tf_op jit(solution)/shard_map/all_gather | solution.py:144
  264.4 6.7 copy.89
  271.1 108.9 %all-gather.13.cloned.1.call-done = bf16[12,2,2048,64]{2,3,0,1:T(8,128)(2,1)} async-done(((bf16[12,2,512,64]{2,3,0,1:T(8,128)(2,1)}), bf16[12,2,2048,64]{2,3,0,1:T(8,128)(2,1)}) %all-gather.13.cloned.1.call-update) | async-done | bytes 6291472 | tf_op jit(solution)/shard_map/all_gather | solution.py:145
  386.5 93.0 %while.30 = (s32[]{:T(128)}, bf16[12,2,512,64]{2,3,0,1:T(8,128)(2,1)S(1)}, f32[12,2,512]{2,1,0:T(2,128)S(1)}, bf16[12,2,512,64]{2,3,1,0:T(8,128)(2,1)S(1)}, bf16...) while((s32[]{:T(128)}, ...), condition=%wide.region_3.4_spmd.clone.clone, body=%wide.region_0.3_spmd.clone.sunk.clone | while | flops 562039808 | bytes 26667096 | solution.py:164
  485.5 92.6 %all-gather.19.cloned.1.call-done = bf16[768,6144]{1,0:T(8,128)(2,1)} async-done(((bf16[192,6144]{1,0:T(8,128)(2,1)}), bf16[768,6144]{1,0:T(8,128)(2,1)}) %all-gather.19.cloned.1.call-update) | async-done | bytes 9437200 | tf_op jit(solution)/shard_map/all_gather | solution.py:110
  578.1 17.1 fusion.59
  595.3 12.8 multiply_convert_fusion.3
  608.1 60.0 %all-gather.23.cloned.1.call-done = bf16[3072,768]{1,0:T(8,128)(2,1)} async-done(((bf16[768,768]{1,0:T(8,128)(2,1)}), bf16[3072,768]{1,0:T(8,128)(2,1)}) %all-gather.23.cloned.1.call-update) | async-done | bytes 4718608 | tf_op jit(solution)/shard_map/all_gather | solution.py:111
  668.1 9.4 fusion.123
  683.8 18.8 multiply_convert_fusion.2
  702.7 18.8 multiply_reduce_fusion.2
  728.0 206.8 %while.31 = (s32[]{:T(128)}, f32[12,2,512,64]{2,3,0,1:T(8,128)}, f32[12,2,2048,64]{2,3,0,1:T(8,128)}, f32[12,2,2048,64]{2,3,0,1:T(8,128)}, bf16[12,2,512,64]{2,3...) while((s32[]{:T(128)}, f32[12,2,512,64]{2,3,0,1:T(8,128)}, ...), condition=%wide.region_14.15_spmd.clone.clone, body=%wide.region_12.14_spmd.clone.sunk.clone | while | flops 1373965312 | bytes 67429488 | solution.py:265
  940.6 10.1 bitcast_convert_fusion.1
  952.7 16.8 bitcast_convert_fusion
  969.6 178.2 %reduce-scatter.9.cloned.1.call-done = f32[12,2,512,64]{2,3,0,1:T(8,128)} async-done(((f32[12,2,2048,64]{2,3,0,1:T(8,128)}), f32[12,2,512,64]{2,3,0,1:T(8,128)}) %reduce-scatter.9.cloned.1.call-update) | async-done | bytes 3145744 | tf_op jit(solution)/shard_map/reduce_scatter | solution.py:269
  1151.0 212.0 %reduce-scatter.11.cloned.1.call-done = f32[12,2,512,64]{2,3,0,1:T(8,128)} async-done(((f32[12,2,2048,64]{2,3,0,1:T(8,128)}), f32[12,2,512,64]{2,3,0,1:T(8,128)}) %reduce-scatter.11.cloned.1.call-update) | async-done | bytes 3145744 | tf_op jit(solution)/shard_map/reduce_scatter | solution.py:270
  1380.3 40.8 %psum.71 = f32[4,768]{1,0:T(4,128)S(1)} all-reduce(f32[4,768]{1,0:T(4,128)S(1)} %pad_maximum_fusion.6), channel_id=1, replica_groups=mesh['rep'=8,'shard'=4] {'rep','shard'}, use_global_device_ids=true, to_apply=%region_177.178 | all-reduce | flops 3072 | bytes 24576 | tf_op jit(solution)/shard_map/psum | solution.py:310
  1423.2 58.2 %reduce-scatter.17.cloned.1.call-done = bf16[768,768]{1,0:T(8,128)(2,1)} async-done(((bf16[3072,768]{1,0:T(8,128)(2,1)}), bf16[768,768]{1,0:T(8,128)(2,1)}) %reduce-scatter.17.cloned.1.call-update) | async-done | bytes 1179664 | tf_op jit(solution)/shard_map/reduce_scatter | solution.py:304
  1484.8 161.2 %reduce-scatter.15.cloned.1.call-done = bf16[192,6144]{1,0:T(8,128)(2,1)} async-done(((bf16[768,6144]{1,0:T(8,128)(2,1)}), bf16[192,6144]{1,0:T(8,128)(2,1)}) %reduce-scatter.15.cloned.1.call-update) | async-done | bytes 2359312 | tf_op jit(solution)/shard_map/reduce_scatter | solution.py:301
  1652.1 7.9 fusion.81
  1660.0 54.9 %reduce-scatter.19.cloned.1.call-done = bf16[192,2304]{1,0:T(8,128)(2,1)} async-done(((bf16[768,2304]{1,0:T(8,128)(2,1)}), bf16[192,2304]{1,0:T(8,128)(2,1)}) %reduce-scatter.19.cloned.1.call-update) | async-done | bytes 884752 | tf_op jit(solution)/shard_map/reduce_scatter | solution.py:292
  1718.0 25.5 %all-reduce = (f32[192,8]{0,1:T(8,128)S(1)}, f32[192,8]{0,1:T(8,128)S(1)}, f32[192,8]{0,1:T(8,128)}, f32[768,8]{0,1:T(8,128)S(1)}) all-reduce(f32[192,8]{0,1:T(8,128)S(1)} %fusion.91, f32[192,8]{0,1:T(8,128)S(1)} %fusion.92, f32[192,8]{0,1:T(8,128)S(1)} %fusion.78, f32[768,8]{0,1:T(8,128)S(1)} %fusion.87), channel_id=1, replica_groups=mesh['rep'=8,'shard'=4] {'rep'}, use_global_device_ids=true, to_apply=%region_18.19 | all-reduce | flops 10752 | bytes 86016 | tf_op jit(solution)/shard_map/psum | solution.py:327
  1828.8 18.6 subtract_multiply_fusion.18
  1890.4 18.0 subtract_multiply_fusion.25
  1908.4 17.5 subtract_multiply_fusion.4
  1932.4 23.9 %all-reduce.1 = (bf16[2304,8]{0,1:T(8,128)(2,1)S(1)}, bf16[768,8]{0,1:T(8,128)(2,1)}, bf16[768,8]{0,1:T(8,128)(2,1)}) all-reduce(bf16[2304,8]{0,1:T(8,128)(2,1)S(1)} %convolution_convert_fusion.1, bf16[768,8]{0,1:T(8,128)(2,1)} %convolution_convert_fusion.4, ...), channel_id=1, replica_groups=mesh['rep'=8,'shard'=4] {'rep'}, use_global_device_ids=true, to_apply=%region_55.56 | all-reduce | flops 30720 | bytes 122880 | tf_op jit(solution)/shard_map/psum | solution.py:336
  2010.1 17.7 subtract_multiply_fusion.11
  2048.8 35.4 %all-reduce.4.cloned.1.call-done = bf16[6144,8]{0,1:T(8,128)(2,1)} async-done(((bf16[6144,8]{0,1:T(8,128)(2,1)}), bf16[6144,8]{0,1:T(8,128)(2,1)}) %all-reduce.4.cloned.1.call-update) | async-done | bytes 98320 | tf_op jit(solution)/shard_map/psum | solution.py:338
  (469 shorter events, 597.4 us)
Async XLA Ops:
  7.2 1638.8 %copy-start = (f32[1,6144,8]{1,2,0:T(8,128)S(1)}, f32[1,6144,8]{1,2,0:T(8,128)}, u32[]{:S(2)}) copy-start(f32[1,6144,8]{1,2,0:T(8,128)} %param.43) | copy-start | bytes 589828
  7.2 83.0 %all-gather.9.cloned.1.call-start = ((), (), s32[]{:S(2)}) async-start(), calls=%async_computation.6 | async-start | bytes 4423680 | tf_op jit(solution)/shard_map/all_gather | solution.py:108
  21.4 100.9 %all-gather.17.cloned.1.call-start = ((), (), s32[]{:S(2)}) async-start(), calls=%async_computation.10 | async-start | bytes 2654208 | tf_op jit(solution)/shard_map/all_gather | solution.py:104
  22.2 126.6 %all-gather.21.cloned.1.call-start = ((), (), s32[]{:S(2)}) async-start(), calls=%async_computation.12 | async-start | bytes 1327104 | tf_op jit(solution)/shard_map/all_gather | solution.py:105
  22.9 241.4 %all-gather.11.cloned.1.call-start = ((), (), s32[]{:S(2)}) async-start(), calls=%async_computation.7 | async-start | bytes 7864320 | tf_op jit(solution)/shard_map/all_gather | solution.py:144
  23.3 77.5 %copy-start.28 = (f32[512,32]{0,1:T(8,128)}, f32[512,32]{0,1:T(8,128)S(1)}, u32[]{:S(2)}) copy-start(f32[512,32]{0,1:T(8,128)S(1)} %get-tuple-element.591) | copy-start | bytes 196612
  23.4 77.5 %copy-start.30 = (f32[512,32]{0,1:T(8,128)}, f32[512,32]{0,1:T(8,128)S(1)}, u32[]{:S(2)}) copy-start(f32[512,32]{0,1:T(8,128)S(1)} %get-tuple-element.592) | copy-start | bytes 196612
  103.2 276.7 %all-gather.13.cloned.1.call-start = ((), (), s32[]{:S(2)}) async-start(), calls=%async_computation.8 | async-start | bytes 7864320 | tf_op jit(solution)/shard_map/all_gather | solution.py:145
  106.6 373.0 %all-gather.15.cloned.1.call-start = ((), (), s32[]{:S(2)}) async-start(), calls=%async_computation.9 | async-start | bytes 1474560 | tf_op jit(solution)/shard_map/all_gather | solution.py:109
  118.0 460.1 %all-gather.19.cloned.1.call-start = ((), (), s32[]{:S(2)}) async-start(), calls=%async_computation.11 | async-start | bytes 11796480 | tf_op jit(solution)/shard_map/all_gather | solution.py:110
  122.3 545.9 %all-gather.23.cloned.1.call-start = ((), (), s32[]{:S(2)}) async-start(), calls=%async_computation.13 | async-start | bytes 5898240 | tf_op jit(solution)/shard_map/all_gather | solution.py:111
  123.8 544.3 %copy-start.56 = (f32[768]{0:T(1024)}, f32[768]{0:T(1024)S(1)}, u32[]{:S(2)}) copy-start(f32[768]{0:T(1024)S(1)} %get-tuple-element.274) | copy-start | bytes 9220
  151.2 996.7 %reduce-scatter.9.cloned.1.call-start = ((), (), s32[]{:S(2)}) async-start(), calls=%async_computation.14 | async-start | bytes 15728640 | tf_op jit(solution)/shard_map/reduce_scatter | solution.py:269
  485.0 110.3 %copy-start.5 = (f32[2,512,768]{2,1,0:T(8,128)}, f32[2,512,768]{2,1,0:T(8,128)S(1)}, u32[]{:S(2)}) copy-start(f32[2,512,768]{2,1,0:T(8,128)S(1)} %get-tuple-element.594) | copy-start | bytes 9437188
  934.8 428.2 %reduce-scatter.11.cloned.1.call-start = ((), (), s32[]{:S(2)}) async-start(), calls=%async_computation.15 | async-start | bytes 15728640 | tf_op jit(solution)/shard_map/reduce_scatter | solution.py:270
  935.4 486.3 %reduce-scatter.13.cloned.1.call-start = ((), (), s32[]{:S(2)}) async-start(), calls=%async_computation.16 | async-start | bytes 1474560 | tf_op jit(solution)/shard_map/reduce_scatter | solution.py:298
  940.6 540.8 %reduce-scatter.17.cloned.1.call-start = ((), (), s32[]{:S(2)}) async-start(), calls=%async_computation.19 | async-start | bytes 5898240 | tf_op jit(solution)/shard_map/reduce_scatter | solution.py:304
  950.8 695.2 %reduce-scatter.15.cloned.1.call-start = ((), (), s32[]{:S(2)}) async-start(), calls=%async_computation.17 | async-start | bytes 11796480 | tf_op jit(solution)/shard_map/reduce_scatter | solution.py:301
  969.5 178.3 %copy-start.21 = (f32[12,2,512,64]{2,3,0,1:T(8,128)S(1)}, f32[12,2,512,64]{2,3,0,1:T(8,128)}, u32[]{:S(2)}) copy-start(f32[12,2,512,64]{2,3,0,1:T(8,128)} %get-tuple-element.118) | copy-start | bytes 9437188
  969.5 178.3 %copy-start.29 = (f32[512,32]{0,1:T(8,128)S(1)}, f32[512,32]{0,1:T(8,128)}, u32[]{:S(2)}) copy-start(f32[512,32]{0,1:T(8,128)} %copy-done.28) | copy-start | bytes 196612
  969.5 178.3 %copy-start.31 = (f32[512,32]{0,1:T(8,128)S(1)}, f32[512,32]{0,1:T(8,128)}, u32[]{:S(2)}) copy-start(f32[512,32]{0,1:T(8,128)} %copy-done.30) | copy-start | bytes 196612
  969.5 745.3 %reduce-scatter.19.cloned.1.call-start = ((), (), s32[]{:S(2)}) async-start(), calls=%async_computation.20 | async-start | bytes 4423680 | tf_op jit(solution)/shard_map/reduce_scatter | solution.py:292
  1379.5 41.5 %copy-start.48 = (f32[4,768]{1,0:T(4,128)S(1)}, f32[4,768]{1,0:T(4,128)}, u32[]{:S(2)}) copy-start(f32[4,768]{1,0:T(4,128)} %param.47) | copy-start | bytes 36868
  1379.6 42.1 %copy-start.15 = (f32[1,192,768]{2,1,0:T(8,128)S(1)}, f32[1,192,768]{2,1,0:T(8,128)}, u32[]{:S(2)}) copy-start(f32[1,192,768]{2,1,0:T(8,128)} %param.38) | copy-start | bytes 1769476
  1379.6 42.1 %copy-start.45 = (f32[1,768,8]{1,2,0:T(8,128)S(1)}, f32[1,768,8]{1,2,0:T(8,128)}, u32[]{:S(2)}) copy-start(f32[1,768,8]{1,2,0:T(8,128)} %param.42) | copy-start | bytes 73732
  1379.6 101.8 %copy-start.1 = (f32[1,768,768]{2,1,0:T(8,128)S(1)}, f32[1,768,768]{2,1,0:T(8,128)}, u32[]{:S(2)}) copy-start(f32[1,768,768]{2,1,0:T(8,128)} %param.40) | copy-start | bytes 7077892
  1379.6 101.8 %copy-start.44 = (f32[1,768,8]{1,2,0:T(8,128)S(1)}, f32[1,768,8]{1,2,0:T(8,128)}, u32[]{:S(2)}) copy-start(f32[1,768,8]{1,2,0:T(8,128)} %param.44) | copy-start | bytes 73732
  1379.7 704.6 %all-reduce.4.cloned.1.call-start = ((), (), s32[]{:S(2)}) async-start(), calls=%async_computation.18 | async-start | bytes 196608 | tf_op jit(solution)/shard_map/psum | solution.py:338
  1652.0 62.8 %copy-start.39 = (f32[1,2304,8]{1,2,0:T(8,128)S(1)}, f32[1,2304,8]{1,2,0:T(8,128)}, u32[]{:S(2)}) copy-start(f32[1,2304,8]{1,2,0:T(8,128)} %param.41) | copy-start | bytes 221188
  1718.0 213.3 %copy-start.12 = (bf16[192,2304]{1,0:T(8,128)(2,1)S(1)}, bf16[192,2304]{1,0:T(8,128)(2,1)}, u32[]{:S(2)}) copy-start(bf16[192,2304]{1,0:T(8,128)(2,1)} %reduce-scatter.19.cloned.1.call-done) | copy-start | bytes 2654212
  1926.7 107.7 %copy-start.37 = (f32[192,8]{0,1:T(8,128)}, f32[192,8]{0,1:T(8,128)S(1)}, u32[]{:S(2)}) copy-start(f32[192,8]{0,1:T(8,128)S(1)} %stack.37) | copy-start | bytes 18436
  2027.8 56.4 %copy-start.40 = (f32[192,8]{0,1:T(8,128)}, f32[192,8]{0,1:T(8,128)S(1)}, u32[]{:S(2)}) copy-start(f32[192,8]{0,1:T(8,128)S(1)} %stack.38) | copy-start | bytes 18436
  (46 other events, 531.5 us)
Sparse Core Ops, SparseCore 0:
  21.5 68.6 all-gather.8
  92.7 29.4 all-gather.16
  124.7 24.0 all-gather.20
  150.8 113.5 all-gather.10
  266.4 113.5 all-gather.12
  381.9 29.5 all-gather.14
  413.1 164.9 all-gather.18
  580.3 87.8 all-gather.22
  934.9 212.8 reduce-scatter.8
  1150.0 212.8 reduce-scatter.10
  1365.3 27.8 reduce-scatter.12
  1395.4 85.9 reduce-scatter.16
  1483.7 162.1 reduce-scatter.14
  1648.2 66.6 reduce-scatter.18
  2034.5 49.6 all-reduce.3
where the time goes:
time: 2120 us; the launch traced here: 2100 us
  waiting for transfers between devices  1170 us (55%)
  matrix products  406 us (19%)
  other arithmetic  325 us (15%)
  blocking collectives  112 us (5%)
  local copies, waits for them, and re-layouts  50.5 us (2%)
  between operations  37.3 us (2%)
    reduce_scatter x1, waiting for transfers between devices, per_device(): lax.psum_scatter(value_parts, 'shard', scatter_dimension=2, tiled=True)  212 us
    reduce_scatter x1, waiting for transfers between devices, per_device(): lax.psum_scatter(key_parts, 'shard', scatter_dimension=2, tiled=True)  178 us
    reduce_scatter x1, waiting for transfers between devices, per_device(): lax.psum_scatter(gate_up_weight_gradient.astype(jnp.bfloat16), 'shard', s...  161 us
    reduce_sum x39, other arithmetic, orthonormal(): vector = vector - jnp.sum(earlier * vector) * earlier  116 us
    all_gather x1, waiting for transfers between devices, per_device(): lax.all_gather(k_half, 'shard', axis=2, tiled=True)  112 us
    all_gather x1, waiting for transfers between devices, per_device(): lax.all_gather(v_half, 'shard', axis=2, tiled=True)  109 us
    all_gather x1, waiting for transfers between devices, per_device(): lax.all_gather(wide_cols[2], 'shard', axis=0, tiled=True)  92.6 us
    mul x5, other arithmetic, orthonormal(): vector = vector * lax.rsqrt(jnp.sum(vector * vector) + 1e-06)  71.8 us
  transfers between devices with their start and end apart: 15, of which 13 were waited for; matrix products, arithmetic and copies ran while one was open for 11% of the time, Pallas kernels for 0%

commit v1 on v0

--- a/solution.py
+++ b/solution.py
@@ -1,8 +1,11 @@
+import functools
 import math
 
 import jax
 import jax.numpy as jnp
 from jax import lax
+from jax.experimental import pallas as pl
+from jax.experimental.pallas import tpu as pltpu
 from jax.sharding import PartitionSpec as P
 
 H = 12
@@ -72,7 +75,7 @@
     return jnp.stack(columns, axis=1)
 
 
-def per_device(
+def general_device(
     tokens,
     cotangent,
     lengths,
@@ -381,6 +384,1256 @@
     )
 
 
+AXES = ("rep", "shard")
+SHARDS = 4
+REPS = 8
+RANK = 8
+DIM = 768
+PAIRS = 6
+LANES = 128
+MIB = 2**20
+
+
+def send(values, move):
+    pairs = []
+    for rep in range(REPS):
+        for shard in range(SHARDS):
+            to = move(rep, shard)
+            if to is not None:
+                pairs.append((rep * SHARDS + shard, to[0] * SHARDS + to[1]))
+    return lax.ppermute(values, AXES, pairs)
+
+
+def spread_move(parity):
+    return lambda r, z: (r - r % 2 + z // 2, 2 * (r % 2) + (z + parity) % 2)
+
+
+def gather_move(parity):
+    table = {}
+    for r in range(REPS):
+        for z in range(SHARDS):
+            table[spread_move(parity)(r, z)] = (r, z)
+    return lambda r, z: table[(r, z)]
+
+
+def sibling(values):
+    return send(values, lambda r, z: (r ^ 1, z))
+
+
+def near_x(values):
+    return send(values, lambda r, z: (r ^ 2, z))
+
+
+def near_y(values):
+    return send(values, lambda r, z: (r ^ 4, z))
+
+
+def pair_z(values):
+    return send(values, lambda r, z: (r, z ^ 1))
+
+
+def mirror_z(values):
+    return send(values, lambda r, z: (r, 3 - z))
+
+
+def to_owner(values):
+    return send(values, lambda r, z: (r ^ 1, 3 - z) if r % 2 != z // 2 else None)
+
+
+def turn_z(values, step):
+    return send(values, lambda r, z: (r, (z + step) % SHARDS))
+
+
+def after(values, *others):
+    return lax.optimization_barrier((values, *others))[0]
+
+
+def shard_gather(piece, shard):
+    parts = jnp.stack([piece] + [turn_z(piece, step) for step in (1, 2, 3)])
+    return [
+        lax.dynamic_index_in_dim(parts, (shard - at) % SHARDS, 0, keepdims=False)
+        for at in range(SHARDS)
+    ]
+
+
+def plane_near(piece):
+    return near_x(piece), near_y(piece)
+
+
+def plane_far(piece, near):
+    half = piece.shape[0] // 2
+    from_x, from_y = near
+    return near_x(from_y[:half]), near_y(from_x[half:])
+
+
+def exchange(piece, near, far):
+    return [sibling(part) for part in (piece, *near, jnp.concatenate(far, axis=0))]
+
+
+def plane_all(piece, near, far, others, rep, ahead=()):
+    return stack_pieces((piece, *near, *far, *others), rep, *piece.shape, ahead)
+
+
+PIECE_STEPS = ((0, None), (2, None), (4, None), (6, 0), (6, 1), (1, None), (3, None), (5, None), (7, None))
+
+
+def stack_kernel(rep_ref, *refs):
+    count = len(PIECE_STEPS)
+    pieces = refs[:count]
+    whole, staged, sems_in, sems_out = refs[-4:]
+    rep = rep_ref[0]
+    half = pieces[3].shape[0]
+    fetches = []
+    stores = []
+    for slot, (step, side) in enumerate(PIECE_STEPS):
+        stage = staged.at[step]
+        place = whole.at[rep ^ step]
+        if side is not None:
+            part = pl.ds(side * half, half)
+            stage = stage.at[part]
+            place = place.at[part]
+        fetches.append(pltpu.make_async_copy(pieces[slot], stage, sems_in.at[slot]))
+        stores.append(pltpu.make_async_copy(stage, place, sems_out.at[slot]))
+    for fetch in fetches:
+        fetch.start()
+    for fetch, store in zip(fetches, stores):
+        fetch.wait()
+        store.start()
+    for store in stores:
+        store.wait()
+
+
+def stack_pieces(pieces, rep, rows, cols, ahead):
+    anywhere = pl.BlockSpec(memory_space=pl.ANY)
+    count = len(pieces)
+    return pl.pallas_call(
+        stack_kernel,
+        in_specs=[pl.BlockSpec(memory_space=pltpu.SMEM)] + [anywhere] * (count + len(ahead)),
+        out_specs=anywhere,
+        out_shape=jax.ShapeDtypeStruct((REPS, rows, cols), pieces[0].dtype),
+        scratch_shapes=[
+            pltpu.VMEM((REPS, rows, cols), pieces[0].dtype),
+            pltpu.SemaphoreType.DMA((count,)),
+            pltpu.SemaphoreType.DMA((count,)),
+        ],
+        compiler_params=limit(40),
+        cost_estimate=pl.CostEstimate(
+            flops=0, bytes_accessed=4 * REPS * rows * cols, transcendentals=0
+        ),
+        name="stack_pieces",
+    )(jnp.reshape(rep, (1,)), *pieces, *ahead)
+
+
+def plane_sum(values):
+    values = values + sibling(values)
+    values = values + near_x(values)
+    return values + near_y(values)
+
+
+def plane_sum_half(values):
+    bf16 = jnp.bfloat16
+    f32 = jnp.float32
+    for step in (sibling, near_x, near_y):
+        rounded = values.astype(bf16)
+        values = rounded.astype(f32) + step(rounded).astype(f32)
+    return values
+
+
+def nt(left, right):
+    return lax.dot_general(
+        left, right, (((1,), (1,)), ((), ())), preferred_element_type=jnp.float32
+    )
+
+
+def nn(left, right):
+    return lax.dot_general(
+        left, right, (((1,), (0,)), ((), ())), preferred_element_type=jnp.float32
+    )
+
+
+def cost(flops, moved, powers=0):
+    return pl.CostEstimate(flops=int(flops), bytes_accessed=int(moved), transcendentals=int(powers))
+
+
+def limit(mib):
+    return pltpu.CompilerParams(vmem_limit_bytes=mib * MIB)
+
+
+def shape(dims, dtype):
+    return jax.ShapeDtypeStruct(dims, dtype)
+
+
+def partner_lanes(values):
+    lane = lax.broadcasted_iota(jnp.int32, values.shape, 1)
+    up = pltpu.roll(values, 96, 1)
+    down = pltpu.roll(values, 32, 1)
+    return jnp.where(lane % HD < HD // 2, up, down)
+
+
+def project_kernel(x_ref, w_ref, cos_ref, sin_ref, out_ref, *, turned, scale):
+    values = nt(x_ref[...], w_ref[...])
+
+    def turn():
+        for at in range(0, values.shape[1], LANES):
+            part = values[:, at : at + LANES]
+            part = part * cos_ref[...] + partner_lanes(part) * sin_ref[...]
+            out_ref[:, at : at + LANES] = (part * scale).astype(out_ref.dtype)
+
+    if turned is None:
+        turn()
+    else:
+        pl.when(pl.program_id(0) < turned)(turn)
+
+        @pl.when(pl.program_id(0) >= turned)
+        def _():
+            out_ref[...] = values.astype(out_ref.dtype)
+
+
+def project(rows_in, qkv_t, cos, sin, first, count, turned, scale):
+    rows = rows_in.shape[0]
+    tile = DIM
+    fixed = lambda j: (0, 0)
+    return pl.pallas_call(
+        functools.partial(project_kernel, turned=turned, scale=scale),
+        grid=(count,),
+        in_specs=[
+            pl.BlockSpec((rows, DIM), fixed),
+            pl.BlockSpec((tile, DIM), lambda j: (j + first, 0)),
+            pl.BlockSpec((rows, LANES), fixed),
+            pl.BlockSpec((rows, LANES), fixed),
+        ],
+        out_specs=pl.BlockSpec((rows, tile), lambda j: (0, j)),
+        out_shape=shape((rows, count * tile), jnp.bfloat16),
+        compiler_params=limit(48),
+        cost_estimate=cost(2 * rows * DIM * tile * count, 4 * rows * DIM + 4 * count * tile * rows),
+        name="project",
+    )(rows_in, qkv_t, cos, sin)
+
+
+def lane_of(dims):
+    return lax.broadcasted_iota(jnp.int32, dims, 1)
+
+
+def head_lanes(dims, head):
+    lane = lane_of(dims)
+    return (lane >= HD) if head else (lane < HD)
+
+
+def extra_lane(head):
+    return 0 if head else HD
+
+
+def key_fill(place_ref, at, count, start):
+    row = lax.broadcasted_iota(jnp.int32, (count, LANES), 0) + start
+    half = place_ref[6]
+    position = jnp.where(row < half, place_ref[at] + row, place_ref[at + 1] + row - half)
+    return jnp.where(position < place_ref[4], 0.0, NEG_FILL).astype(jnp.bfloat16)
+
+
+def attend_kernel(place_ref, q_ref, ka_ref, va_ref, kb_ref, vb_ref, *refs):
+    mix_ref, qx_ref, keys, values = refs[-4:]
+    rows = ka_ref.shape[0]
+    bf16 = jnp.bfloat16
+
+    @pl.when(pl.program_id(1) == 0)
+    def _():
+        dims = (rows, LANES)
+        zero = jnp.zeros(dims, bf16)
+        for source, (k_ref, v_ref) in enumerate(((ka_ref, va_ref), (kb_ref, vb_ref))):
+            fill = key_fill(place_ref, 2 * source, rows, 0)
+            part = pl.ds(source * rows, rows)
+            for head in range(2):
+                inside = head_lanes(dims, head)
+                other = jnp.where(lane_of(dims) == extra_lane(head), fill, zero)
+                keys[head, part] = jnp.where(inside, k_ref[...], other)
+                values[head, part] = jnp.where(inside, v_ref[...], zero)
+
+    queries = q_ref[...]
+    dims = queries.shape
+    lane = lane_of(dims)
+    total = None
+    for head in range(2):
+        inside = head_lanes(dims, head)
+        spare = lane - extra_lane(head)
+        one = jnp.where(spare == 0, 1.0, 0.0).astype(bf16)
+        masked = jnp.where(inside, queries, one)
+        scores = nt(masked, keys[head])
+        peak = jnp.max(scores, axis=1, keepdims=True)
+        powers = jnp.exp(scores - peak)
+        row_sum = jnp.sum(powers, axis=1, keepdims=True)
+        out = nn(powers.astype(bf16), values[head]) / row_sum
+        total = out if total is None else total + out
+        lse = peak + jnp.log(row_sum)
+        high = lse.astype(bf16)
+        middle = (lse - high.astype(jnp.float32)).astype(bf16)
+        low = (lse - high.astype(jnp.float32) - middle.astype(jnp.float32)).astype(bf16)
+        wide = jnp.where(spare == 1, -high, jnp.where(spare == 2, -middle, -low))
+        wide = jnp.where((spare >= 1) & (spare <= 3), wide, one)
+        qx_ref[:, head * LANES : (head + 1) * LANES] = jnp.where(inside, queries, wide)
+    mix_ref[...] = total.astype(bf16)
+
+
+def attend(place, q, kv_own, kv_other, first, count, done=()):
+    rows = q.shape[0]
+    block = 256
+    bf16 = jnp.bfloat16
+    key_spec = pl.BlockSpec((rows, LANES), lambda p, i: (0, p + first))
+    value_spec = pl.BlockSpec((rows, LANES), lambda p, i: (0, p + first + PAIRS))
+    return pl.pallas_call(
+        attend_kernel,
+        grid=(count, rows // block),
+        in_specs=[
+            pl.BlockSpec(memory_space=pltpu.SMEM),
+            pl.BlockSpec((block, LANES), lambda p, i: (i, p + first)),
+            key_spec,
+            value_spec,
+            key_spec,
+            value_spec,
+        ]
+        + [pl.BlockSpec(memory_space=pl.ANY)] * len(done),
+        out_specs=[
+            pl.BlockSpec((block, LANES), lambda p, i: (i, p + first)),
+            pl.BlockSpec((block, 2 * LANES), lambda p, i: (i, p + first)),
+        ],
+        out_shape=[shape((rows, DIM), bf16), shape((rows, 2 * DIM), bf16)],
+        scratch_shapes=[
+            pltpu.VMEM((2, 2 * rows, LANES), bf16),
+            pltpu.VMEM((2, 2 * rows, LANES), bf16),
+        ],
+        input_output_aliases={6: 0, 7: 1} if done else {},
+        compiler_params=limit(48),
+        cost_estimate=cost(
+            64 * count * rows * 2 * rows * HD, 32 * rows * LANES * count, 2 * count * rows * 2 * rows
+        ),
+        name="attend",
+    )(place, q, kv_own, kv_own, kv_other, kv_other, *done)
+
+
+def attend_back_kernel(place_ref, qx_ref, k_ref, v_ref, g_ref, mix_ref, *refs, at, scale):
+    bf16 = jnp.bfloat16
+    f32 = jnp.float32
+    last = at == 0
+    if last:
+        dq_ref, got_k_ref, got_v_ref, cos_ref, sin_ref, out_ref, gx, g0, q0, acc = refs
+    else:
+        dq_ref, dk_ref, dv_ref, gx, g0, q0, acc = refs
+    rows = g_ref.shape[0]
+    count = k_ref.shape[0]
+    step = pl.program_id(1)
+
+    @pl.when(step == 0)
+    def _():
+        dims = (rows, LANES)
+        lane = lane_of(dims)
+        grad = g_ref[...]
+        product = grad.astype(f32) * mix_ref[...].astype(f32)
+        zero = jnp.zeros(dims, bf16)
+        for head in range(2):
+            inside = head_lanes(dims, head)
+            spare = lane - extra_lane(head)
+            delta = jnp.sum(jnp.where(inside, product, 0.0), axis=1, keepdims=True)
+            high = delta.astype(bf16)
+            middle = (delta - high.astype(f32)).astype(bf16)
+            low = (delta - high.astype(f32) - middle.astype(f32)).astype(bf16)
+            wide = jnp.where(spare == 1, -high, jnp.where(spare == 2, -middle, -low))
+            wide = jnp.where((spare >= 1) & (spare <= 3), wide, zero)
+            gx[head] = jnp.where(inside, grad, wide)
+            g0[head] = jnp.where(inside, grad, zero)
+            q0[head] = jnp.where(inside, qx_ref[:, head * LANES : (head + 1) * LANES], zero)
+        acc[...] = jnp.zeros_like(acc)
+
+    keys = k_ref[...]
+    values = v_ref[...]
+    dims = keys.shape
+    lane = lane_of(dims)
+    fill = key_fill(place_ref, at, count, step * count)
+    keys_t = keys.astype(f32).T.astype(bf16)
+    dk = None
+    dv = None
+    for head in range(2):
+        inside = head_lanes(dims, head)
+        spare = lane - extra_lane(head)
+        ones = jnp.where((spare >= 1) & (spare <= 3), 1.0, 0.0).astype(bf16)
+        keys_x = jnp.where(inside, keys, jnp.where(spare == 0, fill, ones))
+        values_x = jnp.where(inside, values, ones)
+        scores = nt(keys_x, qx_ref[:, head * LANES : (head + 1) * LANES])
+        probs = jnp.exp(scores)
+        dv_head = nn(probs.astype(bf16), g0[head])
+        grad_probs = nt(values_x, gx[head])
+        grad_scores = (probs * grad_probs).astype(bf16)
+        dk_head = nn(grad_scores, q0[head])
+        part = slice(head * HD, (head + 1) * HD)
+        acc[part] += nn(keys_t[part], grad_scores)
+        dk = dk_head if dk is None else dk + dk_head
+        dv = dv_head if dv is None else dv + dv_head
+    if last:
+        here = pl.ds(pl.multiple_of(step * count, count), count)
+        dk = dk + got_k_ref[...].astype(f32)
+        dk = dk * cos_ref[here] - partner_lanes(dk) * sin_ref[here]
+        out_ref[1, here] = dk.astype(bf16)
+        out_ref[2, here] = (dv + got_v_ref[...].astype(f32)).astype(bf16)
+    else:
+        dk_ref[...] = dk.astype(bf16)
+        dv_ref[...] = dv.astype(bf16)
+
+    @pl.when(step == pl.num_programs(1) - 1)
+    def _():
+        dq = acc[...].T
+        if last:
+            dq = (dq + dq_ref[...]) * scale
+            dq = dq * cos_ref[...] - partner_lanes(dq) * sin_ref[...]
+            out_ref[0] = dq.astype(bf16)
+        else:
+            dq_ref[...] = dq
+
+
+def attend_back(place, qx, kv, grad, mix, at, first, count, scale, more=()):
+    rows = grad.shape[0]
+    block = 512
+    bf16 = jnp.bfloat16
+    wide = pl.BlockSpec((rows, LANES), lambda p, j: (0, p + first))
+    here = pl.BlockSpec((rows, LANES), lambda p, j: (0, p))
+    keys = pl.BlockSpec((block, LANES), lambda p, j: (j, p))
+    table = pl.BlockSpec((rows, LANES), lambda p, j: (0, 0))
+    dims = (rows, count * LANES)
+    if at == 0:
+        more_specs = [here, keys, keys, table, table]
+        out_specs = pl.BlockSpec((3, rows, LANES), lambda p, j: (0, 0, p))
+        out_shape = shape((3, *dims), bf16)
+    else:
+        more_specs = []
+        out_specs = [here, keys, keys]
+        out_shape = [shape(dims, jnp.float32), shape(dims, bf16), shape(dims, bf16)]
+    return pl.pallas_call(
+        functools.partial(attend_back_kernel, at=at, scale=scale),
+        grid=(count, rows // block),
+        in_specs=[
+            pl.BlockSpec(memory_space=pltpu.SMEM),
+            pl.BlockSpec((rows, 2 * LANES), lambda p, j: (0, p + first)),
+            pl.BlockSpec((block, LANES), lambda p, j: (j, p + first)),
+            pl.BlockSpec((block, LANES), lambda p, j: (j, p + first + PAIRS)),
+            wide,
+            wide,
+        ]
+        + more_specs,
+        out_specs=out_specs,
+        out_shape=out_shape,
+        scratch_shapes=[
+            pltpu.VMEM((2, rows, LANES), bf16),
+            pltpu.VMEM((2, rows, LANES), bf16),
+            pltpu.VMEM((2, rows, LANES), bf16),
+            pltpu.VMEM((LANES, rows), jnp.float32),
+        ],
+        compiler_params=limit(48),
+        cost_estimate=cost(
+            80 * count * rows * rows * HD, 40 * count * rows * LANES, 2 * count * rows * rows
+        ),
+        name="attend_back",
+    )(place, qx, kv, kv, grad, mix, *more)
+
+
+def row_mean(values):
+    return jnp.sum(values, axis=1, keepdims=True) * (1.0 / DIM)
+
+
+def out_norm_kernel(mix_ref, w_ref, x_ref, hat_ref, rstd_ref):
+    weight = w_ref[...].reshape(DIM, DIM)
+    values = x_ref[...].astype(jnp.float32) + nt(mix_ref[...], weight)
+    centred = values - row_mean(values)
+    rstd = lax.rsqrt(row_mean(centred * centred) + EPS)
+    hat_ref[...] = centred * rstd
+    rstd_ref[...] = jnp.broadcast_to(rstd, rstd_ref.shape)
+
+
+def out_norm(mix, stacked, rows_in):
+    rows = mix.shape[0]
+    block = 256
+    spec = pl.BlockSpec((block, DIM), lambda i: (i, 0))
+    return pl.pallas_call(
+        out_norm_kernel,
+        grid=(rows // block,),
+        in_specs=[spec, pl.BlockSpec((REPS, 96, DIM), lambda i: (0, 8, 0)), spec],
+        out_specs=[spec, pl.BlockSpec((block, LANES), lambda i: (i, 0))],
+        out_shape=[shape((rows, DIM), jnp.float32), shape((rows, LANES), jnp.float32)],
+        compiler_params=limit(48),
+        cost_estimate=cost(2 * rows * DIM * DIM, 8 * rows * DIM),
+        name="out_norm",
+    )(mix, stacked, rows_in)
+
+
+FF_TILE = 256
+SUB = DIM // FF_TILE
+FF_PIECES = FF // DIM
+
+
+def row_parts(ref):
+    half = ref.shape[0] // 2
+    return [pl.ds(0, half), pl.ds(half, half)]
+
+
+def sub_lanes():
+    return pl.ds(pl.multiple_of(pl.program_id(1) * FF_TILE, FF_TILE), FF_TILE)
+
+
+def at_step(piece, sub):
+    return (pl.program_id(0) == piece) & (pl.program_id(1) == sub)
+
+
+def feed_forward_kernel(
+    hat_ref,
+    gains_ref,
+    biases_ref,
+    wg_ref,
+    wu_ref,
+    wd_ref,
+    hidden_ref,
+    factor_ref,
+    half_ref,
+    acc,
+    gate_s,
+    up_s,
+):
+    bf16 = jnp.bfloat16
+    f32 = jnp.float32
+    step = pl.program_id(0)
+
+    @pl.when(step == 0)
+    def _():
+        normed = hat_ref[...] * gains_ref[0:1] + biases_ref[0:1]
+        acc[...] = normed
+        half_ref[...] = normed.astype(bf16)
+        gate_s[...] = jnp.zeros_like(gate_s)
+        up_s[...] = jnp.zeros_like(up_s)
+
+    gate = gate_s[...]
+    up = up_s[...]
+    sig = 1.0 / (1.0 + jnp.exp(-gate))
+    act = gate * sig
+    hidden = (act * up).astype(bf16)
+    hidden_ref[...] = hidden
+    factor_ref[0] = (up * sig * (1.0 + gate - act)).astype(bf16)
+    factor_ref[1] = act.astype(bf16)
+    rows_in = half_ref[...]
+    gate_s[...] = nn(rows_in, wg_ref[0])
+    up_s[...] = nn(rows_in, wu_ref[0])
+    acc[...] += nt(hidden, wd_ref[...].reshape(DIM, FF_TILE))
+
+
+def feed_forward(hat, gains, biases, stacked):
+    rows = hat.shape[0]
+    bf16 = jnp.bfloat16
+    f32 = jnp.float32
+    fixed = lambda t: (0, 0)
+    whole = pl.BlockSpec((rows, DIM), fixed)
+    small = pl.BlockSpec((2, DIM), fixed)
+    tiles = FF_PIECES * SUB
+
+    def now(t):
+        return jnp.minimum(t, tiles - 1)
+
+    def before(t):
+        return jnp.maximum(t - 1, 0)
+
+    return pl.pallas_call(
+        feed_forward_kernel,
+        grid=(tiles + 1,),
+        in_specs=[
+            whole,
+            small,
+            small,
+            pl.BlockSpec((1, DIM, FF_TILE), lambda t: (now(t) // SUB, 0, now(t) % SUB)),
+            pl.BlockSpec((1, DIM, FF_TILE), lambda t: (now(t) // SUB + FF_PIECES, 0, now(t) % SUB)),
+            pl.BlockSpec(
+                (REPS, 96, FF_TILE), lambda t: (0, before(t) // SUB + 9, before(t) % SUB)
+            ),
+        ],
+        out_specs=[
+            pl.BlockSpec((rows, FF_TILE), lambda t: (0, before(t))),
+            pl.BlockSpec((2, rows, FF_TILE), lambda t: (0, 0, before(t))),
+            whole,
+            whole,
+        ],
+        out_shape=[
+            shape((rows, FF), bf16),
+            shape((2, rows, FF), bf16),
+            shape((rows, DIM), bf16),
+            shape((rows, DIM), f32),
+        ],
+        scratch_shapes=[
+            pltpu.VMEM((rows, FF_TILE), f32),
+            pltpu.VMEM((rows, FF_TILE), f32),
+        ],
+        compiler_params=limit(60),
+        cost_estimate=cost(6 * rows * DIM * FF, 6 * rows * FF + 6 * DIM * FF, rows * FF),
+        name="feed_forward",
+    )(hat, gains, biases, stacked, stacked, stacked)
+
+
+def norm_back_kernel(
+    place_ref, values_ref, gains_ref, biases_ref, cot_a_ref, cot_b_ref,
+    mixed_ref, grad_ref, branch_ref, vec_ref,
+):
+    bf16 = jnp.bfloat16
+    f32 = jnp.float32
+    step = pl.program_id(0)
+    second = step >= pl.num_programs(0) // 2
+    values = values_ref[...]
+    rows = values.shape[0]
+    centred = values - row_mean(values)
+    rstd = lax.rsqrt(row_mean(centred * centred) + EPS)
+    hat = centred * rstd
+    mixed_ref[...] = (hat * gains_ref[1:2] + biases_ref[1:2]).astype(bf16)
+    row = lax.broadcasted_iota(jnp.int32, (rows, 1), 0) + step * rows
+    half = place_ref[6]
+    position = jnp.where(row < half, place_ref[0] + row, place_ref[1] + row - half)
+    cot = jnp.where(second, cot_b_ref[...].astype(f32), cot_a_ref[...].astype(f32))
+    grad = jnp.where(position < place_ref[4], cot, 0.0)
+
+    @pl.when(step == 0)
+    def _():
+        vec_ref[...] = jnp.zeros_like(vec_ref)
+
+    vec_ref[0:1] += jnp.sum(grad * hat, axis=0, keepdims=True)
+    vec_ref[1:2] += jnp.sum(grad, axis=0, keepdims=True)
+    grad = grad * gains_ref[1:2]
+    grad = rstd * (grad - row_mean(grad) - hat * row_mean(grad * hat))
+    grad_ref[...] = grad
+    branch_ref[...] = grad.astype(bf16)
+
+
+def norm_back(place, values, gains, biases, cot):
+    rows = values.shape[0]
+    block = 256
+    half = rows // block // 2
+    f32 = jnp.float32
+    bf16 = jnp.bfloat16
+    spec = pl.BlockSpec((block, DIM), lambda i: (i, 0))
+    small = pl.BlockSpec((2, DIM), lambda i: (0, 0))
+    return pl.pallas_call(
+        norm_back_kernel,
+        grid=(rows // block,),
+        in_specs=[
+            pl.BlockSpec(memory_space=pltpu.SMEM),
+            spec,
+            small,
+            small,
+            pl.BlockSpec((block, DIM), lambda i: (jnp.minimum(i, half - 1), 0)),
+            pl.BlockSpec((block, DIM), lambda i: (jnp.maximum(i - half, 0), 0)),
+        ],
+        out_specs=[spec, spec, spec, small],
+        out_shape=[
+            shape((rows, DIM), bf16),
+            shape((rows, DIM), f32),
+            shape((rows, DIM), bf16),
+            shape((2, DIM), f32),
+        ],
+        compiler_params=limit(48),
+        cost_estimate=cost(30 * rows * DIM, 14 * rows * DIM),
+        name="norm_back",
+    )(place, values, gains, biases, *cot)
+
+
+def feed_back_kernel(
+    index_ref,
+    grad_ref,
+    branch_ref,
+    factor_ref,
+    wg_ref,
+    wu_ref,
+    wd_ref,
+    left_away_ref,
+    left_keep_ref,
+    *refs,
+):
+    bf16 = jnp.bfloat16
+    f32 = jnp.float32
+    last = len(refs) > 6
+    if last:
+        hat_ref, rstd_ref, gains_ref, wo_ref, away_ref, keep_ref = refs[:6]
+        attn_ref, attn_half_ref, mix_grad_ref, vec_ref, acc, both, left = refs[6:]
+    else:
+        away_ref, keep_ref, acc_ref, acc, both, left = refs
+    half_rows = left_away_ref.shape[0]
+    here = sub_lanes()
+
+    @pl.when(at_step(0, 0))
+    def _():
+        acc[...] = grad_ref[...]
+        left[:half_rows] = left_away_ref[...]
+        left[half_rows:] = left_keep_ref[...]
+
+    grad_hidden = nn(branch_ref[...], wd_ref[...].reshape(DIM, FF_TILE))
+    for side in range(2):
+        grad = (grad_hidden * factor_ref[side].astype(f32)).astype(bf16)
+        both[side, :, here] = grad
+        product = nn(left[...], grad).astype(bf16)
+        away_ref[side] = product[:half_rows]
+        keep_ref[side] = product[half_rows:]
+
+    @pl.when(pl.program_id(1) == SUB - 1)
+    def _():
+        acc[...] += nt(both[0], wg_ref[0]) + nt(both[1], wu_ref[0])
+
+    @pl.when(at_step(pl.num_programs(0) - 1, SUB - 1))
+    def _():
+        grad = acc[...]
+        if not last:
+            acc_ref[...] = grad
+            return
+        hat = hat_ref[...]
+        vec_ref[0:1] = jnp.sum(grad * hat, axis=0, keepdims=True)
+        vec_ref[1:2] = jnp.sum(grad, axis=0, keepdims=True)
+        grad = grad * gains_ref[0:1]
+        rstd = rstd_ref[:, 0:1]
+        grad = rstd * (grad - row_mean(grad) - hat * row_mean(grad * hat))
+        attn_ref[...] = grad
+        half = grad.astype(bf16)
+        attn_half_ref[...] = half
+        mix_grad_ref[...] = nn(half, wo_ref[...].reshape(DIM, DIM)).astype(bf16)
+
+
+def feed_back(index, grad, branch, factor, stacked, normed_t, first, more=()):
+    rows = grad.shape[0]
+    bf16 = jnp.bfloat16
+    f32 = jnp.float32
+    fixed = lambda j, i, s: (0, 0)
+    whole = pl.BlockSpec((rows, DIM), fixed)
+    small = pl.BlockSpec((2, DIM), fixed)
+    pieces = FF_PIECES // 2
+    count = pieces * DIM
+    parts = pl.BlockSpec((2, DIM // 2, FF_TILE), lambda j, i, s: (0, 0, SUB * j + i))
+    in_specs = [
+        whole,
+        whole,
+        pl.BlockSpec((2, rows, FF_TILE), lambda j, i, s: (0, 0, SUB * (j + first) + i)),
+        pl.BlockSpec((1, DIM, DIM), lambda j, i, s: (j + first, 0, 0)),
+        pl.BlockSpec((1, DIM, DIM), lambda j, i, s: (j + first + FF_PIECES, 0, 0)),
+        pl.BlockSpec((REPS, 96, FF_TILE), lambda j, i, s: (0, j + first + 9, i)),
+        pl.BlockSpec((DIM // 2, rows), lambda j, i, s: (s[0], 0)),
+        pl.BlockSpec((DIM // 2, rows), lambda j, i, s: (1 - s[0], 0)),
+    ]
+    out_specs = [parts, parts]
+    out_shape = [shape((2, DIM // 2, count), bf16)] * 2
+    if more:
+        in_specs += [
+            whole,
+            pl.BlockSpec((rows, LANES), fixed),
+            small,
+            pl.BlockSpec((REPS, 96, DIM), lambda j, i, s: (0, 8, 0)),
+        ]
+        out_specs += [whole, whole, whole, small]
+        out_shape += [
+            shape((rows, DIM), f32),
+            shape((rows, DIM), bf16),
+            shape((rows, DIM), bf16),
+            shape((2, DIM), f32),
+        ]
+    else:
+        out_specs += [whole]
+        out_shape += [shape((rows, DIM), f32)]
+    return pl.pallas_call(
+        feed_back_kernel,
+        grid_spec=pltpu.PrefetchScalarGridSpec(
+            num_scalar_prefetch=1,
+            grid=(pieces, SUB),
+            in_specs=in_specs,
+            out_specs=out_specs,
+            scratch_shapes=[
+                pltpu.VMEM((rows, DIM), f32),
+                pltpu.VMEM((2, rows, DIM), bf16),
+                pltpu.VMEM((DIM, rows), bf16),
+            ],
+        ),
+        out_shape=out_shape,
+        compiler_params=limit(60),
+        cost_estimate=cost(10 * rows * DIM * count, 4 * rows * count + 10 * DIM * count),
+        name="feed_back",
+    )(index, grad, branch, factor, stacked, stacked, stacked, normed_t, normed_t, *more)
+
+
+def away_kernel(index_ref, left_ref, right_ref, out_ref):
+    right = right_ref[0] if len(right_ref.shape) == 3 else right_ref[...]
+    out_ref[...] = nn(left_ref[...], right).astype(out_ref.dtype)
+
+
+def keep_kernel(index_ref, la_ref, lb_ref, right_ref, ra_ref, rb_ref, out_a_ref, out_b_ref):
+    right = right_ref[0] if len(right_ref.shape) == 3 else right_ref[...]
+    for left, got, out in ((la_ref, ra_ref, out_a_ref), (lb_ref, rb_ref, out_b_ref)):
+        out[...] = (nn(left[...], right) + got[...].astype(jnp.float32)).astype(out.dtype)
+
+
+def right_spec(right, tile):
+    if right.ndim == 3:
+        per = right.shape[2] // tile
+        return pl.BlockSpec((1, right.shape[1], tile), lambda t, s: (t // per, 0, t % per))
+    return pl.BlockSpec((right.shape[0], tile), lambda t, s: (0, t))
+
+
+def away_rows(index, left_t, right, tile):
+    rows = left_t.shape[1]
+    half = left_t.shape[0] // 2
+    count = right.size // rows
+    return pl.pallas_call(
+        away_kernel,
+        grid_spec=pltpu.PrefetchScalarGridSpec(
+            num_scalar_prefetch=1,
+            grid=(count // tile,),
+            in_specs=[
+                pl.BlockSpec((half, rows), lambda t, s: (s[0], 0)),
+                right_spec(right, tile),
+            ],
+            out_specs=pl.BlockSpec((half, tile), lambda t, s: (0, t)),
+        ),
+        out_shape=shape((half, count), jnp.bfloat16),
+        compiler_params=limit(48),
+        cost_estimate=cost(2 * half * rows * count, 2 * rows * count + 2 * half * count),
+        name="away_rows",
+    )(index, left_t, right)
+
+
+def keep_rows(index, left_t, right, got, tile):
+    rows = left_t.shape[1]
+    block = left_t.shape[0] // 4
+    count = right.size // rows
+    out = pl.BlockSpec((block, tile), lambda t, s: (0, t))
+    return pl.pallas_call(
+        keep_kernel,
+        grid_spec=pltpu.PrefetchScalarGridSpec(
+            num_scalar_prefetch=1,
+            grid=(count // tile,),
+            in_specs=[
+                pl.BlockSpec((block, rows), lambda t, s: (s[1], 0)),
+                pl.BlockSpec((block, rows), lambda t, s: (s[2], 0)),
+                right_spec(right, tile),
+                pl.BlockSpec((block, tile), lambda t, s: (s[3], t)),
+                pl.BlockSpec((block, tile), lambda t, s: (1 - s[3], t)),
+            ],
+            out_specs=[out, out],
+        ),
+        out_shape=[shape((block, count), jnp.bfloat16)] * 2,
+        compiler_params=limit(48),
+        cost_estimate=cost(4 * block * rows * count, 2 * rows * count + 8 * block * count),
+        name="keep_rows",
+    )(index, left_t, left_t, right, got, got)
+
+
+def keep_columns_kernel(index_ref, left_ref, right_a_ref, right_b_ref, ra_ref, rb_ref, oa_ref, ob_ref):
+    left = left_ref[...]
+    for right, got, out in ((right_a_ref, ra_ref, oa_ref), (right_b_ref, rb_ref, ob_ref)):
+        out[...] = (nn(left, right[...]) + got[...].astype(jnp.float32)).astype(out.dtype)
+
+
+def away_columns(index, left_t, right, tile):
+    height, rows = left_t.shape
+    half = right.shape[1] // 2
+    per = half // tile
+    return pl.pallas_call(
+        away_kernel,
+        grid_spec=pltpu.PrefetchScalarGridSpec(
+            num_scalar_prefetch=1,
+            grid=(per,),
+            in_specs=[
+                pl.BlockSpec((height, rows), lambda t, s: (0, 0)),
+                pl.BlockSpec((rows, tile), lambda t, s: (0, s[0] * per + t)),
+            ],
+            out_specs=pl.BlockSpec((height, tile), lambda t, s: (0, t)),
+        ),
+        out_shape=shape((height, half), jnp.bfloat16),
+        compiler_params=limit(48),
+        cost_estimate=cost(2 * height * rows * half, 2 * rows * half + 2 * height * half),
+        name="away_columns",
+    )(index, left_t, right)
+
+
+def keep_columns(index, left_t, right, got, tile):
+    height, rows = left_t.shape
+    block = right.shape[1] // 4
+    per = block // tile
+    out = pl.BlockSpec((height, tile), lambda t, s: (0, t))
+    return pl.pallas_call(
+        keep_columns_kernel,
+        grid_spec=pltpu.PrefetchScalarGridSpec(
+            num_scalar_prefetch=1,
+            grid=(per,),
+            in_specs=[
+                pl.BlockSpec((height, rows), lambda t, s: (0, 0)),
+                pl.BlockSpec((rows, tile), lambda t, s: (0, s[1] * per + t)),
+                pl.BlockSpec((rows, tile), lambda t, s: (0, s[2] * per + t)),
+                pl.BlockSpec((height, tile), lambda t, s: (0, s[3] * per + t)),
+                pl.BlockSpec((height, tile), lambda t, s: (0, (1 - s[3]) * per + t)),
+            ],
+            out_specs=[out, out],
+        ),
+        out_shape=[shape((height, block), jnp.bfloat16)] * 2,
+        compiler_params=limit(48),
+        cost_estimate=cost(4 * height * rows * block, 4 * rows * block + 8 * height * block),
+        name="keep_columns",
+    )(index, left_t, right, right, got, got)
+
+
+def input_kernel(ga_ref, gb_ref, wa_ref, wb_ref, attn_ref, out_ref, acc):
+    step = pl.program_id(0)
+
+    @pl.when(step == 0)
+    def _():
+        acc[...] = attn_ref[...]
+
+    acc[...] += nn(ga_ref[0], wa_ref[0]) + nn(gb_ref[0], wb_ref[0])
+
+    @pl.when(step == pl.num_programs(0) - 1)
+    def _():
+        out_ref[...] = acc[...].astype(out_ref.dtype)
+
+
+def input_rows_of(grads_a, grads_b, qkv_t, grad_attn):
+    rows = grad_attn.shape[0]
+    wide, narrow = grads_a.shape[2], grads_b.shape[2]
+    fixed = lambda i: (0, 0)
+    return pl.pallas_call(
+        input_kernel,
+        grid=(3,),
+        in_specs=[
+            pl.BlockSpec((1, rows, wide), lambda i: (i, 0, 0)),
+            pl.BlockSpec((1, rows, narrow), lambda i: (i, 0, 0)),
+            pl.BlockSpec((1, wide, DIM), lambda i: (i, 0, 0)),
+            pl.BlockSpec((1, narrow, DIM), lambda i: (i, wide // narrow, 0)),
+            pl.BlockSpec((rows, DIM), fixed),
+        ],
+        out_specs=pl.BlockSpec((rows, DIM), fixed),
+        out_shape=shape((rows, DIM), jnp.bfloat16),
+        scratch_shapes=[pltpu.VMEM((rows, DIM), jnp.float32)],
+        compiler_params=limit(48),
+        cost_estimate=cost(6 * rows * DIM * DIM, 14 * rows * DIM),
+        name="input_rows",
+    )(grads_a, grads_b, qkv_t.reshape(3, DIM, DIM), qkv_t.reshape(3, DIM, DIM), grad_attn)
+
+
+def gram_schmidt_kernel(left_ref, basis_ref, *, segments):
+    row = lax.broadcasted_iota(jnp.int32, (RANK, 1), 0)
+    for start, width in segments:
+        values = left_ref[:, start : start + width]
+        for column in range(RANK):
+            vector = values[column : column + 1]
+            vector = vector * lax.rsqrt(jnp.sum(vector * vector, axis=1, keepdims=True) + 1e-06)
+            weights = jnp.sum(values * vector, axis=1, keepdims=True)
+            later = values - weights * vector
+            values = jnp.where(row > column, later, jnp.where(row == column, vector, values))
+        basis_ref[:, start : start + width] = values
+
+
+def compress(merged, starts, masters, moments, rates, rep, rider=None):
+    highest = lax.Precision.HIGHEST
+    lefts = []
+    places = []
+    segments = []
+    at = 0
+    for block, start_set in zip(merged, starts):
+        left = lax.dot_general(start_set[0], block, (((0,), (1,)), ((), ())), precision=highest)
+        size = left.shape[1]
+        padded = (size + 255) // 256 * 256
+        lefts.append(jnp.pad(left, ((0, 0), (0, padded - size))))
+        places.append((at, size))
+        segments.append((at, padded))
+        at += padded
+    if rider is not None:
+        lefts.append(rider)
+    packed = plane_sum(jnp.concatenate(lefts, axis=1)) / REPS
+    rider = packed[:, at:]
+    packed = packed[:, :at]
+    basis_all = pl.pallas_call(
+        functools.partial(gram_schmidt_kernel, segments=tuple(segments)),
+        out_shape=shape(packed.shape, jnp.float32),
+        name="gram_schmidt",
+    )(packed)
+    bases = [basis_all[:, at : at + size] for at, size in places]
+    pulled = [jnp.dot(basis, block, precision=highest) for basis, block in zip(bases, merged)]
+    widths = [part.shape[1] for part in pulled]
+    summed = plane_sum_half(jnp.concatenate(pulled, axis=1)) / REPS
+    results = []
+    at = 0
+    for block, basis, size, master, moment, rate in zip(
+        merged, bases, widths, masters, moments, rates
+    ):
+        factor = summed[:, at : at + size]
+        at += size
+        approx = lax.dot_general(basis, factor, (((0,), (0,)), ((), ())), precision=highest)
+        col_count = master.shape[1]
+        piece = lax.dynamic_slice_in_dim(factor, rep * col_count, col_count, 1)
+        piece = lax.dot_general(basis, piece, (((0,), (0,)), ((), ())), precision=highest)
+        moment_new = MOMENTUM * moment + piece
+        results.append(
+            (master - rate * moment_new, moment_new, (block - approx)[None], basis.T, factor.T[None])
+        )
+    return results, rider
+
+
+def fast_device(
+    tokens,
+    cotangent,
+    lengths,
+    w_qkv,
+    w_out,
+    w_gate_up,
+    w_down,
+    mom_qkv,
+    mom_out,
+    mom_gate_up,
+    mom_down,
+    err_qkv,
+    err_out,
+    err_gate_up,
+    err_down,
+    start_qkv,
+    start_out,
+    start_gate_up,
+    start_down,
+    layer_norm_gains,
+    layer_norm_biases,
+    norm_moments,
+):
+    f32 = jnp.float32
+    bf16 = jnp.bfloat16
+    rep = lax.axis_index("rep")
+    shard = lax.axis_index("shard")
+    core = rep % 2
+    local_len, width = tokens.shape[1:]
+    scale = HD ** (-0.5)
+
+    def spread(values, *before):
+        parts = []
+        for parity in (0, 1):
+            sent = lax.dynamic_index_in_dim(values, (shard + parity) % 2, 0, keepdims=False)
+            parts.append(send(sent, spread_move(parity)))
+        return after(parts, *before)
+
+    def bring_back(rows):
+        first = send(rows[:local_len], gather_move(0))
+        second = send(rows[local_len:], gather_move(1))
+        even = shard % 2 == 0
+        return jnp.stack([jnp.where(even, first, second), jnp.where(even, second, first)])
+
+    side = jnp.concatenate(
+        [
+            w_gate_up.astype(bf16),
+            w_down.astype(bf16).T,
+            w_out.astype(bf16).T.reshape(24, width),
+        ],
+        axis=0,
+    )
+    gathered = lax.all_gather(side, "shard", axis=0)
+    qkv_piece = jnp.concatenate(shard_gather(w_qkv.astype(bf16).T, shard), axis=1)
+    qkv_near = plane_near(qkv_piece)
+    rows_in = jnp.concatenate(spread(tokens), axis=0)
+    qkv_far = plane_far(qkv_piece, qkv_near)
+    both = jnp.stack([lengths, sibling(lengths)])
+    group = shard // 2
+    length = both[jnp.where(group == core, 0, 1), shard % 2]
+    qkv_others = exchange(qkv_piece, qkv_near, qkv_far)
+    inside = jnp.arange(local_len, dtype=jnp.int32)
+
+    def starts_of(k):
+        first = 2 * k + shard % 2
+        second = 2 * k + 1 - shard % 2
+        return [first * local_len, second * local_len]
+
+    place = jnp.stack(
+        starts_of(core) + starts_of(1 - core) + [length, jnp.zeros_like(length), local_len + 0 * length]
+    ).astype(jnp.int32)
+    qkv_t = plane_all(
+        qkv_piece, qkv_near, qkv_far, qkv_others, rep, (gathered.reshape(-1, width), place)
+    )
+    qkv_t = qkv_t.reshape(3 * width, width)
+    position = jnp.concatenate([place[0] + inside, place[1] + inside])
+    inverse = jnp.exp(
+        jnp.arange(HD // 2, dtype=jnp.int32).astype(f32) * (-2.0 * math.log(ROPE_BASE) / HD)
+    )
+    angle = position.astype(f32)[:, None] * inverse[None, :]
+    cosine, sine = jnp.cos(angle), jnp.sin(angle)
+    cos = jnp.concatenate([cosine] * 4, axis=1)
+    sin = jnp.concatenate([-sine, sine] * 2, axis=1)
+
+    kv = project(rows_in, qkv_t, cos, sin, 1, 2, 1, 1.0)
+    kv_other = sibling(kv)
+    q = project(rows_in, qkv_t, cos, sin, 0, 1, None, scale)
+    out_piece = gathered[:, 288:].reshape(SHARDS, 96, 192).transpose(1, 0, 2)
+    piece = jnp.concatenate(
+        [
+            gathered[:, :192].reshape(width, width),
+            out_piece.reshape(96, width),
+            gathered[:, 192:288].reshape(384, width),
+        ],
+        axis=0,
+    )
+    near = plane_near(piece)
+    first = attend(place, q, kv, kv_other, 0, 2)
+    second = attend(place, q, kv, kv_other, 2, 2, first)
+    near = after(near, second[1])
+    far = plane_far(piece, near)
+    mix, qx = attend(place, q, kv, kv_other, 4, 2, second)
+    others = [sibling(part) for part in (after(piece, second[1]), *near)]
+    far = after(far, qx)
+    others.append(sibling(jnp.concatenate(far, axis=0)))
+    stacked = plane_all(piece, near, far, others, rep)
+    cot_in = spread(after(cotangent, stacked))
+    hat, rstd = out_norm(mix, stacked, rows_in)
+    hidden, factor, normed_half, values = feed_forward(
+        hat, layer_norm_gains, layer_norm_biases, stacked
+    )
+    mixed, grad_second, branch, vec_two = norm_back(
+        place, values, layer_norm_gains, layer_norm_biases, cot_in
+    )
+    mixed_out = bring_back(mixed)
+
+    other = 1 - core
+    shard_own = jnp.where((shard == 0) | (shard == 3), 0, 1)
+    kept = jnp.where(core == 0, shard_own, 3 - shard_own)
+    index = jnp.stack([other, kept, 4 * core + 1 - kept, kept - 2 * core]).astype(jnp.int32)
+    owner = core == shard // 2
+
+    def kept_rows(values, at):
+        parts = values.reshape(2, 2, -1, values.shape[2])
+        return lax.dynamic_index_in_dim(parts, at, 1, keepdims=False).astype(f32)
+
+    near = index[3]
+
+    def core_sum(keep, got):
+        mine = (kept_rows(keep, near) + kept_rows(got, near)).astype(bf16)
+        theirs = (kept_rows(keep, 1 - near) + kept_rows(got, 1 - near)).astype(bf16)
+        return mine, theirs
+
+    def add(mine, pair):
+        return (mine.astype(f32) + pair.astype(f32)).astype(bf16)
+
+    branch_t = branch.T
+    down_got = sibling(away_columns(index, branch_t, hidden, DIM))
+    normed_t = normed_half.T
+    away_1, keep_1, partial = feed_back(
+        index, grad_second, branch, factor, stacked, normed_t, 0
+    )
+    got_1 = sibling(away_1)
+    down_mine, down_theirs = keep_columns(index, branch_t, hidden, down_got, DIM)
+    down_pair = pair_z(down_theirs)
+    away_2, keep_2, grad_attn, grad_attn_half, grad_mix, vec_one = feed_back(
+        index, after(partial, down_mine, down_theirs, mixed_out), branch, factor,
+        stacked, normed_t, 2, (hat, rstd, layer_norm_gains, stacked),
+    )
+    got_2 = sibling(away_2)
+    first_mine, first_theirs = core_sum(after(keep_1, grad_mix), got_1)
+    first_pair = pair_z(first_theirs)
+    mix_t = mix.T
+    out_got = sibling(away_rows(index, mix_t, grad_attn_half, DIM))
+    down_sum = add(down_mine, after(down_pair, grad_mix))
+    down_far = to_owner(down_sum)
+
+    def back(grads, kv_set, at, first, count, more=()):
+        return attend_back(place, qx, kv_set, grads, mix, at, first, count, scale, more)
+
+    def join(pair, single):
+        return jnp.concatenate([pair[0], pair[1], single], axis=1)
+
+    vectors = jnp.concatenate([vec_one, vec_two], axis=0)
+    grads = after(grad_mix, first_mine, first_theirs, down_sum)
+    dq_2, dk_2, dv_2 = back(grads, kv_other, 2, 4, 2)
+    other_2 = sibling(dk_2), sibling(dv_2)
+    second_mine, second_theirs = core_sum(keep_2, after(got_2, dq_2))
+    out_mine, out_theirs = keep_rows(index, mix_t, grad_attn_half, after(out_got, dq_2), DIM)
+    second_mine = join(second_mine, out_mine)
+    second_theirs = join(second_theirs, out_theirs)
+    second_pair = pair_z(second_theirs)
+    vectors = after(vectors, dq_2)
+    vectors_pair = pair_z(vectors)
+    grads = after(grads, second_mine, second_theirs)
+    dq_1, dk_1, dv_1 = back(grads, kv_other, 2, 0, 4)
+    other_1 = sibling(dk_1), sibling(dv_1)
+    first_sum = add(first_mine, after(first_pair, dq_1))
+    first_far = to_owner(first_sum)
+    down_far = after(down_far, dq_1)
+    vectors = vectors + after(vectors_pair, dq_1)
+    vectors_mirror = mirror_z(vectors)
+    grads = after(grads, first_sum)
+    grads_b = back(grads, kv, 0, 4, 2, (dq_2, *other_2, cos, sin))
+    second_sum = add(second_mine, after(second_pair, grads_b))
+    second_far = to_owner(second_sum)
+    tokens_t = rows_in.T
+    qkv_got_b = sibling(away_rows(index, tokens_t, grads_b, 256))
+    vectors = vectors + after(vectors_mirror, grads_b)
+    grads = after(grads, second_sum)
+    grads_a = back(grads, kv, 0, 0, 4, (dq_1, *other_1, cos, sin))
+    qkv_got_a = sibling(away_rows(index, tokens_t, grads_a, 512))
+    qkv_mine_b, qkv_theirs_b = keep_rows(index, tokens_t, grads_b, after(qkv_got_b, grads_a), 256)
+    qkv_mine_a, qkv_theirs_a = keep_rows(index, tokens_t, grads_a, qkv_got_a, 512)
+    qkv_theirs = jnp.concatenate([qkv_theirs_a, qkv_theirs_b], axis=1)
+    qkv_mine = jnp.concatenate([qkv_mine_a, qkv_mine_b], axis=1)
+    qkv_pair = pair_z(qkv_theirs)
+    input_rows = input_rows_of(grads_a, grads_b, qkv_t, after(grad_attn, qkv_theirs))
+    qkv_sum = add(qkv_mine, after(qkv_pair, input_rows))
+    qkv_far = to_owner(qkv_sum)
+    input_grad = bring_back(after(input_rows, qkv_sum)).astype(f32)
+
+    def owned(own, far):
+        return jnp.where(owner, own, far).astype(f32)
+
+    own_down = lax.optimization_barrier(jnp.where(owner, down_sum, down_far).T).astype(f32)
+    own_first = owned(first_sum, first_far)
+    own_second = owned(second_sum, second_far)
+    half_ff = FF // 2
+    own_gate_up = jnp.concatenate(
+        [own_first[0], own_second[:, :half_ff], own_first[1], own_second[:, half_ff:FF]], axis=1
+    )
+    own_out = own_second[:, FF:]
+    own_qkv = owned(qkv_sum, qkv_far)
+    own_qkv = jnp.concatenate(
+        [
+            part
+            for i in range(3)
+            for part in (
+                own_qkv[:, 512 * i : 512 * i + 512],
+                own_qkv[:, 1536 + 256 * i : 1792 + 256 * i],
+            )
+        ],
+        axis=1,
+    )
+
+    early, norm_grad = compress(
+        (own_out + err_out[0], own_gate_up + err_gate_up[0], own_down + err_down[0]),
+        (start_out, start_gate_up, start_down),
+        (w_out, w_gate_up, w_down),
+        (mom_out, mom_gate_up, mom_down),
+        LEARN_RATES[1:],
+        rep,
+        vectors.reshape(RANK, width // 2),
+    )
+    norm_grad = norm_grad.reshape(4, width)
+    params = jnp.stack(
+        [layer_norm_gains[0], layer_norm_biases[0], layer_norm_gains[1], layer_norm_biases[1]]
+    )
+    norm_moment_new = MOMENTUM * norm_moments + norm_grad
+    norm_new = params - NORM_RATE * norm_moment_new
+    late, _ = compress(
+        (after(own_qkv, *early[1][:3]) + err_qkv[0],), (start_qkv,), (w_qkv,), (mom_qkv,),
+        LEARN_RATES[:1], rep,
+    )
+    results = late + early
+    new_weights, new_moments, new_errors, bases, factors = zip(*results)
+    return (
+        mixed_out,
+        input_grad,
+        *new_weights,
+        *new_moments,
+        *new_errors,
+        *bases,
+        *factors,
+        norm_moment_new,
+        norm_new,
+    )
+
+
+def choose(mesh):
+    if mesh.shape["rep"] == REPS and mesh.shape["shard"] == SHARDS:
+        return fast_device
+    return general_device
+
+
 def solution(mesh):
     placed = (
         P("rep", "shard", None),
@@ -407,7 +1660,7 @@
         P(),
     )
     return jax.shard_map(
-        per_device,
+        choose(mesh),
         mesh=mesh,
         in_specs=placed,
         out_specs=(

time: 2120 us -> 687 us (0.32)
  waiting for transfers between devices: 1170 us -> 134 us
  matrix products: 406 us -> 45.8 us
  Pallas kernels: 0 us -> 309 us
  other arithmetic: 325 us -> 43.6 us
  blocking collectives: 112 us -> 0 us
  starting transfers between devices: 1.08 us -> 66.1 us
    reduce_scatter x6 -> x0, waiting for transfers between devices: 664 us -> none  [the longest x1 212 us: per_device(): lax.psum_scatter(value_parts, 'shard', scatter_dimension=2, tiled=True)]
    all_gather x8 -> x1, waiting for transfers between devices: 470 us -> 0.02 us  [fast_device(): gathered = lax.all_gather(side, 'shard', axis=0)]
    dot_general x108 -> x16, matrix products: 406 us -> 45.8 us  [the longest x4 19.3 us: compress(): lax.dot_general(basis, factor, (((0,), (0,)), ((), ())), precision=highest)]
    pallas_call x0 -> x27, Pallas kernels: none -> 309 us  [the longest x4 100 us: attend_back(): pl.pallas_call(functools.partial(attend_back_kernel, at=at, scale=scale),...]
    reduce_sum x74 -> x0, other arithmetic: 173 us -> none  [the longest x39 116 us: orthonormal(): vector = vector - jnp.sum(earlier * vector) * earlier]
    ppermute x0 -> x61, waiting for transfers between devices: none -> 134 us  [send(): return lax.ppermute(values, AXES, pairs)]
    psum x3 -> x0, blocking collectives: 90.2 us -> none  [the longest x1 40.8 us: per_device(): norm_grad = lax.psum(vector_parts, ('rep', 'shard')) / replicas]
    mul x6 -> x0, other arithmetic: 74.5 us -> none  [the longest x5 71.8 us: orthonormal(): vector = vector * lax.rsqrt(jnp.sum(vector * vector) + 1e-06)]
  transfers between devices with their start and end apart: 15 -> 62, of which waited for: 13 -> 22; matrix products, arithmetic and copies ran while one was open for 11% -> 16% of each run, Pallas kernels for 0% -> 41%
where the time goes in v1:
time: 687 us; the launch traced here: 679 us
  Pallas kernels  309 us (45%)
  waiting for transfers between devices  134 us (20%)
  starting transfers between devices  66.1 us (10%)
  local copies, waits for them, and re-layouts  64.1 us (9%)
  matrix products  45.8 us (7%)
  other arithmetic  43.6 us (6%)
  between operations  16.1 us (2%)
    ppermute x61, waiting for transfers between devices, send(): return lax.ppermute(values, AXES, pairs)  134 us
    pallas_call x4, Pallas kernels, attend_back(): pl.pallas_call(functools.partial(attend_back_kernel, at=at, scale=scale),...  100 us
    ppermute x61, starting transfers between devices, send(): return lax.ppermute(values, AXES, pairs)  66.1 us
    pallas_call x3, Pallas kernels, attend(): pl.pallas_call(attend_kernel, grid=(count, rows // block), in_specs=[pl.B...  57.8 us
    pallas_call x2, Pallas kernels, feed_back(): pl.pallas_call(feed_back_kernel, grid_spec=pltpu.PrefetchScalarGridSpec(n...  47.9 us
    pallas_call x1, Pallas kernels, feed_forward(): pl.pallas_call(feed_forward_kernel, grid=(tiles + 1,), in_specs=[whole, s...  25.8 us
    unnamed x179, local copies, waits for them, and re-layouts  25.3 us
    dot_general x4, matrix products, compress(): lax.dot_general(basis, factor, (((0,), (0,)), ((), ())), precision=highest)  19.3 us
  transfers between devices with their start and end apart: 62, of which 22 were waited for; matrix products, arithmetic and copies ran while one was open for 16% of the time, Pallas kernels for 41%

profile of v1, /device:TPU:16, one launch (start us, length us, event | category | flops | bytes accessed | tf_op | source)
XLA Modules:
  0.0 679.4 jit_solution(8944604894830655698)
XLA Ops:
  14.6 13.5 %collective-permute-done.3 = bf16[288,192]{0,1:T(8,128)(2,1)S(1)} collective-permute-done((bf16[288,192]{0,1:T(8,128)(2,1)S(1)}, bf16[288,192]{0,1:T(8,128)(2,1)S(1)}, u32[]{:S(2)}, u32[]{:S(2)}) %collective-permute-start.3) | collective-permute-done | bytes 110624 | tf_op jit(solution)/shard_map/ppermute | solution.py:404
  28.1 8.8 %collective-permute-done.5 = bf16[288,192]{0,1:T(8,128)(2,1)S(1)} collective-permute-done((bf16[288,192]{0,1:T(8,128)(2,1)S(1)}, bf16[288,192]{0,1:T(8,128)(2,1)S(1)}, u32[]{:S(2)}, u32[]{:S(2)}) %collective-permute-start.5) | collective-permute-done | bytes 110624 | tf_op jit(solution)/shard_map/ppermute | solution.py:404
  46.0 4.3 collective-permute-start.2
  60.4 21.2 %collective-permute-done.1 = bf16[512,768]{0,1:T(8,128)(2,1)S(1)} collective-permute-done((bf16[512,768]{0,1:T(8,128)(2,1)}, bf16[512,768]{0,1:T(8,128)(2,1)S(1)}, u32[]{:S(2)}, u32[]{:S(2)}) %collective-permute-start.1) | collective-permute-done | bytes 786464 | tf_op jit(solution)/shard_map/ppermute | solution.py:404
  84.3 7.1 %collective-permute-done.2 = bf16[512,768]{0,1:T(8,128)(2,1)} collective-permute-done((bf16[512,768]{0,1:T(8,128)(2,1)}, bf16[512,768]{0,1:T(8,128)(2,1)}, u32[]{:S(2)}, u32[]{:S(2)}) %collective-permute-start.2) | collective-permute-done | bytes 786464 | tf_op jit(solution)/shard_map/ppermute | solution.py:404
  102.9 7.3 %project.3.ka_ref.va_ref.k_ref.v_ref = bf16[1024,1536]{1,0:T(8,128)(2,1)} custom-call(bf16[1024,768]{1,0:T(8,128)(2,1)S(1)} %copy.79.x_ref, bf16[2304,768]{1,0:T(8,128)(2,1)} %bitcast.168, f32[1024,128]{1,0:T(8,128)S(1)} %copy-done.15, f32[1024,128]{1,0:T(8,128)S(1)} %copy-done.11), custom_call_target="tpu_custom_call" | custom-call | flops 2415919104 | bytes 9437184 | tf_op jit(solution)/shard_map/project/pallas_call | solution.py:596
  125.4 19.2 %attend.3 = (bf16[1024,768]{1,0:T(8,128)(2,1)S(1)}, bf16[1024,1536]{1,0:T(8,128)(2,1)}) custom-call(s32[7]{0:T(128)S(1)} %stack.82.refs_10_.place_ref, bf16[1024,768]{1,0:T(8,128)(2,1)S(1)} %project.2.q_ref, bf16[1024,1536]{1,0:T(8,128)(2,1)} %project.3.ka_ref.va_ref.k_ref.v_ref, bf16[1024,1536]{1,0:T(8,128)(2,1)} %project.3.ka_ref.va_ref.k_ref.v_ref, ...), custom_call_target="tpu_custom_call" | custom-call | flops 17179869184 | bytes 8388608 | tf_op jit(solution)/shard_map/attend/pallas_call | solution.py:682
  144.6 19.4 %attend.4 = (bf16[1024,768]{1,0:T(8,128)(2,1)S(1)}, bf16[1024,1536]{1,0:T(8,128)(2,1)}) custom-call(s32[7]{0:T(128)S(1)} %stack.82.refs_10_.place_ref, bf16[1024,768]{1,0:T(8,128)(2,1)S(1)} %project.2.q_ref, bf16[1024,1536]{1,0:T(8,128)(2,1)} %project.3.ka_ref.va_ref.k_ref.v_ref, ...), custom_call_target="tpu_custom_call", output_to_operand_aliasing={{0}: (6, {}), {1}: (7, {})} | custom-call | flops 17179869184 | bytes 8388608 | tf_op jit(solution)/shard_map/attend/pallas_call | solution.py:682
  169.8 19.2 %attend.5 = (bf16[1024,768]{1,0:T(8,128)(2,1)S(1)}, bf16[1024,1536]{1,0:T(8,128)(2,1)}) custom-call(s32[7]{0:T(128)S(1)} %stack.82.refs_10_.place_ref, bf16[1024,768]{1,0:T(8,128)(2,1)S(1)} %project.2.q_ref, bf16[1024,1536]{1,0:T(8,128)(2,1)} %project.3.ka_ref.va_ref.k_ref.v_ref, ...), custom_call_target="tpu_custom_call", output_to_operand_aliasing={{0}: (6, {}), {1}: (7, {})} | custom-call | flops 17179869184 | bytes 8388608 | tf_op jit(solution)/shard_map/attend/pallas_call | solution.py:682
  192.9 4.1 collective-permute-done.22.refs_8_
  199.5 10.6 %stack_pieces.3.w_ref.wg_ref.wu_ref.wd_ref.refs_3_ = bf16[8,1248,768]{2,1,0:T(8,128)(2,1)} custom-call(s32[1]{0:T(128)} %bitcast.9.rep_ref, bf16[1248,768]{1,0:T(8,128)(2,1)} %pad_maximum_fusion.refs_0_, bf16[1248,768]{1,0:T(8,128)(2,1)} %collective-permute-done.15.refs_1_, bf16[1248,768]{1,0:T(8,128)(2,1)} %collective-permute-done.16.refs_2_, ...), custom_call_target="tpu_custom_call" | custom-call | bytes 30670848 | tf_op jit(solution)/shard_map/stack_pieces/pallas_call | solution.py:509
  213.7 5.3 out_norm.1
  219.8 25.8 %feed_forward.1 = (bf16[1024,3072]{1,0:T(8,128)(2,1)}, bf16[2,1024,3072]{2,1,0:T(8,128)(2,1)}, bf16[1024,768]{1,0:T(8,128)(2,1)}, f32[1024,768]{1,0:T(8,128)}) custom-call(f32[1024,768]{1,0:T(8,128)} %get-tuple-element.106.hat_ref.refs_0_, f32[2,768]{1,0:T(2,128)} %refs_2_.1, f32[2,768]{1,0:T(2,128)} %biases_ref.3, ...), custom_call_target="tpu_custom_call" | custom-call | flops 14495514624 | bytes 33030144 | tf_op jit(solution)/shard_map/feed_forward/pallas_call | solution.py:937
  248.9 6.4 norm_back.1
  259.4 5.9 away_columns.1
  277.4 21.7 %feed_back.2 = (bf16[2,384,1536]{2,1,0:T(8,128)(2,1)}, bf16[2,384,1536]{2,1,0:T(8,128)(2,1)}, f32[1024,768]{1,0:T(8,128)}) custom-call(s32[4]{0:T(128)} %copy-done.36, f32[1024,768]{1,0:T(8,128)} %get-tuple-element.112.grad_ref, bf16[1024,768]{1,0:T(8,128)(2,1)} %copy-done.3, bf16[2,1024,3072]{2,1,0:T(8,128)(2,1)} %get-tuple-element.114.factor_ref, ...), custom_call_target="tpu_custom_call" | custom-call | flops 12079595520 | bytes 18087936 | tf_op jit(solution)/shard_map/feed_back/pallas_call | solution.py:1134
  303.1 9.3 %collective-permute-done.26 = bf16[512,768]{1,0:T(8,128)(2,1)} collective-permute-done((bf16[512,768]{1,0:T(8,128)(2,1)}, bf16[512,768]{1,0:T(8,128)(2,1)}, u32[]{:S(2)}, u32[]{:S(2)}) %collective-permute-start.26) | collective-permute-done | bytes 786464 | tf_op jit(solution)/shard_map/ppermute | solution.py:404
  315.2 6.7 keep_columns.1
  322.9 26.3 %feed_back.3 = (bf16[2,384,1536]{2,1,0:T(8,128)(2,1)}, bf16[2,384,1536]{2,1,0:T(8,128)(2,1)}, f32[1024,768]{1,0:T(8,128)}, bf16[1024,768]{1,0:T(8,128)(2,1)}, bf...) custom-call(s32[4]{0:T(128)} %copy-done.36, f32[1024,768]{1,0:T(8,128)} %get-tuple-element.120.grad_ref, ...), custom_call_target="tpu_custom_call" | custom-call | flops 12079595520 | bytes 18087936 | tf_op jit(solution)/shard_map/feed_back/pallas_call | solution.py:1134
  367.0 18.6 %attend_back.4 = (f32[1024,256]{1,0:T(8,128)S(1)}, bf16[1024,256]{1,0:T(8,128)(2,1)S(1)}, bf16[1024,256]{1,0:T(8,128)(2,1)S(1)}) custom-call(s32[7]{0:T(128)S(1)} %stack.82.refs_10_.place_ref, bf16[1024,1536]{1,0:T(8,128)(2,1)} %get-tuple-element.102.qx_ref, bf16[1024,1536]{1,0:T(8,128)(2,1)} %collective-permute-done.14.kb_ref.vb_ref.k_ref.v_ref, ...), custom_call_target="tpu_custom_call" | custom-call | flops 10737418240 | bytes 10485760 | tf_op jit(solution)/shard_map/attend_back/pallas_call | solution.py:807
  394.0 36.2 %attend_back.5 = (f32[1024,512]{1,0:T(8,128)}, bf16[1024,512]{1,0:T(8,128)(2,1)}, bf16[1024,512]{1,0:T(8,128)(2,1)}) custom-call(s32[7]{0:T(128)S(1)} %stack.82.refs_10_.place_ref, bf16[1024,1536]{1,0:T(8,128)(2,1)} %get-tuple-element.102.qx_ref, bf16[1024,1536]{1,0:T(8,128)(2,1)} %collective-permute-done.14.kb_ref.vb_ref.k_ref.v_ref, ...), custom_call_target="tpu_custom_call" | custom-call | flops 21474836480 | bytes 20971520 | tf_op jit(solution)/shard_map/attend_back/pallas_call | solution.py:807
  438.7 15.4 %attend_back.6.right_ref.gb_ref = bf16[3,1024,256]{2,1,0:T(8,128)(2,1)S(1)} custom-call(s32[7]{0:T(128)S(1)} %stack.82.refs_10_.place_ref, bf16[1024,1536]{1,0:T(8,128)(2,1)} %get-tuple-element.102.qx_ref, bf16[1024,1536]{1,0:T(8,128)(2,1)} %project.3.ka_ref.va_ref.k_ref.v_ref, bf16[1024,1536]{1,0:T(8,128)(2,1)} %project.3.ka_ref.va_ref.k_ref.v_ref, ...), custom_call_target="tpu_custom_call" | custom-call | flops 10737418240 | bytes 10485760 | tf_op jit(solution)/shard_map/attend_back/pallas_call | solution.py:807
  462.6 19.5 %collective-permute-done.33 = bf16[192,3840]{1,0:T(8,128)(2,1)} collective-permute-done((bf16[192,3840]{1,0:T(8,128)(2,1)}, bf16[192,3840]{1,0:T(8,128)(2,1)}, u32[]{:S(2)}, u32[]{:S(2)}) %collective-permute-start.33) | collective-permute-done | bytes 1474592 | tf_op jit(solution)/shard_map/ppermute | solution.py:404
  488.2 29.8 %attend_back.7.right_ref.ga_ref = bf16[3,1024,512]{2,1,0:T(8,128)(2,1)} custom-call(s32[7]{0:T(128)S(1)} %stack.82.refs_10_.place_ref, bf16[1024,1536]{1,0:T(8,128)(2,1)} %get-tuple-element.102.qx_ref, bf16[1024,1536]{1,0:T(8,128)(2,1)} %project.3.ka_ref.va_ref.k_ref.v_ref, bf16[1024,1536]{1,0:T(8,128)(2,1)} %project.3.ka_ref.va_ref.k_ref.v_ref, ...), custom_call_target="tpu_custom_call" | custom-call | flops 21474836480 | bytes 20971520 | tf_op jit(solution)/shard_map/attend_back/pallas_call | solution.py:807
  529.7 4.3 keep_rows.4
  551.3 7.8 %input_rows.1 = bf16[1024,768]{1,0:T(8,128)(2,1)S(1)} custom-call(bf16[3,1024,512]{2,1,0:T(8,128)(2,1)} %attend_back.7.right_ref.ga_ref, bf16[3,1024,256]{2,1,0:T(8,128)(2,1)S(1)} %attend_back.6.right_ref.gb_ref, bf16[3,768,768]{2,1,0:T(8,128)(2,1)} %bitcast.170, bf16[3,768,768]{2,1,0:T(8,128)(2,1)} %bitcast.171, f32[1024,768]{1,0:T(8,128)} %get-tuple-element.150.attn_ref), custom_call_target="tpu_custom_call" | custom-call | flops 3623878656 | bytes 11010048 | tf_op jit(solution)/shard_map/input_rows/pallas_call | solution.py:1292
  568.1 5.2 convolution_convert_fusion
  585.3 5.3 subtract_bitcast_fusion
  598.6 8.6 %fusion = f32[1,192,6144]{2,1,0:T(8,128)} fusion(f32[1,192,6144]{2,1,0:T(8,128)} %param.35, f32[192,1536]{1,0:T(8,128)S(1)} %copy-done.56, f32[192,1536]{1,0:T(8,128)S(1)} %copy-done.53, f32[192,1536]{1,0:T(8,128)S(1)} %copy-done.55, f32[192,1536]{1,0:T(8,128)S(1)} %copy-done.51, f32[8,1280]{1,0:T(8,128)S(1)} %copy-done.69, f32[8,7680]{1,0:T(8,128)S(1)} %add_multiply_fusion), kind=kOutput, calls=%fused_computation.1 | convolution fusion | flops 119144448 | bytes 14360576 | tf_op jit(solution)/shard_map/dot_general | solution.py:1359
  607.1 10.2 %collective-permute-done.43 = bf16[192,2304]{1,0:T(8,128)(2,1)S(1)} collective-permute-done((bf16[192,2304]{1,0:T(8,128)(2,1)S(1)}, bf16[192,2304]{1,0:T(8,128)(2,1)S(1)}, u32[]{:S(2)}, u32[]{:S(2)}) %collective-permute-start.43) | collective-permute-done | bytes 884768 | tf_op jit(solution)/shard_map/ppermute | solution.py:404
  639.4 4.8 collective-permute-done.41
  644.1 14.8 %collective-permute-done.42 = bf16[512,768]{1,0:T(8,128)(2,1)S(1)} collective-permute-done((bf16[512,768]{1,0:T(8,128)(2,1)}, bf16[512,768]{1,0:T(8,128)(2,1)S(1)}, u32[]{:S(2)}, u32[]{:S(2)}) %collective-permute-start.42) | collective-permute-done | bytes 786464 | tf_op jit(solution)/shard_map/ppermute | solution.py:404
  (416 shorter events, 240.7 us)
Async XLA Ops:
  7.2 86.8 %all-gather.3.cloned.1.call-start = ((), (), s32[]{:S(2)}) async-start(), calls=%async_computation | async-start | bytes 2396160 | tf_op jit(solution)/shard_map/all_gather | solution.py:1423
  14.6 45.4 %collective-permute-start = (s32[2]{0:T(128)S(1)}, s32[2]{0:T(128)S(1)}, u32[]{:S(2)}, u32[]{:S(2)}) collective-permute-start(s32[2]{0:T(128)S(1)} %copy-done.82), channel_id=1, source_target_pairs={{0,4},{1,5},{2,6},{3,7},{4,0},{5,1},{6,2},{7,3},{8,12},{9,13},{10,... | collective-permute-start | bytes 32 | tf_op jit(solution)/shard_map/ppermute | solution.py:404
  42.9 38.7 %collective-permute-start.1 = (bf16[512,768]{0,1:T(8,128)(2,1)}, bf16[512,768]{0,1:T(8,128)(2,1)S(1)}, u32[]{:S(2)}, u32[]{:S(2)}) collective-permute-start(bf16[512,768]{0,1:T(8,128)(2,1)} %bitcast.196), channel_id=1, source_target_pairs={{0,0},{1,1},{2,4},{3,5},{4,2},{5,3},{6,6},{7,7},{8,8},{9,9},{10,12... | collective-permute-start | bytes 2359304 | tf_op jit(solution)/shard_map/ppermute | solution.py:404
  46.0 45.4 %collective-permute-start.2 = (bf16[512,768]{0,1:T(8,128)(2,1)}, bf16[512,768]{0,1:T(8,128)(2,1)}, u32[]{:S(2)}, u32[]{:S(2)}) collective-permute-start(bf16[512,768]{0,1:T(8,128)(2,1)} %bitcast.8), channel_id=1, source_target_pairs={{0,1},{1,0},{2,5},{3,4},{4,3},{5,2},{6,7},{7,6},{8,9},{9,8},{10,13... | collective-permute-start | bytes 2359304 | tf_op jit(solution)/shard_map/ppermute | solution.py:404
  57.9 36.1 %collective-permute-start.10 = (bf16[288,768]{1,0:T(8,128)(2,1)}, bf16[288,768]{1,0:T(8,128)(2,1)}, u32[]{:S(2)}, u32[]{:S(2)}) collective-permute-start(bf16[288,768]{1,0:T(8,128)(2,1)} %pad_maximum_fusion.9.refs_0_), channel_id=1, source_target_pairs={{0,4},{1,5},{2,6},{3,7},{4,0},{5,1},{6,2},{7,3},{8,12},{9,13},{10,... | collective-permute-start | bytes 1327112 | tf_op jit(solution)/shard_map/ppermute | solution.py:404
  59.1 34.9 %collective-permute-start.11 = (bf16[288,768]{1,0:T(8,128)(2,1)}, bf16[288,768]{1,0:T(8,128)(2,1)}, u32[]{:S(2)}, u32[]{:S(2)}) collective-permute-start(bf16[288,768]{1,0:T(8,128)(2,1)} %collective-permute-done.6.refs_1_), channel_id=1, source_target_pairs={{0,4},{1,5},{2,6},{3,7},{4,0},{5,1},{6,2},{7,3},{8,12},{9,13},{10,... | collective-permute-start | bytes 1327112 | tf_op jit(solution)/shard_map/ppermute | solution.py:404
  60.0 34.0 %collective-permute-start.12 = (bf16[288,768]{1,0:T(8,128)(2,1)}, bf16[288,768]{1,0:T(8,128)(2,1)}, u32[]{:S(2)}, u32[]{:S(2)}) collective-permute-start(bf16[288,768]{1,0:T(8,128)(2,1)} %collective-permute-done.7.refs_2_), channel_id=1, source_target_pairs={{0,4},{1,5},{2,6},{3,7},{4,0},{5,1},{6,2},{7,3},{8,12},{9,13},{10,... | collective-permute-start | bytes 1327112 | tf_op jit(solution)/shard_map/ppermute | solution.py:404
  118.8 45.2 %collective-permute-start.15 = (bf16[1248,768]{1,0:T(8,128)(2,1)}, bf16[1248,768]{1,0:T(8,128)(2,1)}, u32[]{:S(2)}, u32[]{:S(2)}) collective-permute-start(bf16[1248,768]{1,0:T(8,128)(2,1)} %pad_maximum_fusion.refs_0_), channel_id=1, source_target_pairs={{0,8},{1,9},{2,10},{3,11},{4,12},{5,13},{6,14},{7,15},{8,0},{9,1},... | collective-permute-start | bytes 5750792 | tf_op jit(solution)/shard_map/ppermute | solution.py:404
  120.3 44.2 %collective-permute-start.16 = (bf16[1248,768]{1,0:T(8,128)(2,1)}, bf16[1248,768]{1,0:T(8,128)(2,1)}, u32[]{:S(2)}, u32[]{:S(2)}) collective-permute-start(bf16[1248,768]{1,0:T(8,128)(2,1)} %pad_maximum_fusion.refs_0_), channel_id=1, source_target_pairs={{0,16},{1,17},{2,18},{3,19},{4,20},{5,21},{6,22},{7,23},{8,24},{9,... | collective-permute-start | bytes 5750792 | tf_op jit(solution)/shard_map/ppermute | solution.py:404
  165.8 27.1 %collective-permute-start.20 = (bf16[1248,768]{1,0:T(8,128)(2,1)}, bf16[1248,768]{1,0:T(8,128)(2,1)}, u32[]{:S(2)}, u32[]{:S(2)}) collective-permute-start(bf16[1248,768]{1,0:T(8,128)(2,1)} %collective-permute-done.15.refs_1_), channel_id=1, source_target_pairs={{0,4},{1,5},{2,6},{3,7},{4,0},{5,1},{6,2},{7,3},{8,12},{9,13},{10,... | collective-permute-start | bytes 5750792 | tf_op jit(solution)/shard_map/ppermute | solution.py:404
  211.4 34.2 %collective-permute-start.23 = (bf16[512,768]{1,0:T(8,128)(2,1)}, bf16[512,768]{1,0:T(8,128)(2,1)}, u32[]{:S(2)}, u32[]{:S(2)}) collective-permute-start(bf16[512,768]{1,0:T(8,128)(2,1)} %get-tuple-element.233), channel_id=1, source_target_pairs={{0,0},{1,1},{2,4},{3,5},{4,2},{5,3},{6,6},{7,7},{8,8},{9,9},{10,12... | collective-permute-start | bytes 2359304 | tf_op jit(solution)/shard_map/ppermute | solution.py:404
  213.3 35.6 %collective-permute-start.24 = (bf16[512,768]{1,0:T(8,128)(2,1)}, bf16[512,768]{1,0:T(8,128)(2,1)}, u32[]{:S(2)}, u32[]{:S(2)}) collective-permute-start(bf16[512,768]{1,0:T(8,128)(2,1)} %get-tuple-element.232), channel_id=1, source_target_pairs={{0,1},{1,0},{2,5},{3,4},{4,3},{5,2},{6,7},{7,6},{8,9},{9,8},{10,13... | collective-permute-start | bytes 2359304 | tf_op jit(solution)/shard_map/ppermute | solution.py:404
  265.2 49.9 %collective-permute-start.27 = (bf16[768,1536]{1,0:T(8,128)(2,1)}, bf16[768,1536]{1,0:T(8,128)(2,1)}, u32[]{:S(2)}, u32[]{:S(2)}) collective-permute-start(bf16[768,1536]{1,0:T(8,128)(2,1)} %away_columns.1), channel_id=1, source_target_pairs={{0,4},{1,5},{2,6},{3,7},{4,0},{5,1},{6,2},{7,3},{8,12},{9,13},{10,... | collective-permute-start | bytes 7077896 | tf_op jit(solution)/shard_map/ppermute | solution.py:404
  272.5 30.6 %collective-permute-start.25 = (bf16[512,768]{1,0:T(8,128)(2,1)}, bf16[512,768]{1,0:T(8,128)(2,1)}, u32[]{:S(2)}, u32[]{:S(2)}) collective-permute-start(bf16[512,768]{1,0:T(8,128)(2,1)} %get-tuple-element.230), channel_id=1, source_target_pairs={{0,0},{1,1},{2,4},{3,5},{4,2},{5,3},{6,6},{7,7},{8,8},{9,9},{10,12... | collective-permute-start | bytes 2359304 | tf_op jit(solution)/shard_map/ppermute | solution.py:404
  276.3 36.1 %collective-permute-start.26 = (bf16[512,768]{1,0:T(8,128)(2,1)}, bf16[512,768]{1,0:T(8,128)(2,1)}, u32[]{:S(2)}, u32[]{:S(2)}) collective-permute-start(bf16[512,768]{1,0:T(8,128)(2,1)} %get-tuple-element.231), channel_id=1, source_target_pairs={{0,1},{1,0},{2,5},{3,4},{4,3},{5,2},{6,7},{7,6},{8,9},{9,8},{10,13... | collective-permute-start | bytes 2359304 | tf_op jit(solution)/shard_map/ppermute | solution.py:404
  299.1 58.8 %collective-permute-start.28 = (bf16[2,384,1536]{2,1,0:T(8,128)(2,1)}, bf16[2,384,1536]{2,1,0:T(8,128)(2,1)}, u32[]{:S(2)}, u32[]{:S(2)}) collective-permute-start(bf16[2,384,1536]{2,1,0:T(8,128)(2,1)} %get-tuple-element.125), channel_id=1, source_target_pairs={{0,4},{1,5},{2,6},{3,7},{4,0},{5,1},{6,2},{7,3},{8,12},{9,13},{10,... | collective-permute-start | bytes 7077896 | tf_op jit(solution)/shard_map/ppermute | solution.py:404
  322.9 40.4 %collective-permute-start.29 = (bf16[768,768]{1,0:T(8,128)(2,1)}, bf16[768,768]{1,0:T(8,128)(2,1)}, u32[]{:S(2)}, u32[]{:S(2)}) collective-permute-start(bf16[768,768]{1,0:T(8,128)(2,1)} %get-tuple-element.119), channel_id=1, source_target_pairs={{0,1},{1,0},{2,3},{3,2},{4,5},{5,4},{6,7},{7,6},{8,9},{9,8},{10,11... | collective-permute-start | bytes 3538952 | tf_op jit(solution)/shard_map/ppermute | solution.py:404
  349.2 38.8 %collective-permute-start.30 = (bf16[2,384,1536]{2,1,0:T(8,128)(2,1)}, bf16[2,384,1536]{2,1,0:T(8,128)(2,1)}, u32[]{:S(2)}, u32[]{:S(2)}) collective-permute-start(bf16[2,384,1536]{2,1,0:T(8,128)(2,1)} %get-tuple-element.129), channel_id=1, source_target_pairs={{0,4},{1,5},{2,6},{3,7},{4,0},{5,1},{6,2},{7,3},{8,12},{9,13},{10,... | collective-permute-start | bytes 7077896 | tf_op jit(solution)/shard_map/ppermute | solution.py:404
  357.3 29.4 %collective-permute-start.31 = (bf16[384,768]{1,0:T(8,128)(2,1)S(1)}, bf16[384,768]{1,0:T(8,128)(2,1)S(1)}, u32[]{:S(2)}, u32[]{:S(2)}) collective-permute-start(bf16[384,768]{1,0:T(8,128)(2,1)S(1)} %away_rows.3), channel_id=1, source_target_pairs={{0,4},{1,5},{2,6},{3,7},{4,0},{5,1},{6,2},{7,3},{8,12},{9,13},{10,... | collective-permute-start | bytes 1769480 | tf_op jit(solution)/shard_map/ppermute | solution.py:404
  361.3 69.0 %collective-permute-start.32 = (bf16[2,192,1536]{2,1,0:T(8,128)(2,1)}, bf16[2,192,1536]{2,1,0:T(8,128)(2,1)}, u32[]{:S(2)}, u32[]{:S(2)}) collective-permute-start(bf16[2,192,1536]{2,1,0:T(8,128)(2,1)} %get-tuple-element.214), channel_id=1, source_target_pairs={{0,1},{1,0},{2,3},{3,2},{4,5},{5,4},{6,7},{7,6},{8,9},{9,8},{10,11... | collective-permute-start | bytes 3538952 | tf_op jit(solution)/shard_map/ppermute | solution.py:404
  365.0 92.8 %collective-permute-start.46 = (bf16[768,768]{1,0:T(8,128)(2,1)S(1)}, bf16[768,768]{1,0:T(8,128)(2,1)}, u32[]{:S(2)}, u32[]{:S(2)}) collective-permute-start(bf16[768,768]{1,0:T(8,128)(2,1)S(1)} %add_convert_fusion.4), channel_id=1, source_target_pairs={{2,5},{3,4},{4,3},{5,2},{10,13},{11,12},{12,11},{13,10},{18,21},{1... | collective-permute-start | bytes 3538952 | tf_op jit(solution)/shard_map/ppermute | solution.py:404
  385.6 50.8 %collective-permute-start.47 = (f32[4,768]{1,0:T(4,128)S(1)}, f32[4,768]{1,0:T(4,128)S(1)}, u32[]{:S(2)}, u32[]{:S(2)}) collective-permute-start(f32[4,768]{1,0:T(4,128)S(1)} %pad_maximum_fusion.12), channel_id=1, source_target_pairs={{0,1},{1,0},{2,3},{3,2},{4,5},{5,4},{6,7},{7,6},{8,9},{9,8},{10,11... | collective-permute-start | bytes 36872 | tf_op jit(solution)/shard_map/ppermute | solution.py:404
  386.7 51.8 %collective-permute-start.34 = (bf16[1024,256]{1,0:T(8,128)(2,1)S(1)}, bf16[1024,256]{1,0:T(8,128)(2,1)S(1)}, u32[]{:S(2)}, u32[]{:S(2)}) collective-permute-start(bf16[1024,256]{1,0:T(8,128)(2,1)S(1)} %get-tuple-element.140), channel_id=1, source_target_pairs={{0,4},{1,5},{2,6},{3,7},{4,0},{5,1},{6,2},{7,3},{8,12},{9,13},{10,... | collective-permute-start | bytes 1572872 | tf_op jit(solution)/shard_map/ppermute | solution.py:404
  388.0 50.5 %collective-permute-start.35 = (bf16[1024,256]{1,0:T(8,128)(2,1)S(1)}, bf16[1024,256]{1,0:T(8,128)(2,1)S(1)}, u32[]{:S(2)}, u32[]{:S(2)}) collective-permute-start(bf16[1024,256]{1,0:T(8,128)(2,1)S(1)} %get-tuple-element.141), channel_id=1, source_target_pairs={{0,4},{1,5},{2,6},{3,7},{4,0},{5,1},{6,2},{7,3},{8,12},{9,13},{10,... | collective-permute-start | bytes 1572872 | tf_op jit(solution)/shard_map/ppermute | solution.py:404
  433.0 89.4 %collective-permute-start.45 = (bf16[2,192,1536]{2,1,0:T(8,128)(2,1)}, bf16[2,192,1536]{2,1,0:T(8,128)(2,1)}, u32[]{:S(2)}, u32[]{:S(2)}) collective-permute-start(bf16[2,192,1536]{2,1,0:T(8,128)(2,1)} %add_convert_fusion.1), channel_id=1, source_target_pairs={{2,5},{3,4},{4,3},{5,2},{10,13},{11,12},{12,11},{13,10},{18,21},{1... | collective-permute-start | bytes 3538952 | tf_op jit(solution)/shard_map/ppermute | solution.py:404
  436.4 45.7 %collective-permute-start.33 = (bf16[192,3840]{1,0:T(8,128)(2,1)}, bf16[192,3840]{1,0:T(8,128)(2,1)}, u32[]{:S(2)}, u32[]{:S(2)}) collective-permute-start(bf16[192,3840]{1,0:T(8,128)(2,1)} %pad_maximum_fusion.4), channel_id=1, source_target_pairs={{0,1},{1,0},{2,3},{3,2},{4,5},{5,4},{6,7},{7,6},{8,9},{9,8},{10,11... | collective-permute-start | bytes 4423688 | tf_op jit(solution)/shard_map/ppermute | solution.py:404
  438.6 49.6 %collective-permute-start.36 = (bf16[1024,512]{1,0:T(8,128)(2,1)}, bf16[1024,512]{1,0:T(8,128)(2,1)}, u32[]{:S(2)}, u32[]{:S(2)}) collective-permute-start(bf16[1024,512]{1,0:T(8,128)(2,1)} %get-tuple-element.144), channel_id=1, source_target_pairs={{0,4},{1,5},{2,6},{3,7},{4,0},{5,1},{6,2},{7,3},{8,12},{9,13},{10,... | collective-permute-start | bytes 3145736 | tf_op jit(solution)/shard_map/ppermute | solution.py:404
  457.9 30.3 %collective-permute-start.37 = (bf16[1024,512]{1,0:T(8,128)(2,1)}, bf16[1024,512]{1,0:T(8,128)(2,1)}, u32[]{:S(2)}, u32[]{:S(2)}) collective-permute-start(bf16[1024,512]{1,0:T(8,128)(2,1)} %get-tuple-element.145), channel_id=1, source_target_pairs={{0,4},{1,5},{2,6},{3,7},{4,0},{5,1},{6,2},{7,3},{8,12},{9,13},{10,... | collective-permute-start | bytes 3145736 | tf_op jit(solution)/shard_map/ppermute | solution.py:404
  461.8 64.5 %collective-permute-start.39 = (bf16[384,768]{1,0:T(8,128)(2,1)}, bf16[384,768]{1,0:T(8,128)(2,1)}, u32[]{:S(2)}, u32[]{:S(2)}) collective-permute-start(bf16[384,768]{1,0:T(8,128)(2,1)} %away_rows.5), channel_id=1, source_target_pairs={{0,4},{1,5},{2,6},{3,7},{4,0},{5,1},{6,2},{7,3},{8,12},{9,13},{10,... | collective-permute-start | bytes 1769480 | tf_op jit(solution)/shard_map/ppermute | solution.py:404
  484.4 49.5 %collective-permute-start.44 = (bf16[192,3840]{1,0:T(8,128)(2,1)S(1)}, bf16[192,3840]{1,0:T(8,128)(2,1)}, u32[]{:S(2)}, u32[]{:S(2)}) collective-permute-start(bf16[192,3840]{1,0:T(8,128)(2,1)S(1)} %add_convert_fusion), channel_id=1, source_target_pairs={{2,5},{3,4},{4,3},{5,2},{10,13},{11,12},{12,11},{13,10},{18,21},{1... | collective-permute-start | bytes 4423688 | tf_op jit(solution)/shard_map/ppermute | solution.py:404
  547.2 44.7 %collective-permute-start.40 = (bf16[192,2304]{1,0:T(8,128)(2,1)}, bf16[192,2304]{1,0:T(8,128)(2,1)}, u32[]{:S(2)}, u32[]{:S(2)}) collective-permute-start(bf16[192,2304]{1,0:T(8,128)(2,1)} %constant_dynamic-update-slice_fusion.2), channel_id=1, source_target_pairs={{0,1},{1,0},{2,3},{3,2},{4,5},{5,4},{6,7},{7,6},{8,9},{9,8},{10,11... | collective-permute-start | bytes 2654216 | tf_op jit(solution)/shard_map/ppermute | solution.py:404
  623.7 35.2 %collective-permute-start.42 = (bf16[512,768]{1,0:T(8,128)(2,1)}, bf16[512,768]{1,0:T(8,128)(2,1)S(1)}, u32[]{:S(2)}, u32[]{:S(2)}) collective-permute-start(bf16[512,768]{1,0:T(8,128)(2,1)} %get-tuple-element.227), channel_id=1, source_target_pairs={{0,1},{1,0},{2,5},{3,4},{4,3},{5,2},{6,7},{7,6},{8,9},{9,8},{10,13... | collective-permute-start | bytes 2359304 | tf_op jit(solution)/shard_map/ppermute | solution.py:404
  (116 other events, 1415.1 us)
Sparse Core Ops, SparseCore 0:
  11.5 51.9 all-gather.2

commit v2 on v1

--- a/solution.py
+++ b/solution.py
@@ -787,7 +787,7 @@
             dq_ref[...] = dq
 
 
-def attend_back(place, qx, kv, grad, mix, at, first, count, scale, more=()):
+def attend_back(place, qx, kv, grad, mix, at, first, count, scale, more=(), skip=0):
     rows = grad.shape[0]
     block = 512
     bf16 = jnp.bfloat16
@@ -797,7 +797,9 @@
     table = pl.BlockSpec((rows, LANES), lambda p, j: (0, 0))
     dims = (rows, count * LANES)
     if at == 0:
-        more_specs = [here, keys, keys, table, table]
+        ahead = pl.BlockSpec((rows, LANES), lambda p, j: (0, p + skip))
+        ahead_keys = pl.BlockSpec((block, LANES), lambda p, j: (j, p + skip))
+        more_specs = [ahead, ahead_keys, ahead_keys, table, table]
         out_specs = pl.BlockSpec((3, rows, LANES), lambda p, j: (0, 0, p))
         out_shape = shape((3, *dims), bf16)
     else:
@@ -1271,100 +1273,328 @@
     )(index, left_t, right, right, got, got)
 
 
-def input_kernel(ga_ref, gb_ref, wa_ref, wb_ref, attn_ref, out_ref, acc):
+def input_kernel(*refs):
+    grads, weights, (attn_ref, out_ref, acc) = refs[:3], refs[3:6], refs[6:]
     step = pl.program_id(0)
 
     @pl.when(step == 0)
     def _():
         acc[...] = attn_ref[...]
 
-    acc[...] += nn(ga_ref[0], wa_ref[0]) + nn(gb_ref[0], wb_ref[0])
+    grad = jnp.concatenate([ref[0] for ref in grads], axis=1)
+    weight = jnp.concatenate([ref[0] for ref in weights], axis=0)
+    acc[...] += nn(grad, weight)
 
     @pl.when(step == pl.num_programs(0) - 1)
     def _():
         out_ref[...] = acc[...].astype(out_ref.dtype)
 
 
-def input_rows_of(grads_a, grads_b, qkv_t, grad_attn):
+def input_rows_of(parts, qkv_t, grad_attn):
     rows = grad_attn.shape[0]
-    wide, narrow = grads_a.shape[2], grads_b.shape[2]
+    wide = parts[0].shape[2]
     fixed = lambda i: (0, 0)
+    weights = qkv_t.reshape(3, DIM, DIM)
     return pl.pallas_call(
         input_kernel,
         grid=(3,),
-        in_specs=[
-            pl.BlockSpec((1, rows, wide), lambda i: (i, 0, 0)),
-            pl.BlockSpec((1, rows, narrow), lambda i: (i, 0, 0)),
-            pl.BlockSpec((1, wide, DIM), lambda i: (i, 0, 0)),
-            pl.BlockSpec((1, narrow, DIM), lambda i: (i, wide // narrow, 0)),
-            pl.BlockSpec((rows, DIM), fixed),
-        ],
+        in_specs=[pl.BlockSpec((1, rows, wide), lambda i: (i, 0, 0))] * 3
+        + [
+            pl.BlockSpec((1, wide, DIM), functools.partial(lambda at, i: (i, at, 0), at))
+            for at in range(3)
+        ]
+        + [pl.BlockSpec((rows, DIM), fixed)],
         out_specs=pl.BlockSpec((rows, DIM), fixed),
         out_shape=shape((rows, DIM), jnp.bfloat16),
         scratch_shapes=[pltpu.VMEM((rows, DIM), jnp.float32)],
         compiler_params=limit(48),
         cost_estimate=cost(6 * rows * DIM * DIM, 14 * rows * DIM),
         name="input_rows",
-    )(grads_a, grads_b, qkv_t.reshape(3, DIM, DIM), qkv_t.reshape(3, DIM, DIM), grad_attn)
-
-
-def gram_schmidt_kernel(left_ref, basis_ref, *, segments):
+    )(*parts, weights, weights, weights, grad_attn)
+
+
+CHUNK = DIM
+
+
+def halves(values):
+    high = values.astype(jnp.bfloat16)
+    return high, (values - high.astype(jnp.float32)).astype(jnp.bfloat16)
+
+
+def exact_product(product, small, large):
+    small_high, small_low = halves(small)
+    large_high, large_low = halves(large)
+    both = product(jnp.concatenate([small_high, small_low], axis=0), large_high)
+    return both[:RANK] + both[RANK:] + product(small_high, large_low)
+
+
+def merge_main_kernel(
+    owner_ref, fs_ref, ff_ref, ss_ref, sf_ref, eg_ref, eo_ref, tg_ref, to_ref, mg_ref, mo_ref, p_ref
+):
+    f32 = jnp.float32
+    step = pl.program_id(0)
+    rows = mg_ref.shape[0]
+    owner = owner_ref[0] == 1
+    second = jnp.where(owner, ss_ref[...].astype(f32), sf_ref[...].astype(f32))
+
+    @pl.when(step == 0)
+    def _():
+        p_ref[...] = jnp.zeros_like(p_ref)
+
+    @pl.when(step < 8)
+    def _():
+        first = jnp.where(owner, fs_ref[0].astype(f32), ff_ref[0].astype(f32))
+        merged = jnp.where(step // 2 % 2 == 0, first, second) + eg_ref[0]
+        mg_ref[...] = merged
+        p_ref[:, :rows] += exact_product(nt, tg_ref[...], merged)
+
+    @pl.when(step == 8)
+    def _():
+        merged = second + eo_ref[0]
+        mo_ref[...] = merged
+        p_ref[:, 256 : 256 + rows] = exact_product(nt, to_ref[...], merged)
+
+
+def merge_main(owner, first, second, err_gate_up, err_out, start_gate_up, start_out):
+    rows = err_out.shape[1]
+    f32 = jnp.float32
+    last = 2 * FF // CHUNK - 1
+    fixed = lambda i: (0, 0)
+    first_spec = pl.BlockSpec((1, rows, CHUNK), lambda i: (jnp.minimum(i // 4, 1), 0, i % 2))
+    second_spec = pl.BlockSpec(
+        (rows, CHUNK), lambda i: (0, jnp.where(i > last, 4, 2 * (i // 4) + i % 2))
+    )
+    return pl.pallas_call(
+        merge_main_kernel,
+        grid=(last + 2,),
+        in_specs=[
+            pl.BlockSpec(memory_space=pltpu.SMEM),
+            first_spec,
+            first_spec,
+            second_spec,
+            second_spec,
+            pl.BlockSpec((1, rows, CHUNK), lambda i: (0, 0, jnp.minimum(i, last))),
+            pl.BlockSpec((1, rows, CHUNK), lambda i: (0, 0, 0)),
+            pl.BlockSpec((RANK, CHUNK), lambda i: (0, jnp.minimum(i, last))),
+            pl.BlockSpec((RANK, CHUNK), fixed),
+        ],
+        out_specs=[
+            pl.BlockSpec((rows, CHUNK), lambda i: (0, jnp.minimum(i, last))),
+            pl.BlockSpec((rows, CHUNK), fixed),
+            pl.BlockSpec((RANK, 512), fixed),
+        ],
+        out_shape=[
+            shape((rows, 2 * FF), f32),
+            shape((rows, CHUNK), f32),
+            shape((RANK, 512), f32),
+        ],
+        compiler_params=limit(48),
+        cost_estimate=cost(60 * rows * 7 * DIM, 14 * rows * 7 * DIM),
+        name="merge_main",
+    )(owner, *first, *second, err_gate_up, err_out, start_gate_up, start_out)
+
+
+def merge_down_kernel(owner_ref, s_ref, f_ref, e_ref, t_ref, m_ref, p_ref):
+    f32 = jnp.float32
+    own = jnp.where(owner_ref[0] == 1, s_ref[...].astype(f32), f_ref[...].astype(f32))
+    merged = own.T + e_ref[0]
+    m_ref[...] = merged
+    p_ref[...] = exact_product(nt, t_ref[...], merged)
+
+
+def merge_down(owner, own, err, start):
+    block = 256
+    f32 = jnp.float32
+    column = pl.BlockSpec((DIM, block), lambda i: (0, i))
+    return pl.pallas_call(
+        merge_down_kernel,
+        grid=(DIM // block,),
+        in_specs=[
+            pl.BlockSpec(memory_space=pltpu.SMEM),
+            column,
+            column,
+            pl.BlockSpec((1, block, DIM), lambda i: (0, i, 0)),
+            pl.BlockSpec((RANK, DIM), lambda i: (0, 0)),
+        ],
+        out_specs=[
+            pl.BlockSpec((block, DIM), lambda i: (i, 0)),
+            pl.BlockSpec((RANK, block), lambda i: (0, i)),
+        ],
+        out_shape=[shape((DIM, DIM), f32), shape((RANK, DIM), f32)],
+        compiler_params=limit(48),
+        cost_estimate=cost(60 * DIM * DIM, 12 * DIM * DIM),
+        name="merge_down",
+    )(owner, *own, err, start)
+
+
+def merge_qkv_kernel(owner_ref, *refs):
+    f32 = jnp.float32
+    near, far, (e_ref, t_ref, m_ref, p_ref) = refs[:3], refs[3:6], refs[6:]
+    rows = m_ref.shape[0]
+    near = jnp.concatenate([ref[...] for ref in near], axis=1).astype(f32)
+    far = jnp.concatenate([ref[...] for ref in far], axis=1).astype(f32)
+    merged = jnp.where(owner_ref[0] == 1, near, far) + e_ref[0]
+    m_ref[...] = merged
+
+    @pl.when(pl.program_id(0) == 0)
+    def _():
+        p_ref[...] = jnp.zeros_like(p_ref)
+
+    p_ref[:, :rows] += exact_product(nt, t_ref[...], merged)
+
+
+def merge_qkv(owner, near, far, err, start):
+    rows = err.shape[1]
+    f32 = jnp.float32
+    parts = [
+        pl.BlockSpec((rows, 256), functools.partial(lambda at, i: (0, at + i), at))
+        for at in (0, 0, 3)
+    ]
+    return pl.pallas_call(
+        merge_qkv_kernel,
+        grid=(3,),
+        in_specs=[pl.BlockSpec(memory_space=pltpu.SMEM)]
+        + parts
+        + parts
+        + [
+            pl.BlockSpec((1, rows, CHUNK), lambda i: (0, 0, i)),
+            pl.BlockSpec((RANK, CHUNK), lambda i: (0, i)),
+        ],
+        out_specs=[
+            pl.BlockSpec((rows, CHUNK), lambda i: (0, i)),
+            pl.BlockSpec((RANK, 256), lambda i: (0, 0)),
+        ],
+        out_shape=[shape((rows, 3 * DIM), f32), shape((RANK, 256), f32)],
+        compiler_params=limit(48),
+        cost_estimate=cost(60 * rows * 3 * DIM, 14 * rows * 3 * DIM),
+        name="merge_qkv",
+    )(owner, *near, *far, err, start)
+
+
+def chunk_spec(array, first, lead=()):
+    rows, count = array.shape[0], array.shape[1] // CHUNK
+    zeros = tuple(0 for _ in lead)
+    return pl.BlockSpec(
+        (*lead, rows, CHUNK), lambda i: (*zeros, 0, jnp.clip(i - first, 0, count - 1))
+    )
+
+
+def chunk_starts(arrays):
+    starts = [0]
+    for array in arrays:
+        starts.append(starts[-1] + array.shape[1] // CHUNK)
+    return starts
+
+
+def orthonormal_rows(values):
     row = lax.broadcasted_iota(jnp.int32, (RANK, 1), 0)
-    for start, width in segments:
-        values = left_ref[:, start : start + width]
-        for column in range(RANK):
-            vector = values[column : column + 1]
-            vector = vector * lax.rsqrt(jnp.sum(vector * vector, axis=1, keepdims=True) + 1e-06)
-            weights = jnp.sum(values * vector, axis=1, keepdims=True)
-            later = values - weights * vector
-            values = jnp.where(row > column, later, jnp.where(row == column, vector, values))
-        basis_ref[:, start : start + width] = values
-
-
-def compress(merged, starts, masters, moments, rates, rep, rider=None):
+    for column in range(RANK):
+        vector = values[column : column + 1]
+        vector = vector * lax.rsqrt(jnp.sum(vector * vector, axis=1, keepdims=True) + 1e-06)
+        weights = jnp.sum(values * vector, axis=1, keepdims=True)
+        later = values - weights * vector
+        values = jnp.where(row > column, later, jnp.where(row == column, vector, values))
+    return values
+
+
+def pull_kernel(left_ref, *refs, segments, starts):
+    count = len(segments)
+    merged = refs[:count]
+    basis_ref, out_ref = refs[count:]
+    step = pl.program_id(0)
+
+    @pl.when(step == 0)
+    def _():
+        for start, width in segments:
+            part = slice(start, start + (width + 255) // 256 * 256)
+            basis_ref[:, part] = orthonormal_rows(left_ref[:, part] * (1.0 / REPS))
+
+    for at, (start, width) in enumerate(segments):
+
+        @pl.when((step >= starts[at]) & (step < starts[at + 1]))
+        def _():
+            basis = basis_ref[:, start : start + width]
+            out_ref[...] = exact_product(nn, basis, merged[at][...]).astype(out_ref.dtype)
+
+
+def pull(left, merged, segments):
+    starts = chunk_starts(merged)
+    total = sum(array.size for array in merged)
+    fixed = pl.BlockSpec(left.shape, lambda i: (0, 0))
+    return pl.pallas_call(
+        functools.partial(pull_kernel, segments=segments, starts=starts),
+        grid=(starts[-1],),
+        in_specs=[fixed] + [chunk_spec(array, at) for array, at in zip(merged, starts)],
+        out_specs=[fixed, pl.BlockSpec((RANK, CHUNK), lambda i: (0, i))],
+        out_shape=[
+            shape(left.shape, jnp.float32),
+            shape((RANK, starts[-1] * CHUNK), jnp.bfloat16),
+        ],
+        compiler_params=limit(48),
+        cost_estimate=cost(48 * total, 4 * total),
+        name="pull",
+    )(left, *merged)
+
+
+def new_errors_kernel(basis_ref, factor_ref, *refs, segments, starts):
+    count = len(segments)
+    step = pl.program_id(0)
+    for at, (start, width) in enumerate(segments):
+        merged, out = refs[at], refs[count + at]
+
+        @pl.when((step >= starts[at]) & (step < starts[at + 1]))
+        def _():
+            basis_high, basis_low = halves(basis_ref[:, start : start + width])
+            factor_high, factor_low = halves(factor_ref[...])
+            left = jnp.concatenate([basis_high, basis_low, basis_high], axis=0)
+            right = jnp.concatenate([factor_high, factor_high, factor_low], axis=0)
+            approx = lax.dot_general(
+                left, right, (((0,), (0,)), ((), ())), preferred_element_type=jnp.float32
+            )
+            out[0] = merged[...] - approx
+
+
+def new_errors_of(bases, factors, merged, segments):
+    starts = chunk_starts(merged)
+    total = sum(array.size for array in merged)
+    return pl.pallas_call(
+        functools.partial(new_errors_kernel, segments=segments, starts=starts),
+        grid=(starts[-1],),
+        in_specs=[
+            pl.BlockSpec(bases.shape, lambda i: (0, 0)),
+            pl.BlockSpec((RANK, CHUNK), lambda i: (0, i)),
+        ]
+        + [chunk_spec(array, at) for array, at in zip(merged, starts)],
+        out_specs=[chunk_spec(array, at, (1,)) for array, at in zip(merged, starts)],
+        out_shape=[shape((1, *array.shape), jnp.float32) for array in merged],
+        compiler_params=limit(48),
+        cost_estimate=cost(48 * total, 8 * total),
+        name="new_errors",
+    )(bases, factors, *merged)
+
+
+def compress(left, merged, segments, masters, moments, rates, rep):
     highest = lax.Precision.HIGHEST
-    lefts = []
-    places = []
-    segments = []
-    at = 0
-    for block, start_set in zip(merged, starts):
-        left = lax.dot_general(start_set[0], block, (((0,), (1,)), ((), ())), precision=highest)
-        size = left.shape[1]
-        padded = (size + 255) // 256 * 256
-        lefts.append(jnp.pad(left, ((0, 0), (0, padded - size))))
-        places.append((at, size))
-        segments.append((at, padded))
-        at += padded
-    if rider is not None:
-        lefts.append(rider)
-    packed = plane_sum(jnp.concatenate(lefts, axis=1)) / REPS
-    rider = packed[:, at:]
-    packed = packed[:, :at]
-    basis_all = pl.pallas_call(
-        functools.partial(gram_schmidt_kernel, segments=tuple(segments)),
-        out_shape=shape(packed.shape, jnp.float32),
-        name="gram_schmidt",
-    )(packed)
-    bases = [basis_all[:, at : at + size] for at, size in places]
-    pulled = [jnp.dot(basis, block, precision=highest) for basis, block in zip(bases, merged)]
-    widths = [part.shape[1] for part in pulled]
-    summed = plane_sum_half(jnp.concatenate(pulled, axis=1)) / REPS
+    bases, pulled = pull(left, merged, segments)
+    summed = plane_sum_half(pulled) / REPS
+    errors = new_errors_of(bases, summed, merged, segments)
     results = []
     at = 0
-    for block, basis, size, master, moment, rate in zip(
-        merged, bases, widths, masters, moments, rates
+    for (start, width), block, error, master, moment, rate in zip(
+        segments, merged, errors, masters, moments, rates
     ):
+        basis = bases[:, start : start + width]
+        size = block.shape[1]
         factor = summed[:, at : at + size]
-        at += size
-        approx = lax.dot_general(basis, factor, (((0,), (0,)), ((), ())), precision=highest)
         col_count = master.shape[1]
-        piece = lax.dynamic_slice_in_dim(factor, rep * col_count, col_count, 1)
+        piece = lax.dynamic_slice_in_dim(summed, at + rep * col_count, col_count, 1)
         piece = lax.dot_general(basis, piece, (((0,), (0,)), ((), ())), precision=highest)
         moment_new = MOMENTUM * moment + piece
         results.append(
-            (master - rate * moment_new, moment_new, (block - approx)[None], basis.T, factor.T[None])
+            (master - rate * moment_new, moment_new, error, basis.T, factor.T[None])
         )
-    return results, rider
+        at += size
+    return results
 
 
 def fast_device(
@@ -1505,7 +1735,8 @@
         return (mine.astype(f32) + pair.astype(f32)).astype(bf16)
 
     branch_t = branch.T
-    down_got = sibling(away_columns(index, branch_t, hidden, DIM))
+    down_away = away_columns(index, branch_t, hidden, DIM)
+    down_got = sibling(down_away)
     normed_t = normed_half.T
     away_1, keep_1, partial = feed_back(
         index, grad_second, branch, factor, stacked, normed_t, 0
@@ -1513,107 +1744,111 @@
     got_1 = sibling(away_1)
     down_mine, down_theirs = keep_columns(index, branch_t, hidden, down_got, DIM)
     down_pair = pair_z(down_theirs)
+    first_mine, first_theirs = core_sum(keep_1, got_1)
+    first_pair = pair_z(first_theirs)
     away_2, keep_2, grad_attn, grad_attn_half, grad_mix, vec_one = feed_back(
         index, after(partial, down_mine, down_theirs, mixed_out), branch, factor,
         stacked, normed_t, 2, (hat, rstd, layer_norm_gains, stacked),
     )
     got_2 = sibling(away_2)
-    first_mine, first_theirs = core_sum(after(keep_1, grad_mix), got_1)
-    first_pair = pair_z(first_theirs)
     mix_t = mix.T
     out_got = sibling(away_rows(index, mix_t, grad_attn_half, DIM))
     down_sum = add(down_mine, after(down_pair, grad_mix))
     down_far = to_owner(down_sum)
 
-    def back(grads, kv_set, at, first, count, more=()):
-        return attend_back(place, qx, kv_set, grads, mix, at, first, count, scale, more)
+    def back(grads, kv_set, at, first, count, more=(), skip=0):
+        return attend_back(place, qx, kv_set, grads, mix, at, first, count, scale, more, skip)
 
     def join(pair, single):
         return jnp.concatenate([pair[0], pair[1], single], axis=1)
 
     vectors = jnp.concatenate([vec_one, vec_two], axis=0)
-    grads = after(grad_mix, first_mine, first_theirs, down_sum)
-    dq_2, dk_2, dv_2 = back(grads, kv_other, 2, 4, 2)
-    other_2 = sibling(dk_2), sibling(dv_2)
-    second_mine, second_theirs = core_sum(keep_2, after(got_2, dq_2))
-    out_mine, out_theirs = keep_rows(index, mix_t, grad_attn_half, after(out_got, dq_2), DIM)
+    second_mine, second_theirs = core_sum(keep_2, got_2)
+    out_mine, out_theirs = keep_rows(index, mix_t, grad_attn_half, out_got, DIM)
     second_mine = join(second_mine, out_mine)
     second_theirs = join(second_theirs, out_theirs)
     second_pair = pair_z(second_theirs)
-    vectors = after(vectors, dq_2)
-    vectors_pair = pair_z(vectors)
-    grads = after(grads, second_mine, second_theirs)
+    grads = after(grad_mix, down_sum, second_mine, second_theirs)
+    dq_2, dk_2, dv_2 = back(grads, kv_other, 2, 4, 2)
+    other_2 = sibling(dk_2), sibling(dv_2)
+    first_sum = add(first_mine, after(first_pair, dq_2))
+    first_far = to_owner(first_sum)
+    vectors = vectors + pair_z(after(vectors, dq_2))
+    grads = after(grads, first_sum)
     dq_1, dk_1, dv_1 = back(grads, kv_other, 2, 0, 4)
     other_1 = sibling(dk_1), sibling(dv_1)
-    first_sum = add(first_mine, after(first_pair, dq_1))
-    first_far = to_owner(first_sum)
-    down_far = after(down_far, dq_1)
-    vectors = vectors + after(vectors_pair, dq_1)
-    vectors_mirror = mirror_z(vectors)
-    grads = after(grads, first_sum)
-    grads_b = back(grads, kv, 0, 4, 2, (dq_2, *other_2, cos, sin))
-    second_sum = add(second_mine, after(second_pair, grads_b))
+    second_sum = add(second_mine, after(second_pair, dq_1))
     second_far = to_owner(second_sum)
+    flag = owner.astype(jnp.int32).reshape(1)
+    merged_down, left_down = merge_down(
+        flag, (down_sum, after(down_far, dq_1)), err_down, start_down[0].T
+    )
     tokens_t = rows_in.T
-    qkv_got_b = sibling(away_rows(index, tokens_t, grads_b, 256))
-    vectors = vectors + after(vectors_mirror, grads_b)
+
+    def away_part(right):
+        return away_rows(index, tokens_t, right, 256)
+
+    def keep_part(right, got):
+        return keep_rows(index, tokens_t, right, got, 256)
+
     grads = after(grads, second_sum)
-    grads_a = back(grads, kv, 0, 0, 4, (dq_1, *other_1, cos, sin))
-    qkv_got_a = sibling(away_rows(index, tokens_t, grads_a, 512))
-    qkv_mine_b, qkv_theirs_b = keep_rows(index, tokens_t, grads_b, after(qkv_got_b, grads_a), 256)
-    qkv_mine_a, qkv_theirs_a = keep_rows(index, tokens_t, grads_a, qkv_got_a, 512)
-    qkv_theirs = jnp.concatenate([qkv_theirs_a, qkv_theirs_b], axis=1)
-    qkv_mine = jnp.concatenate([qkv_mine_a, qkv_mine_b], axis=1)
+    grads_2 = back(grads, kv, 0, 4, 2, (dq_2, *other_2, cos, sin))
+    away_2 = away_part(grads_2)
+    got_2 = sibling(away_2)
+    vectors = vectors + mirror_z(after(vectors, grads_2))
+    grads = after(grads, away_2, first_far, down_far)
+    grads_0 = back(grads, kv, 0, 0, 2, (dq_1, *other_1, cos, sin))
+    away_0 = away_part(grads_0)
+    got_0 = sibling(away_0)
+    mine_2, theirs_2 = keep_part(grads_2, after(got_2, away_0))
+    mine_0, theirs_0 = keep_part(grads_0, got_0)
+    qkv_mine = jnp.concatenate([mine_0, mine_2], axis=1)
+    qkv_theirs = jnp.concatenate([theirs_0, theirs_2], axis=1)
     qkv_pair = pair_z(qkv_theirs)
-    input_rows = input_rows_of(grads_a, grads_b, qkv_t, after(grad_attn, qkv_theirs))
-    qkv_sum = add(qkv_mine, after(qkv_pair, input_rows))
+    grads = after(grads, qkv_mine, qkv_theirs, second_far)
+    grads_1 = back(grads, kv, 0, 2, 2, (dq_1, *other_1, cos, sin), 2)
+    away_1 = away_part(grads_1)
+    got_1 = sibling(away_1)
+    qkv_sum = add(qkv_mine, after(qkv_pair, away_1))
     qkv_far = to_owner(qkv_sum)
-    input_grad = bring_back(after(input_rows, qkv_sum)).astype(f32)
-
-    def owned(own, far):
-        return jnp.where(owner, own, far).astype(f32)
-
-    own_down = lax.optimization_barrier(jnp.where(owner, down_sum, down_far).T).astype(f32)
-    own_first = owned(first_sum, first_far)
-    own_second = owned(second_sum, second_far)
-    half_ff = FF // 2
-    own_gate_up = jnp.concatenate(
-        [own_first[0], own_second[:, :half_ff], own_first[1], own_second[:, half_ff:FF]], axis=1
-    )
-    own_out = own_second[:, FF:]
-    own_qkv = owned(qkv_sum, qkv_far)
-    own_qkv = jnp.concatenate(
-        [
-            part
-            for i in range(3)
-            for part in (
-                own_qkv[:, 512 * i : 512 * i + 512],
-                own_qkv[:, 1536 + 256 * i : 1792 + 256 * i],
-            )
-        ],
-        axis=1,
-    )
-
-    early, norm_grad = compress(
-        (own_out + err_out[0], own_gate_up + err_gate_up[0], own_down + err_down[0]),
-        (start_out, start_gate_up, start_down),
-        (w_out, w_gate_up, w_down),
-        (mom_out, mom_gate_up, mom_down),
-        LEARN_RATES[1:],
-        rep,
-        vectors.reshape(RANK, width // 2),
-    )
-    norm_grad = norm_grad.reshape(4, width)
+    merged_gate_up, merged_out, left_main = merge_main(
+        flag, (first_sum, first_far), (second_sum, after(second_far, qkv_sum)),
+        err_gate_up, err_out, start_gate_up[0].T, start_out[0].T,
+    )
+    packed = jnp.concatenate([left_main, left_down, vectors.reshape(RANK, width // 2)], axis=1)
+    packed = plane_sum(packed)
+    mine_1, theirs_1 = keep_part(grads_1, after(got_1, left_main))
+    pair_1 = pair_z(theirs_1)
+    input_rows = input_rows_of(
+        (grads_0, grads_1, grads_2), qkv_t, after(grad_attn, mine_1, theirs_1)
+    )
+    input_grad = bring_back(input_rows).astype(f32)
+    sum_1 = add(mine_1, after(pair_1, input_rows))
+    far_1 = to_owner(sum_1)
+
+    norm_grad = packed[:, 1280:].reshape(4, width) / REPS
     params = jnp.stack(
         [layer_norm_gains[0], layer_norm_biases[0], layer_norm_gains[1], layer_norm_biases[1]]
     )
     norm_moment_new = MOMENTUM * norm_moments + norm_grad
     norm_new = params - NORM_RATE * norm_moment_new
-    late, _ = compress(
-        (after(own_qkv, *early[1][:3]) + err_qkv[0],), (start_qkv,), (w_qkv,), (mom_qkv,),
+    early = compress(
+        packed[:, :1280],
+        (merged_gate_up, merged_out, merged_down),
+        ((0, 192), (256, 192), (512, 768)),
+        (w_gate_up, w_out, w_down),
+        (mom_gate_up, mom_out, mom_down),
+        (LEARN_RATES[2], LEARN_RATES[1], LEARN_RATES[3]),
+        rep,
+    )
+    merged_qkv, left_qkv = merge_qkv(
+        flag, (qkv_sum, sum_1, qkv_sum), (qkv_far, far_1, qkv_far), err_qkv, start_qkv[0].T
+    )
+    late = compress(
+        plane_sum(left_qkv), (merged_qkv,), ((0, 192),), (w_qkv,), (mom_qkv,),
         LEARN_RATES[:1], rep,
     )
-    results = late + early
+    results = (late[0], early[1], early[0], early[2])
     new_weights, new_moments, new_errors, bases, factors = zip(*results)
     return (
         mixed_out,

time: 687 us -> 683 us (level)
  Pallas kernels: 309 us -> 351 us
  matrix products: 45.8 us -> 5.44 us
  local copies, waits for them, and re-layouts: 64.1 us -> 52.7 us
  other arithmetic: 43.6 us -> 34.9 us
  starting transfers between devices: 66.1 us -> 74 us
    dot_general x12 -> x0, matrix products: 39.7 us -> none  [the longest x4 19.3 us: compress(): lax.dot_general(basis, factor, (((0,), (0,)), ((), ())), precision=highest)]
    pallas_call x2 -> x7, Pallas kernels: 5.28 us -> 37.7 us  [the longest x2 12 us: new_errors_of(): pl.pallas_call(functools.partial(new_errors_kernel, segments=segments, st...]
    ppermute x61 -> x64, starting transfers between devices: 66.1 us -> 73.9 us  [send(): return lax.ppermute(values, AXES, pairs)]
    ppermute x61 -> x64, waiting for transfers between devices: 134 us -> 139 us  [send(): return lax.ppermute(values, AXES, pairs)]
    pallas_call x4 -> x5, Pallas kernels: 100 us -> 103 us  [attend_back(): pl.pallas_call(functools.partial(attend_back_kernel, at=at, scale=scale),...]
    unnamed x179 -> x173, local copies, waits for them, and re-layouts: 25.3 us -> 23 us
  transfers between devices with their start and end apart: 62 -> 65, of which waited for: 22 -> 25; matrix products, arithmetic and copies ran while one was open for 16% -> 9% of each run, Pallas kernels for 41% -> 45%
where the time goes in v2:
time: 683 us; the launch traced here: 673 us
  Pallas kernels  351 us (51%)
  waiting for transfers between devices  139 us (20%)
  starting transfers between devices  74 us (11%)
  local copies, waits for them, and re-layouts  52.7 us (8%)
  other arithmetic  34.9 us (5%)
  between operations  15.7 us (2%)
    ppermute x64, waiting for transfers between devices, send(): return lax.ppermute(values, AXES, pairs)  139 us
    pallas_call x5, Pallas kernels, attend_back(): pl.pallas_call(functools.partial(attend_back_kernel, at=at, scale=scale),...  103 us
    ppermute x64, starting transfers between devices, send(): return lax.ppermute(values, AXES, pairs)  73.9 us
    pallas_call x3, Pallas kernels, attend(): pl.pallas_call(attend_kernel, grid=(count, rows // block), in_specs=[pl.B...  57.8 us
    pallas_call x2, Pallas kernels, feed_back(): pl.pallas_call(feed_back_kernel, grid_spec=pltpu.PrefetchScalarGridSpec(n...  48 us
    pallas_call x1, Pallas kernels, feed_forward(): pl.pallas_call(feed_forward_kernel, grid=(tiles + 1,), in_specs=[whole, s...  25.8 us
    unnamed x173, local copies, waits for them, and re-layouts  23 us
    pallas_call x2, Pallas kernels, stack_pieces(): pl.pallas_call(stack_kernel, in_specs=[pl.BlockSpec(memory_space=pltpu.SM...  14.2 us
  transfers between devices with their start and end apart: 65, of which 25 were waited for; matrix products, arithmetic and copies ran while one was open for 9% of the time, Pallas kernels for 45%

profile of v2, /device:TPU:16, one launch (start us, length us, event | category | flops | bytes accessed | tf_op | source)
XLA Modules:
  0.0 672.8 jit_solution(14561592721311146541)
XLA Ops:
  14.6 13.5 %collective-permute-done.3 = bf16[288,192]{0,1:T(8,128)(2,1)S(1)} collective-permute-done((bf16[288,192]{0,1:T(8,128)(2,1)S(1)}, bf16[288,192]{0,1:T(8,128)(2,1)S(1)}, u32[]{:S(2)}, u32[]{:S(2)}) %collective-permute-start.3) | collective-permute-done | bytes 110624 | tf_op jit(solution)/shard_map/ppermute | solution.py:404
  28.1 8.8 %collective-permute-done.5 = bf16[288,192]{0,1:T(8,128)(2,1)S(1)} collective-permute-done((bf16[288,192]{0,1:T(8,128)(2,1)S(1)}, bf16[288,192]{0,1:T(8,128)(2,1)S(1)}, u32[]{:S(2)}, u32[]{:S(2)}) %collective-permute-start.5) | collective-permute-done | bytes 110624 | tf_op jit(solution)/shard_map/ppermute | solution.py:404
  46.0 4.3 collective-permute-start.2
  60.4 21.2 %collective-permute-done.1 = bf16[512,768]{0,1:T(8,128)(2,1)S(1)} collective-permute-done((bf16[512,768]{0,1:T(8,128)(2,1)}, bf16[512,768]{0,1:T(8,128)(2,1)S(1)}, u32[]{:S(2)}, u32[]{:S(2)}) %collective-permute-start.1) | collective-permute-done | bytes 786464 | tf_op jit(solution)/shard_map/ppermute | solution.py:404
  84.2 7.1 %collective-permute-done.2 = bf16[512,768]{0,1:T(8,128)(2,1)} collective-permute-done((bf16[512,768]{0,1:T(8,128)(2,1)}, bf16[512,768]{0,1:T(8,128)(2,1)}, u32[]{:S(2)}, u32[]{:S(2)}) %collective-permute-start.2) | collective-permute-done | bytes 786464 | tf_op jit(solution)/shard_map/ppermute | solution.py:404
  101.6 7.3 %project.3.ka_ref.va_ref.k_ref.v_ref = bf16[1024,1536]{1,0:T(8,128)(2,1)} custom-call(bf16[1024,768]{1,0:T(8,128)(2,1)S(1)} %copy.90.x_ref, bf16[2304,768]{1,0:T(8,128)(2,1)} %bitcast.127, f32[1024,128]{1,0:T(8,128)S(1)} %copy-done.25, f32[1024,128]{1,0:T(8,128)S(1)} %copy-done.21), custom_call_target="tpu_custom_call" | custom-call | flops 2415919104 | bytes 9437184 | tf_op jit(solution)/shard_map/project/pallas_call | solution.py:596
  122.5 19.2 %attend.3 = (bf16[1024,768]{1,0:T(8,128)(2,1)S(1)}, bf16[1024,1536]{1,0:T(8,128)(2,1)}) custom-call(s32[7]{0:T(128)S(1)} %stack.82.refs_10_.place_ref, bf16[1024,768]{1,0:T(8,128)(2,1)S(1)} %project.2.q_ref, bf16[1024,1536]{1,0:T(8,128)(2,1)} %project.3.ka_ref.va_ref.k_ref.v_ref, bf16[1024,1536]{1,0:T(8,128)(2,1)} %project.3.ka_ref.va_ref.k_ref.v_ref, ...), custom_call_target="tpu_custom_call" | custom-call | flops 17179869184 | bytes 8388608 | tf_op jit(solution)/shard_map/attend/pallas_call | solution.py:682
  141.7 19.4 %attend.4 = (bf16[1024,768]{1,0:T(8,128)(2,1)S(1)}, bf16[1024,1536]{1,0:T(8,128)(2,1)}) custom-call(s32[7]{0:T(128)S(1)} %stack.82.refs_10_.place_ref, bf16[1024,768]{1,0:T(8,128)(2,1)S(1)} %project.2.q_ref, bf16[1024,1536]{1,0:T(8,128)(2,1)} %project.3.ka_ref.va_ref.k_ref.v_ref, ...), custom_call_target="tpu_custom_call", output_to_operand_aliasing={{0}: (6, {}), {1}: (7, {})} | custom-call | flops 17179869184 | bytes 8388608 | tf_op jit(solution)/shard_map/attend/pallas_call | solution.py:682
  166.8 19.2 %attend.5 = (bf16[1024,768]{1,0:T(8,128)(2,1)S(1)}, bf16[1024,1536]{1,0:T(8,128)(2,1)}) custom-call(s32[7]{0:T(128)S(1)} %stack.82.refs_10_.place_ref, bf16[1024,768]{1,0:T(8,128)(2,1)S(1)} %project.2.q_ref, bf16[1024,1536]{1,0:T(8,128)(2,1)} %project.3.ka_ref.va_ref.k_ref.v_ref, ...), custom_call_target="tpu_custom_call", output_to_operand_aliasing={{0}: (6, {}), {1}: (7, {})} | custom-call | flops 17179869184 | bytes 8388608 | tf_op jit(solution)/shard_map/attend/pallas_call | solution.py:682
  190.0 4.1 collective-permute-done.22.refs_8_
  196.5 10.6 %stack_pieces.3.w_ref.wg_ref.wu_ref.wd_ref.refs_3_ = bf16[8,1248,768]{2,1,0:T(8,128)(2,1)} custom-call(s32[1]{0:T(128)} %bitcast.9.rep_ref, bf16[1248,768]{1,0:T(8,128)(2,1)} %pad_maximum_fusion.refs_0_, bf16[1248,768]{1,0:T(8,128)(2,1)} %collective-permute-done.15.refs_1_, bf16[1248,768]{1,0:T(8,128)(2,1)} %collective-permute-done.16.refs_2_, ...), custom_call_target="tpu_custom_call" | custom-call | bytes 30670848 | tf_op jit(solution)/shard_map/stack_pieces/pallas_call | solution.py:509
  210.7 5.4 out_norm.1
  216.8 25.8 %feed_forward.1 = (bf16[1024,3072]{1,0:T(8,128)(2,1)}, bf16[2,1024,3072]{2,1,0:T(8,128)(2,1)}, bf16[1024,768]{1,0:T(8,128)(2,1)}, f32[1024,768]{1,0:T(8,128)}) custom-call(f32[1024,768]{1,0:T(8,128)} %get-tuple-element.120.hat_ref.refs_0_, f32[2,768]{1,0:T(2,128)} %refs_2_.1, f32[2,768]{1,0:T(2,128)} %biases_ref.3, ...), custom_call_target="tpu_custom_call" | custom-call | flops 14495514624 | bytes 33030144 | tf_op jit(solution)/shard_map/feed_forward/pallas_call | solution.py:939
  245.9 6.5 norm_back.1
  256.4 5.8 away_columns.1
  274.5 21.7 %feed_back.2 = (bf16[2,384,1536]{2,1,0:T(8,128)(2,1)}, bf16[2,384,1536]{2,1,0:T(8,128)(2,1)}, f32[1024,768]{1,0:T(8,128)}) custom-call(s32[4]{0:T(128)} %copy-done.50, f32[1024,768]{1,0:T(8,128)} %get-tuple-element.126.grad_ref, bf16[1024,768]{1,0:T(8,128)(2,1)} %copy-done.5, bf16[2,1024,3072]{2,1,0:T(8,128)(2,1)} %get-tuple-element.128.factor_ref, ...), custom_call_target="tpu_custom_call" | custom-call | flops 12079595520 | bytes 18087936 | tf_op jit(solution)/shard_map/feed_back/pallas_call | solution.py:1136
  300.3 9.1 %collective-permute-done.26 = bf16[512,768]{1,0:T(8,128)(2,1)} collective-permute-done((bf16[512,768]{1,0:T(8,128)(2,1)}, bf16[512,768]{1,0:T(8,128)(2,1)}, u32[]{:S(2)}, u32[]{:S(2)}) %collective-permute-start.26) | collective-permute-done | bytes 786464 | tf_op jit(solution)/shard_map/ppermute | solution.py:404
  312.2 6.8 %keep_columns.1 = (bf16[768,768]{1,0:T(8,128)(2,1)S(1)}, bf16[768,768]{1,0:T(8,128)(2,1)}) custom-call(s32[4]{0:T(128)S(1)} %copy-done.51, bf16[768,1024]{1,0:T(8,128)(2,1)S(1)} %bitcast.136, bf16[1024,3072]{1,0:T(8,128)(2,1)} %get-tuple-element.131.right_ref.right_a_ref.right_b_ref, bf16[1024,3072]{1,0:T(8,128)(2,1)} %get-tuple-element.131.right_ref.right_a_ref.right_b_ref, ...), custom_call_target="tpu_custom_call" | custom-call | flops 2415919104 | bytes 7864320 | tf_op jit(solution)/shard_map/keep_columns/pallas_call | solution.py:1255
  320.0 26.3 %feed_back.3 = (bf16[2,384,1536]{2,1,0:T(8,128)(2,1)}, bf16[2,384,1536]{2,1,0:T(8,128)(2,1)}, f32[1024,768]{1,0:T(8,128)}, bf16[1024,768]{1,0:T(8,128)(2,1)}, bf...) custom-call(s32[4]{0:T(128)} %copy-done.50, f32[1024,768]{1,0:T(8,128)} %get-tuple-element.134.grad_ref, ...), custom_call_target="tpu_custom_call" | custom-call | flops 12079595520 | bytes 18087936 | tf_op jit(solution)/shard_map/feed_back/pallas_call | solution.py:1136
  359.5 16.0 %collective-permute-done.28 = bf16[768,768]{1,0:T(8,128)(2,1)} collective-permute-done((bf16[768,768]{1,0:T(8,128)(2,1)}, bf16[768,768]{1,0:T(8,128)(2,1)}, u32[]{:S(2)}, u32[]{:S(2)}) %collective-permute-start.28) | collective-permute-done | bytes 1179680 | tf_op jit(solution)/shard_map/ppermute | solution.py:404
  383.9 18.4 %attend_back.5 = (f32[1024,256]{1,0:T(8,128)S(1)}, bf16[1024,256]{1,0:T(8,128)(2,1)S(1)}, bf16[1024,256]{1,0:T(8,128)(2,1)S(1)}) custom-call(s32[7]{0:T(128)S(1)} %stack.82.refs_10_.place_ref, bf16[1024,1536]{1,0:T(8,128)(2,1)} %get-tuple-element.116.qx_ref, bf16[1024,1536]{1,0:T(8,128)(2,1)} %collective-permute-done.14.kb_ref.vb_ref.k_ref.v_ref, ...), custom_call_target="tpu_custom_call" | custom-call | flops 10737418240 | bytes 10485760 | tf_op jit(solution)/shard_map/attend_back/pallas_call | solution.py:809
  410.3 36.3 %attend_back.6 = (f32[1024,512]{1,0:T(8,128)}, bf16[1024,512]{1,0:T(8,128)(2,1)}, bf16[1024,512]{1,0:T(8,128)(2,1)}) custom-call(s32[7]{0:T(128)S(1)} %stack.82.refs_10_.place_ref, bf16[1024,1536]{1,0:T(8,128)(2,1)} %get-tuple-element.116.qx_ref, bf16[1024,1536]{1,0:T(8,128)(2,1)} %collective-permute-done.14.kb_ref.vb_ref.k_ref.v_ref, ...), custom_call_target="tpu_custom_call" | custom-call | flops 21474836480 | bytes 20971520 | tf_op jit(solution)/shard_map/attend_back/pallas_call | solution.py:809
  452.1 15.8 %attend_back.7.right_ref.refs_2_ = bf16[3,1024,256]{2,1,0:T(8,128)(2,1)S(1)} custom-call(s32[7]{0:T(128)S(1)} %stack.82.refs_10_.place_ref, bf16[1024,1536]{1,0:T(8,128)(2,1)} %get-tuple-element.116.qx_ref, bf16[1024,1536]{1,0:T(8,128)(2,1)} %project.3.ka_ref.va_ref.k_ref.v_ref, bf16[1024,1536]{1,0:T(8,128)(2,1)} %project.3.ka_ref.va_ref.k_ref.v_ref, ...), custom_call_target="tpu_custom_call" | custom-call | flops 10737418240 | bytes 10485760 | tf_op jit(solution)/shard_map/attend_back/pallas_call | solution.py:809
  470.7 17.0 %attend_back.8.right_ref.refs_0_ = bf16[3,1024,256]{2,1,0:T(8,128)(2,1)S(1)} custom-call(s32[7]{0:T(128)S(1)} %stack.82.refs_10_.place_ref, bf16[1024,1536]{1,0:T(8,128)(2,1)} %get-tuple-element.116.qx_ref, bf16[1024,1536]{1,0:T(8,128)(2,1)} %project.3.ka_ref.va_ref.k_ref.v_ref, bf16[1024,1536]{1,0:T(8,128)(2,1)} %project.3.ka_ref.va_ref.k_ref.v_ref, ...), custom_call_target="tpu_custom_call" | custom-call | flops 10737418240 | bytes 10485760 | tf_op jit(solution)/shard_map/attend_back/pallas_call | solution.py:809
  515.3 15.7 %attend_back.9.right_ref.refs_1_ = bf16[3,1024,256]{2,1,0:T(8,128)(2,1)S(1)} custom-call(s32[7]{0:T(128)S(1)} %stack.82.refs_10_.place_ref, bf16[1024,1536]{1,0:T(8,128)(2,1)} %get-tuple-element.116.qx_ref, bf16[1024,1536]{1,0:T(8,128)(2,1)} %project.3.ka_ref.va_ref.k_ref.v_ref, bf16[1024,1536]{1,0:T(8,128)(2,1)} %project.3.ka_ref.va_ref.k_ref.v_ref, ...), custom_call_target="tpu_custom_call" | custom-call | flops 10737418240 | bytes 10485760 | tf_op jit(solution)/shard_map/attend_back/pallas_call | solution.py:809
  533.9 10.3 %merge_main.1 = (f32[192,6144]{1,0:T(8,128)}, f32[192,768]{1,0:T(8,128)S(1)}, f32[8,512]{1,0:T(8,128)S(1)}) custom-call(s32[1]{0:T(128)} %bitcast.49.owner_ref, bf16[2,192,1536]{2,1,0:T(8,128)(2,1)S(1)} %copy-done.18, bf16[2,192,1536]{2,1,0:T(8,128)(2,1)S(1)} %copy-done.39, bf16[192,3840]{1,0:T(8,128)(2,1)} %add_convert_fusion.ss_ref, ...), custom_call_target="tpu_custom_call" | custom-call | flops 61931520 | bytes 14450688 | tf_op jit(solution)/shard_map/merge_main/pallas_call | solution.py:1367
  557.5 7.4 %pull.3 = (f32[8,1280]{1,0:T(8,128)S(1)}, bf16[8,7680]{1,0:T(8,128)(2,1)S(1)}) custom-call(f32[8,1280]{1,0:T(8,128)S(1)} %slice.127.left_ref, f32[192,6144]{1,0:T(8,128)} %get-tuple-element.182.refs_0_, f32[192,768]{1,0:T(8,128)S(1)} %copy-done.34, f32[768,768]{1,0:T(8,128)S(1)} %copy-done.7), custom_call_target="tpu_custom_call" | custom-call | flops 92012544 | bytes 7667712 | tf_op jit(solution)/shard_map/pull/pallas_call | solution.py:1524
  581.8 7.3 %input_rows.1 = bf16[1024,768]{1,0:T(8,128)(2,1)S(1)} custom-call(bf16[3,1024,256]{2,1,0:T(8,128)(2,1)S(1)} %copy-done.4, bf16[3,1024,256]{2,1,0:T(8,128)(2,1)S(1)} %attend_back.9.right_ref.refs_1_, bf16[3,1024,256]{2,1,0:T(8,128)(2,1)} %copy-done.1, bf16[3,768,768]{2,1,0:T(8,128)(2,1)} %bitcast.129, bf16[3,768,768]{2,1,0:T(8,128)(2,1)} %bitcast.130, ...), custom_call_target="tpu_custom_call" | custom-call | flops 3623878656 | bytes 11010048 | tf_op jit(solution)/shard_map/input_rows/pallas_call | solution.py:1298
  591.8 8.6 %collective-permute-done.49.refs_4_ = bf16[192,768]{1,0:T(8,128)(2,1)S(1)} collective-permute-done((bf16[192,768]{1,0:T(8,128)(2,1)S(1)}, bf16[192,768]{1,0:T(8,128)(2,1)S(1)}, u32[]{:S(2)}, u32[]{:S(2)}) %collective-permute-start.49) | collective-permute-done | bytes 294944 | tf_op jit(solution)/shard_map/ppermute | solution.py:404
  615.1 9.8 %new_errors.3 = (f32[1,192,6144]{2,1,0:T(8,128)}, f32[1,192,768]{2,1,0:T(8,128)}, f32[1,768,768]{2,1,0:T(8,128)}) custom-call(f32[8,1280]{1,0:T(8,128)S(1)} %get-tuple-element.185.basis_ref, f32[8,7680]{1,0:T(8,128)S(1)} %add_multiply_fusion.factor_ref, f32[192,6144]{1,0:T(8,128)} %get-tuple-element.182.refs_0_, f32[192,768]{1,0:T(8,128)S(1)} %copy-done.35, ...), custom_call_target="tpu_custom_call" | custom-call | flops 92012544 | bytes 15335424 | tf_op jit(solution)/shard_map/new_errors/pallas_call | solution.py:1560
  637.3 17.6 %collective-permute-done.45 = bf16[512,768]{1,0:T(8,128)(2,1)S(1)} collective-permute-done((bf16[512,768]{1,0:T(8,128)(2,1)S(1)}, bf16[512,768]{1,0:T(8,128)(2,1)S(1)}, u32[]{:S(2)}, u32[]{:S(2)}) %collective-permute-start.45) | collective-permute-done | bytes 786464 | tf_op jit(solution)/shard_map/ppermute | solution.py:404
  654.9 9.0 %collective-permute-done.46 = bf16[512,768]{1,0:T(8,128)(2,1)S(1)} collective-permute-done((bf16[512,768]{1,0:T(8,128)(2,1)S(1)}, bf16[512,768]{1,0:T(8,128)(2,1)S(1)}, u32[]{:S(2)}, u32[]{:S(2)}) %collective-permute-start.46) | collective-permute-done | bytes 786464 | tf_op jit(solution)/shard_map/ppermute | solution.py:404
  (403 shorter events, 225.8 us)
Async XLA Ops:
  7.2 86.4 %all-gather.3.cloned.1.call-start = ((), (), s32[]{:S(2)}) async-start(), calls=%async_computation | async-start | bytes 2396160 | tf_op jit(solution)/shard_map/all_gather | solution.py:1653
  14.6 45.4 %collective-permute-start = (s32[2]{0:T(128)S(1)}, s32[2]{0:T(128)S(1)}, u32[]{:S(2)}, u32[]{:S(2)}) collective-permute-start(s32[2]{0:T(128)S(1)} %copy-done.83), channel_id=1, source_target_pairs={{0,4},{1,5},{2,6},{3,7},{4,0},{5,1},{6,2},{7,3},{8,12},{9,13},{10,... | collective-permute-start | bytes 32 | tf_op jit(solution)/shard_map/ppermute | solution.py:404
  42.9 38.7 %collective-permute-start.1 = (bf16[512,768]{0,1:T(8,128)(2,1)}, bf16[512,768]{0,1:T(8,128)(2,1)S(1)}, u32[]{:S(2)}, u32[]{:S(2)}) collective-permute-start(bf16[512,768]{0,1:T(8,128)(2,1)} %bitcast.7), channel_id=1, source_target_pairs={{0,0},{1,1},{2,4},{3,5},{4,2},{5,3},{6,6},{7,7},{8,8},{9,9},{10,12... | collective-permute-start | bytes 2359304 | tf_op jit(solution)/shard_map/ppermute | solution.py:404
  46.0 45.4 %collective-permute-start.2 = (bf16[512,768]{0,1:T(8,128)(2,1)}, bf16[512,768]{0,1:T(8,128)(2,1)}, u32[]{:S(2)}, u32[]{:S(2)}) collective-permute-start(bf16[512,768]{0,1:T(8,128)(2,1)} %bitcast.8), channel_id=1, source_target_pairs={{0,1},{1,0},{2,5},{3,4},{4,3},{5,2},{6,7},{7,6},{8,9},{9,8},{10,13... | collective-permute-start | bytes 2359304 | tf_op jit(solution)/shard_map/ppermute | solution.py:404
  57.9 35.7 %collective-permute-start.10 = (bf16[288,768]{1,0:T(8,128)(2,1)}, bf16[288,768]{1,0:T(8,128)(2,1)}, u32[]{:S(2)}, u32[]{:S(2)}) collective-permute-start(bf16[288,768]{1,0:T(8,128)(2,1)} %pad_maximum_fusion.9.refs_0_), channel_id=1, source_target_pairs={{0,4},{1,5},{2,6},{3,7},{4,0},{5,1},{6,2},{7,3},{8,12},{9,13},{10,... | collective-permute-start | bytes 1327112 | tf_op jit(solution)/shard_map/ppermute | solution.py:404
  59.1 34.5 %collective-permute-start.11 = (bf16[288,768]{1,0:T(8,128)(2,1)}, bf16[288,768]{1,0:T(8,128)(2,1)}, u32[]{:S(2)}, u32[]{:S(2)}) collective-permute-start(bf16[288,768]{1,0:T(8,128)(2,1)} %collective-permute-done.6.refs_1_), channel_id=1, source_target_pairs={{0,4},{1,5},{2,6},{3,7},{4,0},{5,1},{6,2},{7,3},{8,12},{9,13},{10,... | collective-permute-start | bytes 1327112 | tf_op jit(solution)/shard_map/ppermute | solution.py:404
  59.9 33.7 %collective-permute-start.12 = (bf16[288,768]{1,0:T(8,128)(2,1)}, bf16[288,768]{1,0:T(8,128)(2,1)}, u32[]{:S(2)}, u32[]{:S(2)}) collective-permute-start(bf16[288,768]{1,0:T(8,128)(2,1)} %collective-permute-done.7.refs_2_), channel_id=1, source_target_pairs={{0,4},{1,5},{2,6},{3,7},{4,0},{5,1},{6,2},{7,3},{8,12},{9,13},{10,... | collective-permute-start | bytes 1327112 | tf_op jit(solution)/shard_map/ppermute | solution.py:404
  115.9 45.2 %collective-permute-start.15 = (bf16[1248,768]{1,0:T(8,128)(2,1)}, bf16[1248,768]{1,0:T(8,128)(2,1)}, u32[]{:S(2)}, u32[]{:S(2)}) collective-permute-start(bf16[1248,768]{1,0:T(8,128)(2,1)} %pad_maximum_fusion.refs_0_), channel_id=1, source_target_pairs={{0,8},{1,9},{2,10},{3,11},{4,12},{5,13},{6,14},{7,15},{8,0},{9,1},... | collective-permute-start | bytes 5750792 | tf_op jit(solution)/shard_map/ppermute | solution.py:404
  117.4 44.2 %collective-permute-start.16 = (bf16[1248,768]{1,0:T(8,128)(2,1)}, bf16[1248,768]{1,0:T(8,128)(2,1)}, u32[]{:S(2)}, u32[]{:S(2)}) collective-permute-start(bf16[1248,768]{1,0:T(8,128)(2,1)} %pad_maximum_fusion.refs_0_), channel_id=1, source_target_pairs={{0,16},{1,17},{2,18},{3,19},{4,20},{5,21},{6,22},{7,23},{8,24},{9,... | collective-permute-start | bytes 5750792 | tf_op jit(solution)/shard_map/ppermute | solution.py:404
  162.9 27.1 %collective-permute-start.20 = (bf16[1248,768]{1,0:T(8,128)(2,1)}, bf16[1248,768]{1,0:T(8,128)(2,1)}, u32[]{:S(2)}, u32[]{:S(2)}) collective-permute-start(bf16[1248,768]{1,0:T(8,128)(2,1)} %collective-permute-done.15.refs_1_), channel_id=1, source_target_pairs={{0,4},{1,5},{2,6},{3,7},{4,0},{5,1},{6,2},{7,3},{8,12},{9,13},{10,... | collective-permute-start | bytes 5750792 | tf_op jit(solution)/shard_map/ppermute | solution.py:404
  164.2 25.8 %collective-permute-start.21 = (bf16[1248,768]{1,0:T(8,128)(2,1)}, bf16[1248,768]{1,0:T(8,128)(2,1)}, u32[]{:S(2)}, u32[]{:S(2)}) collective-permute-start(bf16[1248,768]{1,0:T(8,128)(2,1)} %collective-permute-done.16.refs_2_), channel_id=1, source_target_pairs={{0,4},{1,5},{2,6},{3,7},{4,0},{5,1},{6,2},{7,3},{8,12},{9,13},{10,... | collective-permute-start | bytes 5750792 | tf_op jit(solution)/shard_map/ppermute | solution.py:404
  208.5 34.2 %collective-permute-start.23 = (bf16[512,768]{1,0:T(8,128)(2,1)}, bf16[512,768]{1,0:T(8,128)(2,1)}, u32[]{:S(2)}, u32[]{:S(2)}) collective-permute-start(bf16[512,768]{1,0:T(8,128)(2,1)} %get-tuple-element.203), channel_id=1, source_target_pairs={{0,0},{1,1},{2,4},{3,5},{4,2},{5,3},{6,6},{7,7},{8,8},{9,9},{10,12... | collective-permute-start | bytes 2359304 | tf_op jit(solution)/shard_map/ppermute | solution.py:404
  210.4 35.5 %collective-permute-start.24 = (bf16[512,768]{1,0:T(8,128)(2,1)}, bf16[512,768]{1,0:T(8,128)(2,1)}, u32[]{:S(2)}, u32[]{:S(2)}) collective-permute-start(bf16[512,768]{1,0:T(8,128)(2,1)} %get-tuple-element.202), channel_id=1, source_target_pairs={{0,1},{1,0},{2,5},{3,4},{4,3},{5,2},{6,7},{7,6},{8,9},{9,8},{10,13... | collective-permute-start | bytes 2359304 | tf_op jit(solution)/shard_map/ppermute | solution.py:404
  262.2 50.0 %collective-permute-start.27 = (bf16[768,1536]{1,0:T(8,128)(2,1)}, bf16[768,1536]{1,0:T(8,128)(2,1)}, u32[]{:S(2)}, u32[]{:S(2)}) collective-permute-start(bf16[768,1536]{1,0:T(8,128)(2,1)} %away_columns.1), channel_id=1, source_target_pairs={{0,4},{1,5},{2,6},{3,7},{4,0},{5,1},{6,2},{7,3},{8,12},{9,13},{10,... | collective-permute-start | bytes 7077896 | tf_op jit(solution)/shard_map/ppermute | solution.py:404
  269.6 30.7 %collective-permute-start.25 = (bf16[512,768]{1,0:T(8,128)(2,1)}, bf16[512,768]{1,0:T(8,128)(2,1)}, u32[]{:S(2)}, u32[]{:S(2)}) collective-permute-start(bf16[512,768]{1,0:T(8,128)(2,1)} %get-tuple-element.200), channel_id=1, source_target_pairs={{0,0},{1,1},{2,4},{3,5},{4,2},{5,3},{6,6},{7,7},{8,8},{9,9},{10,12... | collective-permute-start | bytes 2359304 | tf_op jit(solution)/shard_map/ppermute | solution.py:404
  273.4 36.0 %collective-permute-start.26 = (bf16[512,768]{1,0:T(8,128)(2,1)}, bf16[512,768]{1,0:T(8,128)(2,1)}, u32[]{:S(2)}, u32[]{:S(2)}) collective-permute-start(bf16[512,768]{1,0:T(8,128)(2,1)} %get-tuple-element.201), channel_id=1, source_target_pairs={{0,1},{1,0},{2,5},{3,4},{4,3},{5,2},{6,7},{7,6},{8,9},{9,8},{10,13... | collective-permute-start | bytes 2359304 | tf_op jit(solution)/shard_map/ppermute | solution.py:404
  296.2 56.2 %collective-permute-start.31 = (bf16[2,384,1536]{2,1,0:T(8,128)(2,1)}, bf16[2,384,1536]{2,1,0:T(8,128)(2,1)}, u32[]{:S(2)}, u32[]{:S(2)}) collective-permute-start(bf16[2,384,1536]{2,1,0:T(8,128)(2,1)} %get-tuple-element.145), channel_id=1, source_target_pairs={{0,4},{1,5},{2,6},{3,7},{4,0},{5,1},{6,2},{7,3},{8,12},{9,13},{10,... | collective-permute-start | bytes 7077896 | tf_op jit(solution)/shard_map/ppermute | solution.py:404
  346.3 32.8 %collective-permute-start.29 = (bf16[2,384,1536]{2,1,0:T(8,128)(2,1)}, bf16[2,384,1536]{2,1,0:T(8,128)(2,1)}, u32[]{:S(2)}, u32[]{:S(2)}) collective-permute-start(bf16[2,384,1536]{2,1,0:T(8,128)(2,1)} %get-tuple-element.139), channel_id=1, source_target_pairs={{0,4},{1,5},{2,6},{3,7},{4,0},{5,1},{6,2},{7,3},{8,12},{9,13},{10,... | collective-permute-start | bytes 7077896 | tf_op jit(solution)/shard_map/ppermute | solution.py:404
  346.4 29.1 %collective-permute-start.28 = (bf16[768,768]{1,0:T(8,128)(2,1)}, bf16[768,768]{1,0:T(8,128)(2,1)}, u32[]{:S(2)}, u32[]{:S(2)}) collective-permute-start(bf16[768,768]{1,0:T(8,128)(2,1)} %get-tuple-element.133), channel_id=1, source_target_pairs={{0,1},{1,0},{2,3},{3,2},{4,5},{5,4},{6,7},{7,6},{8,9},{9,8},{10,11... | collective-permute-start | bytes 3538952 | tf_op jit(solution)/shard_map/ppermute | solution.py:404
  355.4 47.9 %collective-permute-start.32 = (bf16[2,192,1536]{2,1,0:T(8,128)(2,1)}, bf16[2,192,1536]{2,1,0:T(8,128)(2,1)S(1)}, u32[]{:S(2)}, u32[]{:S(2)}) collective-permute-start(bf16[2,192,1536]{2,1,0:T(8,128)(2,1)} %fusion.2), channel_id=1, source_target_pairs={{0,1},{1,0},{2,3},{3,2},{4,5},{5,4},{6,7},{7,6},{8,9},{9,8},{10,11... | collective-permute-start | bytes 3538952 | tf_op jit(solution)/shard_map/ppermute | solution.py:404
  377.2 93.4 %collective-permute-start.37 = (bf16[768,768]{1,0:T(8,128)(2,1)S(1)}, bf16[768,768]{1,0:T(8,128)(2,1)S(1)}, u32[]{:S(2)}, u32[]{:S(2)}) collective-permute-start(bf16[768,768]{1,0:T(8,128)(2,1)S(1)} %add_convert_fusion.5.s_ref), channel_id=1, source_target_pairs={{2,5},{3,4},{4,3},{5,2},{10,13},{11,12},{12,11},{13,10},{18,21},{1... | collective-permute-start | bytes 3538952 | tf_op jit(solution)/shard_map/ppermute | solution.py:404
  382.8 63.8 %collective-permute-start.33 = (bf16[192,3840]{1,0:T(8,128)(2,1)}, bf16[192,3840]{1,0:T(8,128)(2,1)}, u32[]{:S(2)}, u32[]{:S(2)}) collective-permute-start(bf16[192,3840]{1,0:T(8,128)(2,1)} %pad_maximum_fusion.4), channel_id=1, source_target_pairs={{0,1},{1,0},{2,3},{3,2},{4,5},{5,4},{6,7},{7,6},{8,9},{9,8},{10,11... | collective-permute-start | bytes 4423688 | tf_op jit(solution)/shard_map/ppermute | solution.py:404
  405.0 65.6 %collective-permute-start.36 = (bf16[2,192,1536]{2,1,0:T(8,128)(2,1)S(1)}, bf16[2,192,1536]{2,1,0:T(8,128)(2,1)S(1)}, u32[]{:S(2)}, u32[]{:S(2)}) collective-permute-start(bf16[2,192,1536]{2,1,0:T(8,128)(2,1)S(1)} %fusion.fs_ref), channel_id=1, source_target_pairs={{2,5},{3,4},{4,3},{5,2},{10,13},{11,12},{12,11},{13,10},{18,21},{1... | collective-permute-start | bytes 3538952 | tf_op jit(solution)/shard_map/ppermute | solution.py:404
  409.8 40.1 %collective-permute-start.34 = (bf16[1024,256]{1,0:T(8,128)(2,1)S(1)}, bf16[1024,256]{1,0:T(8,128)(2,1)S(1)}, u32[]{:S(2)}, u32[]{:S(2)}) collective-permute-start(bf16[1024,256]{1,0:T(8,128)(2,1)S(1)} %get-tuple-element.152), channel_id=1, source_target_pairs={{0,4},{1,5},{2,6},{3,7},{4,0},{5,1},{6,2},{7,3},{8,12},{9,13},{10,... | collective-permute-start | bytes 1572872 | tf_op jit(solution)/shard_map/ppermute | solution.py:404
  409.8 40.4 %collective-permute-start.35 = (bf16[1024,256]{1,0:T(8,128)(2,1)S(1)}, bf16[1024,256]{1,0:T(8,128)(2,1)S(1)}, u32[]{:S(2)}, u32[]{:S(2)}) collective-permute-start(bf16[1024,256]{1,0:T(8,128)(2,1)S(1)} %get-tuple-element.153), channel_id=1, source_target_pairs={{0,4},{1,5},{2,6},{3,7},{4,0},{5,1},{6,2},{7,3},{8,12},{9,13},{10,... | collective-permute-start | bytes 1572872 | tf_op jit(solution)/shard_map/ppermute | solution.py:404
  446.6 24.1 %collective-permute-start.38 = (bf16[1024,512]{1,0:T(8,128)(2,1)}, bf16[1024,512]{1,0:T(8,128)(2,1)S(1)}, u32[]{:S(2)}, u32[]{:S(2)}) collective-permute-start(bf16[1024,512]{1,0:T(8,128)(2,1)} %get-tuple-element.155), channel_id=1, source_target_pairs={{0,4},{1,5},{2,6},{3,7},{4,0},{5,1},{6,2},{7,3},{8,12},{9,13},{10,... | collective-permute-start | bytes 3145736 | tf_op jit(solution)/shard_map/ppermute | solution.py:404
  450.2 65.1 %collective-permute-start.42 = (bf16[192,3840]{1,0:T(8,128)(2,1)}, bf16[192,3840]{1,0:T(8,128)(2,1)}, u32[]{:S(2)}, u32[]{:S(2)}) collective-permute-start(bf16[192,3840]{1,0:T(8,128)(2,1)} %add_convert_fusion.ss_ref), channel_id=1, source_target_pairs={{2,5},{3,4},{4,3},{5,2},{10,13},{11,12},{12,11},{13,10},{18,21},{1... | collective-permute-start | bytes 4423688 | tf_op jit(solution)/shard_map/ppermute | solution.py:404
  470.6 34.9 %collective-permute-start.41 = (bf16[384,768]{1,0:T(8,128)(2,1)}, bf16[384,768]{1,0:T(8,128)(2,1)}, u32[]{:S(2)}, u32[]{:S(2)}) collective-permute-start(bf16[384,768]{1,0:T(8,128)(2,1)} %away_rows.5), channel_id=1, source_target_pairs={{0,4},{1,5},{2,6},{3,7},{4,0},{5,1},{6,2},{7,3},{8,12},{9,13},{10,... | collective-permute-start | bytes 1769480 | tf_op jit(solution)/shard_map/ppermute | solution.py:404
  552.2 24.6 %collective-permute-start.43 = (bf16[384,768]{1,0:T(8,128)(2,1)}, bf16[384,768]{1,0:T(8,128)(2,1)}, u32[]{:S(2)}, u32[]{:S(2)}) collective-permute-start(bf16[384,768]{1,0:T(8,128)(2,1)} %copy-done.47), channel_id=1, source_target_pairs={{0,4},{1,5},{2,6},{3,7},{4,0},{5,1},{6,2},{7,3},{8,12},{9,13},{10,... | collective-permute-start | bytes 1769480 | tf_op jit(solution)/shard_map/ppermute | solution.py:404
  552.2 39.6 %collective-permute-start.48 = (bf16[192,1536]{1,0:T(8,128)(2,1)}, bf16[192,1536]{1,0:T(8,128)(2,1)}, u32[]{:S(2)}, u32[]{:S(2)}) collective-permute-start(bf16[192,1536]{1,0:T(8,128)(2,1)} %add_convert_fusion.6.refs_0_.refs_2_), channel_id=1, source_target_pairs={{2,5},{3,4},{4,3},{5,2},{10,13},{11,12},{12,11},{13,10},{18,21},{1... | collective-permute-start | bytes 1769480 | tf_op jit(solution)/shard_map/ppermute | solution.py:404
  626.5 28.3 %collective-permute-start.45 = (bf16[512,768]{1,0:T(8,128)(2,1)S(1)}, bf16[512,768]{1,0:T(8,128)(2,1)S(1)}, u32[]{:S(2)}, u32[]{:S(2)}) collective-permute-start(bf16[512,768]{1,0:T(8,128)(2,1)S(1)} %get-tuple-element.196), channel_id=1, source_target_pairs={{0,0},{1,1},{2,4},{3,5},{4,2},{5,3},{6,6},{7,7},{8,8},{9,9},{10,12... | collective-permute-start | bytes 2359304 | tf_op jit(solution)/shard_map/ppermute | solution.py:404
  628.4 35.4 %collective-permute-start.46 = (bf16[512,768]{1,0:T(8,128)(2,1)S(1)}, bf16[512,768]{1,0:T(8,128)(2,1)S(1)}, u32[]{:S(2)}, u32[]{:S(2)}) collective-permute-start(bf16[512,768]{1,0:T(8,128)(2,1)S(1)} %get-tuple-element.197), channel_id=1, source_target_pairs={{0,1},{1,0},{2,5},{3,4},{4,3},{5,2},{6,7},{7,6},{8,9},{9,8},{10,13... | collective-permute-start | bytes 2359304 | tf_op jit(solution)/shard_map/ppermute | solution.py:404
  (117 other events, 1081.3 us)
Sparse Core Ops, SparseCore 0:
  11.5 51.9 all-gather.2

commit v3 on v2

--- a/solution.py
+++ b/solution.py
@@ -399,7 +399,7 @@
     for rep in range(REPS):
         for shard in range(SHARDS):
             to = move(rep, shard)
-            if to is not None:
+            if to is not None and to != (rep, shard):
                 pairs.append((rep * SHARDS + shard, to[0] * SHARDS + to[1]))
     return lax.ppermute(values, AXES, pairs)
 
@@ -570,7 +570,8 @@
     return jnp.where(lane % HD < HD // 2, up, down)
 
 
-def project_kernel(x_ref, w_ref, cos_ref, sin_ref, out_ref, *, turned, scale):
+def project_kernel(x_ref, w_ref, cos_ref, sin_ref, *refs, turned, scale):
+    out_ref = refs[-1]
     values = nt(x_ref[...], w_ref[...])
 
     def turn():
@@ -589,7 +590,7 @@
             out_ref[...] = values.astype(out_ref.dtype)
 
 
-def project(rows_in, qkv_t, cos, sin, first, count, turned, scale):
+def project(rows_in, qkv_t, cos, sin, first, count, turned, scale, ahead=()):
     rows = rows_in.shape[0]
     tile = DIM
     fixed = lambda j: (0, 0)
@@ -601,13 +602,14 @@
             pl.BlockSpec((tile, DIM), lambda j: (j + first, 0)),
             pl.BlockSpec((rows, LANES), fixed),
             pl.BlockSpec((rows, LANES), fixed),
-        ],
+        ]
+        + [pl.BlockSpec(memory_space=pl.ANY)] * len(ahead),
         out_specs=pl.BlockSpec((rows, tile), lambda j: (0, j)),
         out_shape=shape((rows, count * tile), jnp.bfloat16),
         compiler_params=limit(48),
         cost_estimate=cost(2 * rows * DIM * tile * count, 4 * rows * DIM + 4 * count * tile * rows),
         name="project",
-    )(rows_in, qkv_t, cos, sin)
+    )(rows_in, qkv_t, cos, sin, *ahead)
 
 
 def lane_of(dims):
@@ -1314,6 +1316,7 @@
 
 
 CHUNK = DIM
+WIDE = 2 * DIM
 
 
 def halves(values):
@@ -1329,28 +1332,29 @@
 
 
 def merge_main_kernel(
-    owner_ref, fs_ref, ff_ref, ss_ref, sf_ref, eg_ref, eo_ref, tg_ref, to_ref, mg_ref, mo_ref, p_ref
+    owner_ref, fs_ref, ff_ref, ss_ref, sf_ref, os_ref, of_ref,
+    eg_ref, eo_ref, tg_ref, to_ref, mg_ref, mo_ref, p_ref,
 ):
     f32 = jnp.float32
     step = pl.program_id(0)
     rows = mg_ref.shape[0]
     owner = owner_ref[0] == 1
-    second = jnp.where(owner, ss_ref[...].astype(f32), sf_ref[...].astype(f32))
-
     @pl.when(step == 0)
     def _():
         p_ref[...] = jnp.zeros_like(p_ref)
 
-    @pl.when(step < 8)
+    @pl.when(step < 4)
     def _():
+        second = jnp.where(owner, ss_ref[...].astype(f32), sf_ref[...].astype(f32))
         first = jnp.where(owner, fs_ref[0].astype(f32), ff_ref[0].astype(f32))
-        merged = jnp.where(step // 2 % 2 == 0, first, second) + eg_ref[0]
+        merged = jnp.where(step % 2 == 0, first, second) + eg_ref[0]
         mg_ref[...] = merged
         p_ref[:, :rows] += exact_product(nt, tg_ref[...], merged)
 
-    @pl.when(step == 8)
+    @pl.when(step == 4)
     def _():
-        merged = second + eo_ref[0]
+        own = jnp.where(owner, os_ref[...].astype(f32), of_ref[...].astype(f32))
+        merged = own + eo_ref[0]
         mo_ref[...] = merged
         p_ref[:, 256 : 256 + rows] = exact_product(nt, to_ref[...], merged)
 
@@ -1358,12 +1362,11 @@
 def merge_main(owner, first, second, err_gate_up, err_out, start_gate_up, start_out):
     rows = err_out.shape[1]
     f32 = jnp.float32
-    last = 2 * FF // CHUNK - 1
+    last = 2 * FF // WIDE - 1
     fixed = lambda i: (0, 0)
-    first_spec = pl.BlockSpec((1, rows, CHUNK), lambda i: (jnp.minimum(i // 4, 1), 0, i % 2))
-    second_spec = pl.BlockSpec(
-        (rows, CHUNK), lambda i: (0, jnp.where(i > last, 4, 2 * (i // 4) + i % 2))
-    )
+    first_spec = pl.BlockSpec((1, rows, WIDE), lambda i: (jnp.minimum(i // 2, 1), 0, 0))
+    second_spec = pl.BlockSpec((rows, WIDE), lambda i: (0, jnp.minimum(i // 2, 1)))
+    out_spec = pl.BlockSpec((rows, CHUNK), lambda i: (0, 4))
     return pl.pallas_call(
         merge_main_kernel,
         grid=(last + 2,),
@@ -1373,13 +1376,15 @@
             first_spec,
             second_spec,
             second_spec,
-            pl.BlockSpec((1, rows, CHUNK), lambda i: (0, 0, jnp.minimum(i, last))),
+            out_spec,
+            out_spec,
+            pl.BlockSpec((1, rows, WIDE), lambda i: (0, 0, jnp.minimum(i, last))),
             pl.BlockSpec((1, rows, CHUNK), lambda i: (0, 0, 0)),
-            pl.BlockSpec((RANK, CHUNK), lambda i: (0, jnp.minimum(i, last))),
+            pl.BlockSpec((RANK, WIDE), lambda i: (0, jnp.minimum(i, last))),
             pl.BlockSpec((RANK, CHUNK), fixed),
         ],
         out_specs=[
-            pl.BlockSpec((rows, CHUNK), lambda i: (0, jnp.minimum(i, last))),
+            pl.BlockSpec((rows, WIDE), lambda i: (0, jnp.minimum(i, last))),
             pl.BlockSpec((rows, CHUNK), fixed),
             pl.BlockSpec((RANK, 512), fixed),
         ],
@@ -1391,7 +1396,7 @@
         compiler_params=limit(48),
         cost_estimate=cost(60 * rows * 7 * DIM, 14 * rows * 7 * DIM),
         name="merge_main",
-    )(owner, *first, *second, err_gate_up, err_out, start_gate_up, start_out)
+    )(owner, *first, *second, *second, err_gate_up, err_out, start_gate_up, start_out)
 
 
 def merge_down_kernel(owner_ref, s_ref, f_ref, e_ref, t_ref, m_ref, p_ref):
@@ -1471,18 +1476,24 @@
     )(owner, *near, *far, err, start)
 
 
-def chunk_spec(array, first, lead=()):
-    rows, count = array.shape[0], array.shape[1] // CHUNK
+def chunk_of(array):
+    return WIDE if array.shape[1] == 2 * FF else CHUNK
+
+
+def chunk_spec(rows, array, first, lead=(), ahead=0):
+    chunk = chunk_of(array)
+    count = array.shape[1] // chunk
     zeros = tuple(0 for _ in lead)
     return pl.BlockSpec(
-        (*lead, rows, CHUNK), lambda i: (*zeros, 0, jnp.clip(i - first, 0, count - 1))
+        (*lead, rows, chunk),
+        lambda i: (*zeros, 0, jnp.clip(i - first, 0, count - 1) + ahead // chunk),
     )
 
 
 def chunk_starts(arrays):
     starts = [0]
     for array in arrays:
-        starts.append(starts[-1] + array.shape[1] // CHUNK)
+        starts.append(starts[-1] + array.shape[1] // chunk_of(array))
     return starts
 
 
@@ -1500,7 +1511,7 @@
 def pull_kernel(left_ref, *refs, segments, starts):
     count = len(segments)
     merged = refs[:count]
-    basis_ref, out_ref = refs[count:]
+    basis_ref, outs = refs[-count - 1], refs[-count:]
     step = pl.program_id(0)
 
     @pl.when(step == 0)
@@ -1514,30 +1525,32 @@
         @pl.when((step >= starts[at]) & (step < starts[at + 1]))
         def _():
             basis = basis_ref[:, start : start + width]
-            out_ref[...] = exact_product(nn, basis, merged[at][...]).astype(out_ref.dtype)
-
-
-def pull(left, merged, segments):
+            outs[at][...] = exact_product(nn, basis, merged[at][...]).astype(outs[at].dtype)
+
+
+def pull(left, merged, segments, ahead=()):
     starts = chunk_starts(merged)
     total = sum(array.size for array in merged)
     fixed = pl.BlockSpec(left.shape, lambda i: (0, 0))
-    return pl.pallas_call(
+    results = pl.pallas_call(
         functools.partial(pull_kernel, segments=segments, starts=starts),
         grid=(starts[-1],),
-        in_specs=[fixed] + [chunk_spec(array, at) for array, at in zip(merged, starts)],
-        out_specs=[fixed, pl.BlockSpec((RANK, CHUNK), lambda i: (0, i))],
-        out_shape=[
-            shape(left.shape, jnp.float32),
-            shape((RANK, starts[-1] * CHUNK), jnp.bfloat16),
-        ],
+        in_specs=[fixed]
+        + [chunk_spec(array.shape[0], array, at) for array, at in zip(merged, starts)]
+        + [pl.BlockSpec(memory_space=pl.ANY)] * len(ahead),
+        out_specs=[fixed] + [chunk_spec(RANK, array, at) for array, at in zip(merged, starts)],
+        out_shape=[shape(left.shape, jnp.float32)]
+        + [shape((RANK, array.shape[1]), jnp.bfloat16) for array in merged],
         compiler_params=limit(48),
         cost_estimate=cost(48 * total, 4 * total),
         name="pull",
-    )(left, *merged)
-
-
-def new_errors_kernel(basis_ref, factor_ref, *refs, segments, starts):
+    )(left, *merged, *ahead)
+    return results[0], jnp.concatenate(results[1:], axis=1)
+
+
+def new_errors_kernel(basis_ref, *refs, segments, starts):
     count = len(segments)
+    factors, refs = refs[:count], refs[count:]
     step = pl.program_id(0)
     for at, (start, width) in enumerate(segments):
         merged, out = refs[at], refs[count + at]
@@ -1545,7 +1558,7 @@
         @pl.when((step >= starts[at]) & (step < starts[at + 1]))
         def _():
             basis_high, basis_low = halves(basis_ref[:, start : start + width])
-            factor_high, factor_low = halves(factor_ref[...])
+            factor_high, factor_low = halves(factors[at][...])
             left = jnp.concatenate([basis_high, basis_low, basis_high], axis=0)
             right = jnp.concatenate([factor_high, factor_high, factor_low], axis=0)
             approx = lax.dot_general(
@@ -1557,25 +1570,31 @@
 def new_errors_of(bases, factors, merged, segments):
     starts = chunk_starts(merged)
     total = sum(array.size for array in merged)
+    places = [0]
+    for array in merged:
+        places.append(places[-1] + array.shape[1])
     return pl.pallas_call(
         functools.partial(new_errors_kernel, segments=segments, starts=starts),
         grid=(starts[-1],),
-        in_specs=[
-            pl.BlockSpec(bases.shape, lambda i: (0, 0)),
-            pl.BlockSpec((RANK, CHUNK), lambda i: (0, i)),
+        in_specs=[pl.BlockSpec(bases.shape, lambda i: (0, 0))]
+        + [
+            chunk_spec(RANK, array, at, (), place)
+            for array, at, place in zip(merged, starts, places)
         ]
-        + [chunk_spec(array, at) for array, at in zip(merged, starts)],
-        out_specs=[chunk_spec(array, at, (1,)) for array, at in zip(merged, starts)],
+        + [chunk_spec(array.shape[0], array, at) for array, at in zip(merged, starts)],
+        out_specs=[
+            chunk_spec(array.shape[0], array, at, (1,)) for array, at in zip(merged, starts)
+        ],
         out_shape=[shape((1, *array.shape), jnp.float32) for array in merged],
         compiler_params=limit(48),
         cost_estimate=cost(48 * total, 8 * total),
         name="new_errors",
-    )(bases, factors, *merged)
-
-
-def compress(left, merged, segments, masters, moments, rates, rep):
+    )(bases, *[factors] * len(merged), *merged)
+
+
+def compress(left, merged, segments, masters, moments, rates, rep, ahead=()):
     highest = lax.Precision.HIGHEST
-    bases, pulled = pull(left, merged, segments)
+    bases, pulled = pull(left, merged, segments, ahead)
     summed = plane_sum_half(pulled) / REPS
     errors = new_errors_of(bases, summed, merged, segments)
     results = []
@@ -1629,15 +1648,19 @@
     local_len, width = tokens.shape[1:]
     scale = HD ** (-0.5)
 
-    def spread(values, *before):
+    stays = core == shard // 2
+
+    def spread(values):
         parts = []
         for parity in (0, 1):
             sent = lax.dynamic_index_in_dim(values, (shard + parity) % 2, 0, keepdims=False)
-            parts.append(send(sent, spread_move(parity)))
-        return after(parts, *before)
+            got = send(sent, spread_move(parity))
+            parts.append(jnp.where(stays, sent, got) if parity == 0 else got)
+        return parts
 
     def bring_back(rows):
         first = send(rows[:local_len], gather_move(0))
+        first = jnp.where(stays, rows[:local_len], first)
         second = send(rows[local_len:], gather_move(1))
         even = shard % 2 == 0
         return jnp.stack([jnp.where(even, first, second), jnp.where(even, second, first)])
@@ -1753,8 +1776,6 @@
     got_2 = sibling(away_2)
     mix_t = mix.T
     out_got = sibling(away_rows(index, mix_t, grad_attn_half, DIM))
-    down_sum = add(down_mine, after(down_pair, grad_mix))
-    down_far = to_owner(down_sum)
 
     def back(grads, kv_set, at, first, count, more=(), skip=0):
         return attend_back(place, qx, kv_set, grads, mix, at, first, count, scale, more, skip)
@@ -1768,13 +1789,15 @@
     second_mine = join(second_mine, out_mine)
     second_theirs = join(second_theirs, out_theirs)
     second_pair = pair_z(second_theirs)
-    grads = after(grad_mix, down_sum, second_mine, second_theirs)
+    grads = after(grad_mix, second_mine, second_theirs)
     dq_2, dk_2, dv_2 = back(grads, kv_other, 2, 4, 2)
     other_2 = sibling(dk_2), sibling(dv_2)
+    down_sum = add(down_mine, after(down_pair, dq_2))
+    down_far = to_owner(down_sum)
     first_sum = add(first_mine, after(first_pair, dq_2))
     first_far = to_owner(first_sum)
     vectors = vectors + pair_z(after(vectors, dq_2))
-    grads = after(grads, first_sum)
+    grads = after(grads, first_sum, down_sum)
     dq_1, dk_1, dv_1 = back(grads, kv_other, 2, 0, 4)
     other_1 = sibling(dk_1), sibling(dv_1)
     second_sum = add(second_mine, after(second_pair, dq_1))
@@ -1822,7 +1845,7 @@
     input_rows = input_rows_of(
         (grads_0, grads_1, grads_2), qkv_t, after(grad_attn, mine_1, theirs_1)
     )
-    input_grad = bring_back(input_rows).astype(f32)
+    input_grad = bring_back(input_rows)
     sum_1 = add(mine_1, after(pair_1, input_rows))
     far_1 = to_owner(sum_1)
 
@@ -1846,13 +1869,13 @@
     )
     late = compress(
         plane_sum(left_qkv), (merged_qkv,), ((0, 192),), (w_qkv,), (mom_qkv,),
-        LEARN_RATES[:1], rep,
+        LEARN_RATES[:1], rep, (input_grad.reshape(-1, width),),
     )
     results = (late[0], early[1], early[0], early[2])
     new_weights, new_moments, new_errors, bases, factors = zip(*results)
     return (
         mixed_out,
-        input_grad,
+        input_grad.astype(f32),
         *new_weights,
         *new_moments,
         *new_errors,

time: 683 us -> 679 us (level)
  Pallas kernels: 351 us -> 344 us
  starting transfers between devices: 74 us -> 67 us
    unnamed x173 -> x210, local copies, waits for them, and re-layouts: 23 us -> 33.8 us
    ppermute x64, starting transfers between devices: 73.9 us -> 67 us  [send(): return lax.ppermute(values, AXES, pairs)]
  transfers between devices with their start and end apart: 65 -> 65, of which waited for: 25 -> 28; matrix products, arithmetic and copies ran while one was open for 9% -> 8% of each run, Pallas kernels for 45% -> 45%
where the time goes in v3:
time: 679 us; the launch traced here: 667 us
  Pallas kernels  344 us (51%)
  waiting for transfers between devices  141 us (21%)
  starting transfers between devices  67 us (10%)
  local copies, waits for them, and re-layouts  57 us (8%)
  other arithmetic  36.4 us (5%)
  between operations  15.9 us (2%)
    ppermute x64, waiting for transfers between devices, send(): return lax.ppermute(values, AXES, pairs)  141 us
    pallas_call x5, Pallas kernels, attend_back(): pl.pallas_call(functools.partial(attend_back_kernel, at=at, scale=scale),...  103 us
    ppermute x64, starting transfers between devices, send(): return lax.ppermute(values, AXES, pairs)  67 us
    pallas_call x3, Pallas kernels, attend(): pl.pallas_call(attend_kernel, grid=(count, rows // block), in_specs=[pl.B...  58.1 us
    pallas_call x2, Pallas kernels, feed_back(): pl.pallas_call(feed_back_kernel, grid_spec=pltpu.PrefetchScalarGridSpec(n...  48 us
    unnamed x210, local copies, waits for them, and re-layouts  33.8 us
    pallas_call x1, Pallas kernels, feed_forward(): pl.pallas_call(feed_forward_kernel, grid=(tiles + 1,), in_specs=[whole, s...  25.8 us
    pallas_call x2, Pallas kernels, stack_pieces(): pl.pallas_call(stack_kernel, in_specs=[pl.BlockSpec(memory_space=pltpu.SM...  14.5 us
  transfers between devices with their start and end apart: 65, of which 28 were waited for; matrix products, arithmetic and copies ran while one was open for 8% of the time, Pallas kernels for 45%

profile of v3, /device:TPU:16, one launch (start us, length us, event | category | flops | bytes accessed | tf_op | source)
XLA Modules:
  0.0 667.1 jit_solution(3086637534569930520)
XLA Ops:
  15.7 4.7 collective-permute-start.1
  20.5 9.8 %collective-permute-done.3 = bf16[288,192]{0,1:T(8,128)(2,1)S(1)} collective-permute-done((bf16[288,192]{0,1:T(8,128)(2,1)S(1)}, bf16[288,192]{0,1:T(8,128)(2,1)S(1)}, u32[]{:S(2)}, u32[]{:S(2)}) %collective-permute-start.3) | collective-permute-done | bytes 110624 | tf_op jit(solution)/shard_map/ppermute | solution.py:404
  30.3 5.8 collective-permute-done.5
  43.5 5.0 collective-permute-done.7.refs_2_
  57.7 23.8 %collective-permute-done.1 = bf16[512,768]{1,0:T(8,128)(2,1)} collective-permute-done((bf16[512,768]{1,0:T(8,128)(2,1)S(1)}, bf16[512,768]{1,0:T(8,128)(2,1)}, u32[]{:S(2)}, u32[]{:S(2)}) %collective-permute-start.1) | collective-permute-done | bytes 786464 | tf_op jit(solution)/shard_map/ppermute | solution.py:404
  82.8 8.4 %collective-permute-done.2 = bf16[512,768]{1,0:T(8,128)(2,1)} collective-permute-done((bf16[512,768]{1,0:T(8,128)(2,1)}, bf16[512,768]{1,0:T(8,128)(2,1)}, u32[]{:S(2)}, u32[]{:S(2)}) %collective-permute-start.2) | collective-permute-done | bytes 786464 | tf_op jit(solution)/shard_map/ppermute | solution.py:404
  110.6 7.3 %project.3.ka_ref.va_ref.k_ref.v_ref = bf16[1024,1536]{1,0:T(8,128)(2,1)} custom-call(bf16[1024,768]{1,0:T(8,128)(2,1)S(1)} %get-tuple-element.199.x_ref, bf16[2304,768]{1,0:T(8,128)(2,1)} %bitcast.122, f32[1024,128]{1,0:T(8,128)S(1)} %pad_maximum_fusion.8.cos_ref.refs_3_, f32[1024,128]{1,0:T(8,128)S(1)} %pad_maximum_fusion.9.sin_ref.refs_4_), custom_call_target="tpu_custom_call" | custom-call | flops 2415919104 | bytes 9437184 | tf_op jit(solution)/shard_map/project/pallas_call | solution.py:597
  129.5 19.2 %attend.3 = (bf16[1024,768]{1,0:T(8,128)(2,1)S(1)}, bf16[1024,1536]{1,0:T(8,128)(2,1)}) custom-call(s32[7]{0:T(128)S(1)} %stack.82.refs_10_.place_ref, bf16[1024,768]{1,0:T(8,128)(2,1)S(1)} %project.2.q_ref, bf16[1024,1536]{1,0:T(8,128)(2,1)} %project.3.ka_ref.va_ref.k_ref.v_ref, bf16[1024,1536]{1,0:T(8,128)(2,1)} %project.3.ka_ref.va_ref.k_ref.v_ref, ...), custom_call_target="tpu_custom_call" | custom-call | flops 17179869184 | bytes 8388608 | tf_op jit(solution)/shard_map/attend/pallas_call | solution.py:684
  148.7 19.7 %attend.4 = (bf16[1024,768]{1,0:T(8,128)(2,1)S(1)}, bf16[1024,1536]{1,0:T(8,128)(2,1)}) custom-call(s32[7]{0:T(128)S(1)} %stack.82.refs_10_.place_ref, bf16[1024,768]{1,0:T(8,128)(2,1)S(1)} %project.2.q_ref, bf16[1024,1536]{1,0:T(8,128)(2,1)} %project.3.ka_ref.va_ref.k_ref.v_ref, ...), custom_call_target="tpu_custom_call", output_to_operand_aliasing={{0}: (6, {}), {1}: (7, {})} | custom-call | flops 17179869184 | bytes 8388608 | tf_op jit(solution)/shard_map/attend/pallas_call | solution.py:684
  173.6 19.2 %attend.5 = (bf16[1024,768]{1,0:T(8,128)(2,1)S(1)}, bf16[1024,1536]{1,0:T(8,128)(2,1)}) custom-call(s32[7]{0:T(128)S(1)} %stack.82.refs_10_.place_ref, bf16[1024,768]{1,0:T(8,128)(2,1)S(1)} %project.2.q_ref, bf16[1024,1536]{1,0:T(8,128)(2,1)} %project.3.ka_ref.va_ref.k_ref.v_ref, ...), custom_call_target="tpu_custom_call", output_to_operand_aliasing={{0}: (6, {}), {1}: (7, {})} | custom-call | flops 17179869184 | bytes 8388608 | tf_op jit(solution)/shard_map/attend/pallas_call | solution.py:684
  203.3 9.9 %stack_pieces.3.w_ref.wg_ref.wu_ref.wd_ref.refs_3_ = bf16[8,1248,768]{2,1,0:T(8,128)(2,1)} custom-call(s32[1]{0:T(128)} %bitcast.9.rep_ref, bf16[1248,768]{1,0:T(8,128)(2,1)S(1)} %pad_maximum_fusion.refs_0_, bf16[1248,768]{1,0:T(8,128)(2,1)} %collective-permute-done.15.refs_1_, bf16[1248,768]{1,0:T(8,128)(2,1)} %collective-permute-done.16.refs_2_, ...), custom_call_target="tpu_custom_call" | custom-call | bytes 30670848 | tf_op jit(solution)/shard_map/stack_pieces/pallas_call | solution.py:509
  216.2 5.5 out_norm.1
  223.3 25.8 %feed_forward.1 = (bf16[1024,3072]{1,0:T(8,128)(2,1)}, bf16[2,1024,3072]{2,1,0:T(8,128)(2,1)}, bf16[1024,768]{1,0:T(8,128)(2,1)}, f32[1024,768]{1,0:T(8,128)}) custom-call(f32[1024,768]{1,0:T(8,128)} %get-tuple-element.116.hat_ref.refs_0_, f32[2,768]{1,0:T(2,128)} %refs_2_.1, f32[2,768]{1,0:T(2,128)} %biases_ref.3, ...), custom_call_target="tpu_custom_call" | custom-call | flops 14495514624 | bytes 33030144 | tf_op jit(solution)/shard_map/feed_forward/pallas_call | solution.py:941
  252.0 6.1 norm_back.1
  260.0 5.9 away_columns.1
  274.1 21.6 %feed_back.2 = (bf16[2,384,1536]{2,1,0:T(8,128)(2,1)}, bf16[2,384,1536]{2,1,0:T(8,128)(2,1)}, f32[1024,768]{1,0:T(8,128)}) custom-call(s32[4]{0:T(128)} %copy-done.62, f32[1024,768]{1,0:T(8,128)} %get-tuple-element.120.grad_ref, bf16[1024,768]{1,0:T(8,128)(2,1)} %copy-done.5, bf16[2,1024,3072]{2,1,0:T(8,128)(2,1)} %get-tuple-element.122.factor_ref, ...), custom_call_target="tpu_custom_call" | custom-call | flops 12079595520 | bytes 18087936 | tf_op jit(solution)/shard_map/feed_back/pallas_call | solution.py:1138
  299.8 9.5 %collective-permute-done.26 = bf16[512,768]{1,0:T(8,128)(2,1)} collective-permute-done((bf16[512,768]{1,0:T(8,128)(2,1)}, bf16[512,768]{1,0:T(8,128)(2,1)}, u32[]{:S(2)}, u32[]{:S(2)}) %collective-permute-start.26) | collective-permute-done | bytes 786464 | tf_op jit(solution)/shard_map/ppermute | solution.py:404
  312.1 5.7 keep_columns.1
  319.9 26.5 %feed_back.3 = (bf16[2,384,1536]{2,1,0:T(8,128)(2,1)}, bf16[2,384,1536]{2,1,0:T(8,128)(2,1)}, f32[1024,768]{1,0:T(8,128)}, bf16[1024,768]{1,0:T(8,128)(2,1)}, bf...) custom-call(s32[4]{0:T(128)} %copy-done.62, f32[1024,768]{1,0:T(8,128)} %get-tuple-element.128.grad_ref, ...), custom_call_target="tpu_custom_call" | custom-call | flops 12079595520 | bytes 18087936 | tf_op jit(solution)/shard_map/feed_back/pallas_call | solution.py:1138
  365.3 18.5 %attend_back.5 = (f32[1024,256]{1,0:T(8,128)S(1)}, bf16[1024,256]{1,0:T(8,128)(2,1)S(1)}, bf16[1024,256]{1,0:T(8,128)(2,1)S(1)}) custom-call(s32[7]{0:T(128)S(1)} %stack.82.refs_10_.place_ref, bf16[1024,1536]{1,0:T(8,128)(2,1)} %get-tuple-element.112.qx_ref, bf16[1024,1536]{1,0:T(8,128)(2,1)} %collective-permute-done.14.kb_ref.vb_ref.k_ref.v_ref, ...), custom_call_target="tpu_custom_call" | custom-call | flops 10737418240 | bytes 10485760 | tf_op jit(solution)/shard_map/attend_back/pallas_call | solution.py:811
  385.9 21.8 %collective-permute-done.31 = bf16[2,192,1536]{2,1,0:T(8,128)(2,1)} collective-permute-done((bf16[2,192,1536]{2,1,0:T(8,128)(2,1)}, bf16[2,192,1536]{2,1,0:T(8,128)(2,1)}, u32[]{:S(2)}, u32[]{:S(2)}) %collective-permute-start.31) | collective-permute-done | bytes 1179680 | tf_op jit(solution)/shard_map/ppermute | solution.py:404
  416.8 36.4 %attend_back.6 = (f32[1024,512]{1,0:T(8,128)}, bf16[1024,512]{1,0:T(8,128)(2,1)}, bf16[1024,512]{1,0:T(8,128)(2,1)S(1)}) custom-call(s32[7]{0:T(128)S(1)} %stack.82.refs_10_.place_ref, bf16[1024,1536]{1,0:T(8,128)(2,1)} %get-tuple-element.112.qx_ref, bf16[1024,1536]{1,0:T(8,128)(2,1)} %collective-permute-done.14.kb_ref.vb_ref.k_ref.v_ref, ...), custom_call_target="tpu_custom_call" | custom-call | flops 21474836480 | bytes 20971520 | tf_op jit(solution)/shard_map/attend_back/pallas_call | solution.py:811
  462.4 15.8 %attend_back.7.right_ref.refs_2_ = bf16[3,1024,256]{2,1,0:T(8,128)(2,1)S(1)} custom-call(s32[7]{0:T(128)S(1)} %stack.82.refs_10_.place_ref, bf16[1024,1536]{1,0:T(8,128)(2,1)} %get-tuple-element.112.qx_ref, bf16[1024,1536]{1,0:T(8,128)(2,1)} %project.3.ka_ref.va_ref.k_ref.v_ref, bf16[1024,1536]{1,0:T(8,128)(2,1)} %project.3.ka_ref.va_ref.k_ref.v_ref, ...), custom_call_target="tpu_custom_call" | custom-call | flops 10737418240 | bytes 10485760 | tf_op jit(solution)/shard_map/attend_back/pallas_call | solution.py:811
  480.9 17.0 %attend_back.8.right_ref.refs_0_ = bf16[3,1024,256]{2,1,0:T(8,128)(2,1)S(1)} custom-call(s32[7]{0:T(128)S(1)} %stack.82.refs_10_.place_ref, bf16[1024,1536]{1,0:T(8,128)(2,1)} %get-tuple-element.112.qx_ref, bf16[1024,1536]{1,0:T(8,128)(2,1)} %project.3.ka_ref.va_ref.k_ref.v_ref, bf16[1024,1536]{1,0:T(8,128)(2,1)} %project.3.ka_ref.va_ref.k_ref.v_ref, ...), custom_call_target="tpu_custom_call" | custom-call | flops 10737418240 | bytes 10485760 | tf_op jit(solution)/shard_map/attend_back/pallas_call | solution.py:811
  525.4 15.7 %attend_back.9.right_ref.refs_1_ = bf16[3,1024,256]{2,1,0:T(8,128)(2,1)S(1)} custom-call(s32[7]{0:T(128)S(1)} %stack.82.refs_10_.place_ref, bf16[1024,1536]{1,0:T(8,128)(2,1)} %get-tuple-element.112.qx_ref, bf16[1024,1536]{1,0:T(8,128)(2,1)} %project.3.ka_ref.va_ref.k_ref.v_ref, bf16[1024,1536]{1,0:T(8,128)(2,1)} %project.3.ka_ref.va_ref.k_ref.v_ref, ...), custom_call_target="tpu_custom_call" | custom-call | flops 10737418240 | bytes 10485760 | tf_op jit(solution)/shard_map/attend_back/pallas_call | solution.py:811
  544.0 7.8 %merge_main.1 = (f32[192,6144]{1,0:T(8,128)}, f32[192,768]{1,0:T(8,128)S(1)}, f32[8,512]{1,0:T(8,128)S(1)}) custom-call(s32[1]{0:T(128)} %bitcast.49.owner_ref, bf16[2,192,1536]{2,1,0:T(8,128)(2,1)S(1)} %copy-done.19, bf16[2,192,1536]{2,1,0:T(8,128)(2,1)S(1)} %copy-done.41, bf16[192,3840]{1,0:T(8,128)(2,1)} %add_convert_fusion.ss_ref.os_ref, ...), custom_call_target="tpu_custom_call" | custom-call | flops 61931520 | bytes 14450688 | tf_op jit(solution)/shard_map/merge_main/pallas_call | solution.py:1370
  565.2 5.5 pull.3
  584.0 7.2 %input_rows.1 = bf16[1024,768]{1,0:T(8,128)(2,1)S(1)} custom-call(bf16[3,1024,256]{2,1,0:T(8,128)(2,1)S(1)} %copy-done.4, bf16[3,1024,256]{2,1,0:T(8,128)(2,1)S(1)} %attend_back.9.right_ref.refs_1_, bf16[3,1024,256]{2,1,0:T(8,128)(2,1)} %copy-done.1, bf16[3,768,768]{2,1,0:T(8,128)(2,1)} %bitcast.124, bf16[3,768,768]{2,1,0:T(8,128)(2,1)} %bitcast.125, ...), custom_call_target="tpu_custom_call" | custom-call | flops 3623878656 | bytes 11010048 | tf_op jit(solution)/shard_map/input_rows/pallas_call | solution.py:1300
  593.5 5.1 collective-permute-start.45
  612.9 13.2 %collective-permute-done.45 = bf16[512,768]{1,0:T(8,128)(2,1)S(1)} collective-permute-done((bf16[512,768]{1,0:T(8,128)(2,1)S(1)}, bf16[512,768]{1,0:T(8,128)(2,1)S(1)}, u32[]{:S(2)}, u32[]{:S(2)}) %collective-permute-start.45) | collective-permute-done | bytes 786464 | tf_op jit(solution)/shard_map/ppermute | solution.py:404
  626.1 10.3 %collective-permute-done.46 = bf16[512,768]{1,0:T(8,128)(2,1)S(1)} collective-permute-done((bf16[512,768]{1,0:T(8,128)(2,1)S(1)}, bf16[512,768]{1,0:T(8,128)(2,1)S(1)}, u32[]{:S(2)}, u32[]{:S(2)}) %collective-permute-start.46) | collective-permute-done | bytes 786464 | tf_op jit(solution)/shard_map/ppermute | solution.py:404
  643.8 7.9 %new_errors.3 = (f32[1,192,6144]{2,1,0:T(8,128)}, f32[1,192,768]{2,1,0:T(8,128)}, f32[1,768,768]{2,1,0:T(8,128)}) custom-call(f32[8,1280]{1,0:T(8,128)S(1)} %get-tuple-element.179.basis_ref, f32[8,7680]{1,0:T(8,128)S(1)} %add_multiply_fusion.refs_0_.refs_1_.refs_2_, f32[8,7680]{1,0:T(8,128)S(1)} %add_multiply_fusion.refs_0_.refs_1_.refs_2_, ...), custom_call_target="tpu_custom_call" | custom-call | flops 92012544 | bytes 15335424 | tf_op jit(solution)/shard_map/new_errors/pallas_call | solution.py:1576
  (441 shorter events, 229.7 us)
Async XLA Ops:
  7.2 89.6 %all-gather.3.cloned.1.call-start = ((), (), s32[]{:S(2)}) async-start(), calls=%async_computation | async-start | bytes 2396160 | tf_op jit(solution)/shard_map/all_gather | solution.py:1676
  14.7 38.9 %collective-permute-start = (s32[2]{0:T(128)S(1)}, s32[2]{0:T(128)S(1)}, u32[]{:S(2)}, u32[]{:S(2)}) collective-permute-start(s32[2]{0:T(128)S(1)} %copy-done.101), channel_id=1, source_target_pairs={{0,4},{1,5},{2,6},{3,7},{4,0},{5,1},{6,2},{7,3},{8,12},{9,13},{10,... | collective-permute-start | bytes 32 | tf_op jit(solution)/shard_map/ppermute | solution.py:404
  15.7 65.9 %collective-permute-start.1 = (bf16[512,768]{1,0:T(8,128)(2,1)S(1)}, bf16[512,768]{1,0:T(8,128)(2,1)}, u32[]{:S(2)}, u32[]{:S(2)}) collective-permute-start(bf16[512,768]{1,0:T(8,128)(2,1)S(1)} %get-tuple-element.204), channel_id=1, source_target_pairs={{2,4},{3,5},{4,2},{5,3},{10,12},{11,13},{12,10},{13,11},{18,20},{1... | collective-permute-start | bytes 2359304 | tf_op jit(solution)/shard_map/ppermute | solution.py:404
  30.3 61.0 %collective-permute-start.2 = (bf16[512,768]{1,0:T(8,128)(2,1)}, bf16[512,768]{1,0:T(8,128)(2,1)}, u32[]{:S(2)}, u32[]{:S(2)}) collective-permute-start(bf16[512,768]{1,0:T(8,128)(2,1)} %get-tuple-element.205), channel_id=1, source_target_pairs={{0,1},{1,0},{2,5},{3,4},{4,3},{5,2},{6,7},{7,6},{8,9},{9,8},{10,13... | collective-permute-start | bytes 2359304 | tf_op jit(solution)/shard_map/ppermute | solution.py:404
  55.0 38.7 %collective-permute-start.10 = (bf16[288,768]{1,0:T(8,128)(2,1)S(1)}, bf16[288,768]{1,0:T(8,128)(2,1)S(1)}, u32[]{:S(2)}, u32[]{:S(2)}) collective-permute-start(bf16[288,768]{1,0:T(8,128)(2,1)S(1)} %pad_maximum_fusion.11.refs_0_), channel_id=1, source_target_pairs={{0,4},{1,5},{2,6},{3,7},{4,0},{5,1},{6,2},{7,3},{8,12},{9,13},{10,... | collective-permute-start | bytes 1327112 | tf_op jit(solution)/shard_map/ppermute | solution.py:404
  55.0 39.4 %collective-permute-start.11 = (bf16[288,768]{1,0:T(8,128)(2,1)}, bf16[288,768]{1,0:T(8,128)(2,1)S(1)}, u32[]{:S(2)}, u32[]{:S(2)}) collective-permute-start(bf16[288,768]{1,0:T(8,128)(2,1)} %collective-permute-done.6.refs_1_), channel_id=1, source_target_pairs={{0,4},{1,5},{2,6},{3,7},{4,0},{5,1},{6,2},{7,3},{8,12},{9,13},{10,... | collective-permute-start | bytes 1327112 | tf_op jit(solution)/shard_map/ppermute | solution.py:404
  57.7 37.6 %collective-permute-start.12 = (bf16[288,768]{1,0:T(8,128)(2,1)S(1)}, bf16[288,768]{1,0:T(8,128)(2,1)S(1)}, u32[]{:S(2)}, u32[]{:S(2)}) collective-permute-start(bf16[288,768]{1,0:T(8,128)(2,1)S(1)} %collective-permute-done.7.refs_2_), channel_id=1, source_target_pairs={{0,4},{1,5},{2,6},{3,7},{4,0},{5,1},{6,2},{7,3},{8,12},{9,13},{10,... | collective-permute-start | bytes 1327112 | tf_op jit(solution)/shard_map/ppermute | solution.py:404
  122.8 45.5 %collective-permute-start.15 = (bf16[1248,768]{1,0:T(8,128)(2,1)S(1)}, bf16[1248,768]{1,0:T(8,128)(2,1)}, u32[]{:S(2)}, u32[]{:S(2)}) collective-permute-start(bf16[1248,768]{1,0:T(8,128)(2,1)S(1)} %pad_maximum_fusion.refs_0_), channel_id=1, source_target_pairs={{0,8},{1,9},{2,10},{3,11},{4,12},{5,13},{6,14},{7,15},{8,0},{9,1},... | collective-permute-start | bytes 5750792 | tf_op jit(solution)/shard_map/ppermute | solution.py:404
  124.4 44.0 %collective-permute-start.16 = (bf16[1248,768]{1,0:T(8,128)(2,1)S(1)}, bf16[1248,768]{1,0:T(8,128)(2,1)}, u32[]{:S(2)}, u32[]{:S(2)}) collective-permute-start(bf16[1248,768]{1,0:T(8,128)(2,1)S(1)} %pad_maximum_fusion.refs_0_), channel_id=1, source_target_pairs={{0,16},{1,17},{2,18},{3,19},{4,20},{5,21},{6,22},{7,23},{8,24},{9,... | collective-permute-start | bytes 5750792 | tf_op jit(solution)/shard_map/ppermute | solution.py:404
  169.7 27.1 %collective-permute-start.20 = (bf16[1248,768]{1,0:T(8,128)(2,1)}, bf16[1248,768]{1,0:T(8,128)(2,1)}, u32[]{:S(2)}, u32[]{:S(2)}) collective-permute-start(bf16[1248,768]{1,0:T(8,128)(2,1)} %collective-permute-done.15.refs_1_), channel_id=1, source_target_pairs={{0,4},{1,5},{2,6},{3,7},{4,0},{5,1},{6,2},{7,3},{8,12},{9,13},{10,... | collective-permute-start | bytes 5750792 | tf_op jit(solution)/shard_map/ppermute | solution.py:404
  171.0 25.8 %collective-permute-start.21 = (bf16[1248,768]{1,0:T(8,128)(2,1)}, bf16[1248,768]{1,0:T(8,128)(2,1)}, u32[]{:S(2)}, u32[]{:S(2)}) collective-permute-start(bf16[1248,768]{1,0:T(8,128)(2,1)} %collective-permute-done.16.refs_2_), channel_id=1, source_target_pairs={{0,4},{1,5},{2,6},{3,7},{4,0},{5,1},{6,2},{7,3},{8,12},{9,13},{10,... | collective-permute-start | bytes 5750792 | tf_op jit(solution)/shard_map/ppermute | solution.py:404
  171.6 23.2 %collective-permute-start.17 = (bf16[624,768]{1,0:T(8,128)(2,1)S(1)}, bf16[624,768]{1,0:T(8,128)(2,1)S(1)}, u32[]{:S(2)}, u32[]{:S(2)}) collective-permute-start(bf16[624,768]{1,0:T(8,128)(2,1)S(1)} %slice.95), channel_id=1, source_target_pairs={{0,8},{1,9},{2,10},{3,11},{4,12},{5,13},{6,14},{7,15},{8,0},{9,1},... | collective-permute-start | bytes 2875400 | tf_op jit(solution)/shard_map/ppermute | solution.py:404
  214.3 34.8 %collective-permute-start.23 = (bf16[512,768]{1,0:T(8,128)(2,1)S(1)}, bf16[512,768]{1,0:T(8,128)(2,1)S(1)}, u32[]{:S(2)}, u32[]{:S(2)}) collective-permute-start(bf16[512,768]{1,0:T(8,128)(2,1)S(1)} %get-tuple-element.203), channel_id=1, source_target_pairs={{2,4},{3,5},{4,2},{5,3},{10,12},{11,13},{12,10},{13,11},{18,20},{1... | collective-permute-start | bytes 2359304 | tf_op jit(solution)/shard_map/ppermute | solution.py:404
  222.5 29.5 %collective-permute-start.24 = (bf16[512,768]{1,0:T(8,128)(2,1)}, bf16[512,768]{1,0:T(8,128)(2,1)S(1)}, u32[]{:S(2)}, u32[]{:S(2)}) collective-permute-start(bf16[512,768]{1,0:T(8,128)(2,1)} %get-tuple-element.202), channel_id=1, source_target_pairs={{0,1},{1,0},{2,5},{3,4},{4,3},{5,2},{6,7},{7,6},{8,9},{9,8},{10,13... | collective-permute-start | bytes 2359304 | tf_op jit(solution)/shard_map/ppermute | solution.py:404
  265.9 46.3 %collective-permute-start.27 = (bf16[768,1536]{1,0:T(8,128)(2,1)}, bf16[768,1536]{1,0:T(8,128)(2,1)}, u32[]{:S(2)}, u32[]{:S(2)}) collective-permute-start(bf16[768,1536]{1,0:T(8,128)(2,1)} %away_columns.1), channel_id=1, source_target_pairs={{0,4},{1,5},{2,6},{3,7},{4,0},{5,1},{6,2},{7,3},{8,12},{9,13},{10,... | collective-permute-start | bytes 7077896 | tf_op jit(solution)/shard_map/ppermute | solution.py:404
  269.9 29.9 %collective-permute-start.25 = (bf16[512,768]{1,0:T(8,128)(2,1)}, bf16[512,768]{1,0:T(8,128)(2,1)}, u32[]{:S(2)}, u32[]{:S(2)}) collective-permute-start(bf16[512,768]{1,0:T(8,128)(2,1)} %get-tuple-element.200), channel_id=1, source_target_pairs={{2,4},{3,5},{4,2},{5,3},{10,12},{11,13},{12,10},{13,11},{18,20},{1... | collective-permute-start | bytes 2359304 | tf_op jit(solution)/shard_map/ppermute | solution.py:404
  273.1 36.2 %collective-permute-start.26 = (bf16[512,768]{1,0:T(8,128)(2,1)}, bf16[512,768]{1,0:T(8,128)(2,1)}, u32[]{:S(2)}, u32[]{:S(2)}) collective-permute-start(bf16[512,768]{1,0:T(8,128)(2,1)} %get-tuple-element.201), channel_id=1, source_target_pairs={{0,1},{1,0},{2,5},{3,4},{4,3},{5,2},{6,7},{7,6},{8,9},{9,8},{10,13... | collective-permute-start | bytes 2359304 | tf_op jit(solution)/shard_map/ppermute | solution.py:404
  295.7 57.6 %collective-permute-start.30 = (bf16[2,384,1536]{2,1,0:T(8,128)(2,1)}, bf16[2,384,1536]{2,1,0:T(8,128)(2,1)}, u32[]{:S(2)}, u32[]{:S(2)}) collective-permute-start(bf16[2,384,1536]{2,1,0:T(8,128)(2,1)} %get-tuple-element.138), channel_id=1, source_target_pairs={{0,4},{1,5},{2,6},{3,7},{4,0},{5,1},{6,2},{7,3},{8,12},{9,13},{10,... | collective-permute-start | bytes 7077896 | tf_op jit(solution)/shard_map/ppermute | solution.py:404
  353.2 30.7 %collective-permute-start.32 = (bf16[768,768]{1,0:T(8,128)(2,1)}, bf16[768,768]{1,0:T(8,128)(2,1)}, u32[]{:S(2)}, u32[]{:S(2)}) collective-permute-start(bf16[768,768]{1,0:T(8,128)(2,1)} %copy-done.72), channel_id=1, source_target_pairs={{0,1},{1,0},{2,3},{3,2},{4,5},{5,4},{6,7},{7,6},{8,9},{9,8},{10,11... | collective-permute-start | bytes 3538952 | tf_op jit(solution)/shard_map/ppermute | solution.py:404
  356.3 51.4 %collective-permute-start.31 = (bf16[2,192,1536]{2,1,0:T(8,128)(2,1)}, bf16[2,192,1536]{2,1,0:T(8,128)(2,1)}, u32[]{:S(2)}, u32[]{:S(2)}) collective-permute-start(bf16[2,192,1536]{2,1,0:T(8,128)(2,1)} %fusion.2), channel_id=1, source_target_pairs={{0,1},{1,0},{2,3},{3,2},{4,5},{5,4},{6,7},{7,6},{8,9},{9,8},{10,11... | collective-permute-start | bytes 3538952 | tf_op jit(solution)/shard_map/ppermute | solution.py:404
  364.2 89.0 %collective-permute-start.33 = (bf16[192,3840]{1,0:T(8,128)(2,1)}, bf16[192,3840]{1,0:T(8,128)(2,1)}, u32[]{:S(2)}, u32[]{:S(2)}) collective-permute-start(bf16[192,3840]{1,0:T(8,128)(2,1)} %pad_maximum_fusion.6), channel_id=1, source_target_pairs={{0,1},{1,0},{2,3},{3,2},{4,5},{5,4},{6,7},{7,6},{8,9},{9,8},{10,11... | collective-permute-start | bytes 4423688 | tf_op jit(solution)/shard_map/ppermute | solution.py:404
  409.8 71.0 %collective-permute-start.37 = (bf16[768,768]{1,0:T(8,128)(2,1)S(1)}, bf16[768,768]{1,0:T(8,128)(2,1)S(1)}, u32[]{:S(2)}, u32[]{:S(2)}) collective-permute-start(bf16[768,768]{1,0:T(8,128)(2,1)S(1)} %add_convert_fusion.1.s_ref), channel_id=1, source_target_pairs={{2,5},{3,4},{4,3},{5,2},{10,13},{11,12},{12,11},{13,10},{18,21},{1... | collective-permute-start | bytes 3538952 | tf_op jit(solution)/shard_map/ppermute | solution.py:404
  411.7 69.1 %collective-permute-start.36 = (bf16[2,192,1536]{2,1,0:T(8,128)(2,1)S(1)}, bf16[2,192,1536]{2,1,0:T(8,128)(2,1)S(1)}, u32[]{:S(2)}, u32[]{:S(2)}) collective-permute-start(bf16[2,192,1536]{2,1,0:T(8,128)(2,1)S(1)} %fusion.fs_ref), channel_id=1, source_target_pairs={{2,5},{3,4},{4,3},{5,2},{10,13},{11,12},{12,11},{13,10},{18,21},{1... | collective-permute-start | bytes 3538952 | tf_op jit(solution)/shard_map/ppermute | solution.py:404
  416.3 40.1 %collective-permute-start.34 = (bf16[1024,256]{1,0:T(8,128)(2,1)S(1)}, bf16[1024,256]{1,0:T(8,128)(2,1)S(1)}, u32[]{:S(2)}, u32[]{:S(2)}) collective-permute-start(bf16[1024,256]{1,0:T(8,128)(2,1)S(1)} %get-tuple-element.146), channel_id=1, source_target_pairs={{0,4},{1,5},{2,6},{3,7},{4,0},{5,1},{6,2},{7,3},{8,12},{9,13},{10,... | collective-permute-start | bytes 1572872 | tf_op jit(solution)/shard_map/ppermute | solution.py:404
  416.3 41.3 %collective-permute-start.35 = (bf16[1024,256]{1,0:T(8,128)(2,1)S(1)}, bf16[1024,256]{1,0:T(8,128)(2,1)S(1)}, u32[]{:S(2)}, u32[]{:S(2)}) collective-permute-start(bf16[1024,256]{1,0:T(8,128)(2,1)S(1)} %get-tuple-element.147), channel_id=1, source_target_pairs={{0,4},{1,5},{2,6},{3,7},{4,0},{5,1},{6,2},{7,3},{8,12},{9,13},{10,... | collective-permute-start | bytes 1572872 | tf_op jit(solution)/shard_map/ppermute | solution.py:404
  453.2 27.7 %collective-permute-start.38 = (bf16[1024,512]{1,0:T(8,128)(2,1)}, bf16[1024,512]{1,0:T(8,128)(2,1)S(1)}, u32[]{:S(2)}, u32[]{:S(2)}) collective-permute-start(bf16[1024,512]{1,0:T(8,128)(2,1)} %get-tuple-element.149), channel_id=1, source_target_pairs={{0,4},{1,5},{2,6},{3,7},{4,0},{5,1},{6,2},{7,3},{8,12},{9,13},{10,... | collective-permute-start | bytes 3145736 | tf_op jit(solution)/shard_map/ppermute | solution.py:404
  457.1 23.8 %collective-permute-start.39 = (bf16[1024,512]{1,0:T(8,128)(2,1)S(1)}, bf16[1024,512]{1,0:T(8,128)(2,1)S(1)}, u32[]{:S(2)}, u32[]{:S(2)}) collective-permute-start(bf16[1024,512]{1,0:T(8,128)(2,1)S(1)} %get-tuple-element.150), channel_id=1, source_target_pairs={{0,4},{1,5},{2,6},{3,7},{4,0},{5,1},{6,2},{7,3},{8,12},{9,13},{10,... | collective-permute-start | bytes 3145736 | tf_op jit(solution)/shard_map/ppermute | solution.py:404
  458.4 67.0 %collective-permute-start.42 = (bf16[192,3840]{1,0:T(8,128)(2,1)}, bf16[192,3840]{1,0:T(8,128)(2,1)}, u32[]{:S(2)}, u32[]{:S(2)}) collective-permute-start(bf16[192,3840]{1,0:T(8,128)(2,1)} %add_convert_fusion.ss_ref.os_ref), channel_id=1, source_target_pairs={{2,5},{3,4},{4,3},{5,2},{10,13},{11,12},{12,11},{13,10},{18,21},{1... | collective-permute-start | bytes 4423688 | tf_op jit(solution)/shard_map/ppermute | solution.py:404
  480.9 34.7 %collective-permute-start.41 = (bf16[384,768]{1,0:T(8,128)(2,1)}, bf16[384,768]{1,0:T(8,128)(2,1)}, u32[]{:S(2)}, u32[]{:S(2)}) collective-permute-start(bf16[384,768]{1,0:T(8,128)(2,1)} %away_rows.5), channel_id=1, source_target_pairs={{0,4},{1,5},{2,6},{3,7},{4,0},{5,1},{6,2},{7,3},{8,12},{9,13},{10,... | collective-permute-start | bytes 1769480 | tf_op jit(solution)/shard_map/ppermute | solution.py:404
  559.6 39.0 %collective-permute-start.48 = (bf16[192,1536]{1,0:T(8,128)(2,1)}, bf16[192,1536]{1,0:T(8,128)(2,1)}, u32[]{:S(2)}, u32[]{:S(2)}) collective-permute-start(bf16[192,1536]{1,0:T(8,128)(2,1)} %add_convert_fusion.6.refs_0_.refs_2_), channel_id=1, source_target_pairs={{2,5},{3,4},{4,3},{5,2},{10,13},{11,12},{12,11},{13,10},{18,21},{1... | collective-permute-start | bytes 1769480 | tf_op jit(solution)/shard_map/ppermute | solution.py:404
  593.5 32.5 %collective-permute-start.45 = (bf16[512,768]{1,0:T(8,128)(2,1)S(1)}, bf16[512,768]{1,0:T(8,128)(2,1)S(1)}, u32[]{:S(2)}, u32[]{:S(2)}) collective-permute-start(bf16[512,768]{1,0:T(8,128)(2,1)S(1)} %get-tuple-element.196), channel_id=1, source_target_pairs={{2,4},{3,5},{4,2},{5,3},{10,12},{11,13},{12,10},{13,11},{18,20},{1... | collective-permute-start | bytes 2359304 | tf_op jit(solution)/shard_map/ppermute | solution.py:404
  598.6 37.7 %collective-permute-start.46 = (bf16[512,768]{1,0:T(8,128)(2,1)S(1)}, bf16[512,768]{1,0:T(8,128)(2,1)S(1)}, u32[]{:S(2)}, u32[]{:S(2)}) collective-permute-start(bf16[512,768]{1,0:T(8,128)(2,1)S(1)} %get-tuple-element.197), channel_id=1, source_target_pairs={{0,1},{1,0},{2,5},{3,4},{4,3},{5,2},{6,7},{7,6},{8,9},{9,8},{10,13... | collective-permute-start | bytes 2359304 | tf_op jit(solution)/shard_map/ppermute | solution.py:404
  (135 other events, 1194.8 us)
Sparse Core Ops, SparseCore 0:
  11.6 67.2 all-gather.2

commit v4 on v3

--- a/solution.py
+++ b/solution.py
@@ -467,17 +467,25 @@
 
 
 def exchange(piece, near, far):
-    return [sibling(part) for part in (piece, *near, jnp.concatenate(far, axis=0))]
+    near = jnp.concatenate(near, axis=0)
+    return [sibling(part) for part in (piece, near, jnp.concatenate(far, axis=0))]
 
 
 def plane_all(piece, near, far, others, rep, ahead=()):
-    return stack_pieces((piece, *near, *far, *others), rep, *piece.shape, ahead)
+    offsets = [0] * len(PIECE_STEPS)
+    if len(others) == 3:
+        own, both, opposite = others
+        others = own, both, both, opposite
+        offsets[7] = piece.shape[0]
+    return stack_pieces(
+        (piece, *near, *far, *others), rep, *piece.shape, ahead, tuple(offsets)
+    )
 
 
 PIECE_STEPS = ((0, None), (2, None), (4, None), (6, 0), (6, 1), (1, None), (3, None), (5, None), (7, None))
 
 
-def stack_kernel(rep_ref, *refs):
+def stack_kernel(rep_ref, *refs, offsets):
     count = len(PIECE_STEPS)
     pieces = refs[:count]
     whole, staged, sems_in, sems_out = refs[-4:]
@@ -492,7 +500,8 @@
             part = pl.ds(side * half, half)
             stage = stage.at[part]
             place = place.at[part]
-        fetches.append(pltpu.make_async_copy(pieces[slot], stage, sems_in.at[slot]))
+        source = pieces[slot].at[pl.ds(offsets[slot], stage.shape[0])]
+        fetches.append(pltpu.make_async_copy(source, stage, sems_in.at[slot]))
         stores.append(pltpu.make_async_copy(stage, place, sems_out.at[slot]))
     for fetch in fetches:
         fetch.start()
@@ -503,11 +512,11 @@
         store.wait()
 
 
-def stack_pieces(pieces, rep, rows, cols, ahead):
+def stack_pieces(pieces, rep, rows, cols, ahead, offsets):
     anywhere = pl.BlockSpec(memory_space=pl.ANY)
     count = len(pieces)
     return pl.pallas_call(
-        stack_kernel,
+        functools.partial(stack_kernel, offsets=offsets),
         in_specs=[pl.BlockSpec(memory_space=pltpu.SMEM)] + [anywhere] * (count + len(ahead)),
         out_specs=anywhere,
         out_shape=jax.ShapeDtypeStruct((REPS, rows, cols), pieces[0].dtype),
@@ -1794,12 +1803,12 @@
     other_2 = sibling(dk_2), sibling(dv_2)
     down_sum = add(down_mine, after(down_pair, dq_2))
     down_far = to_owner(down_sum)
-    first_sum = add(first_mine, after(first_pair, dq_2))
-    first_far = to_owner(first_sum)
     vectors = vectors + pair_z(after(vectors, dq_2))
-    grads = after(grads, first_sum, down_sum)
+    grads = after(grads, down_sum)
     dq_1, dk_1, dv_1 = back(grads, kv_other, 2, 0, 4)
     other_1 = sibling(dk_1), sibling(dv_1)
+    first_sum = add(first_mine, after(first_pair, dq_1))
+    first_far = to_owner(first_sum)
     second_sum = add(second_mine, after(second_pair, dq_1))
     second_far = to_owner(second_sum)
     flag = owner.astype(jnp.int32).reshape(1)
@@ -1814,12 +1823,12 @@
     def keep_part(right, got):
         return keep_rows(index, tokens_t, right, got, 256)
 
-    grads = after(grads, second_sum)
+    grads = after(grads, first_sum, second_sum)
     grads_2 = back(grads, kv, 0, 4, 2, (dq_2, *other_2, cos, sin))
     away_2 = away_part(grads_2)
     got_2 = sibling(away_2)
     vectors = vectors + mirror_z(after(vectors, grads_2))
-    grads = after(grads, away_2, first_far, down_far)
+    grads = after(grads, away_2, down_far)
     grads_0 = back(grads, kv, 0, 0, 2, (dq_1, *other_1, cos, sin))
     away_0 = away_part(grads_0)
     got_0 = sibling(away_0)
@@ -1828,25 +1837,23 @@
     qkv_mine = jnp.concatenate([mine_0, mine_2], axis=1)
     qkv_theirs = jnp.concatenate([theirs_0, theirs_2], axis=1)
     qkv_pair = pair_z(qkv_theirs)
-    grads = after(grads, qkv_mine, qkv_theirs, second_far)
+    grads = after(grads, qkv_mine, qkv_theirs, first_far, second_far)
     grads_1 = back(grads, kv, 0, 2, 2, (dq_1, *other_1, cos, sin), 2)
     away_1 = away_part(grads_1)
     got_1 = sibling(away_1)
     qkv_sum = add(qkv_mine, after(qkv_pair, away_1))
     qkv_far = to_owner(qkv_sum)
+    input_rows = input_rows_of((grads_0, grads_1, grads_2), qkv_t, after(grad_attn, away_1))
+    input_grad = bring_back(input_rows)
     merged_gate_up, merged_out, left_main = merge_main(
-        flag, (first_sum, first_far), (second_sum, after(second_far, qkv_sum)),
+        flag, (first_sum, first_far), (second_sum, after(second_far, qkv_sum, input_rows)),
         err_gate_up, err_out, start_gate_up[0].T, start_out[0].T,
     )
     packed = jnp.concatenate([left_main, left_down, vectors.reshape(RANK, width // 2)], axis=1)
     packed = plane_sum(packed)
     mine_1, theirs_1 = keep_part(grads_1, after(got_1, left_main))
     pair_1 = pair_z(theirs_1)
-    input_rows = input_rows_of(
-        (grads_0, grads_1, grads_2), qkv_t, after(grad_attn, mine_1, theirs_1)
-    )
-    input_grad = bring_back(input_rows)
-    sum_1 = add(mine_1, after(pair_1, input_rows))
+    sum_1 = add(mine_1, pair_1)
     far_1 = to_owner(sum_1)
 
     norm_grad = packed[:, 1280:].reshape(4, width) / REPS

time: 679 us -> 688 us (1.013)
  local copies, waits for them, and re-layouts: 57 us -> 80.6 us
  waiting for transfers between devices: 141 us -> 120 us
  other arithmetic: 36.4 us -> 46.1 us
    ppermute x64 -> x63, waiting for transfers between devices: 141 us -> 120 us  [send(): return lax.ppermute(values, AXES, pairs)]
    unnamed x210 -> x180, local copies, waits for them, and re-layouts: 33.8 us -> 42.1 us
    ppermute x64 -> x63, starting transfers between devices: 67 us -> 64.3 us  [send(): return lax.ppermute(values, AXES, pairs)]
  transfers between devices with their start and end apart: 65 -> 64, of which waited for: 28 -> 25; matrix products, arithmetic and copies ran while one was open for 8% -> 13% of each run, Pallas kernels for 45% -> 43%
where the time goes in v4:
time: 688 us; the launch traced here: 676 us
  Pallas kernels  344 us (50%)
  waiting for transfers between devices  120 us (17%)
  local copies, waits for them, and re-layouts  80.6 us (12%)
  starting transfers between devices  64.4 us (9%)
  other arithmetic  46.1 us (7%)
  between operations  15.7 us (2%)
    ppermute x63, waiting for transfers between devices, send(): return lax.ppermute(values, AXES, pairs)  120 us
    pallas_call x5, Pallas kernels, attend_back(): pl.pallas_call(functools.partial(attend_back_kernel, at=at, scale=scale),...  103 us
    ppermute x63, starting transfers between devices, send(): return lax.ppermute(values, AXES, pairs)  64.3 us
    pallas_call x3, Pallas kernels, attend(): pl.pallas_call(attend_kernel, grid=(count, rows // block), in_specs=[pl.B...  57.8 us
    pallas_call x2, Pallas kernels, feed_back(): pl.pallas_call(feed_back_kernel, grid_spec=pltpu.PrefetchScalarGridSpec(n...  48 us
    unnamed x180, local copies, waits for them, and re-layouts  42.1 us
    pallas_call x1, Pallas kernels, feed_forward(): pl.pallas_call(feed_forward_kernel, grid=(tiles + 1,), in_specs=[whole, s...  25.8 us
    pallas_call x2, Pallas kernels, stack_pieces(): pl.pallas_call(functools.partial(stack_kernel, offsets=offsets), in_specs...  14.2 us
  transfers between devices with their start and end apart: 64, of which 25 were waited for; matrix products, arithmetic and copies ran while one was open for 13% of the time, Pallas kernels for 43%

profile of v4, /device:TPU:16, one launch (start us, length us, event | category | flops | bytes accessed | tf_op | source)
XLA Modules:
  0.0 676.4 jit_solution(10567630338545796106)
XLA Ops:
  21.7 9.0 %collective-permute-done.3 = bf16[288,192]{0,1:T(8,128)(2,1)S(1)} collective-permute-done((bf16[288,192]{0,1:T(8,128)(2,1)}, bf16[288,192]{0,1:T(8,128)(2,1)S(1)}, u32[]{:S(2)}, u32[]{:S(2)}) %collective-permute-start.3) | collective-permute-done | bytes 110624 | tf_op jit(solution)/shard_map/ppermute | solution.py:404
  30.7 7.0 %collective-permute-done.5 = bf16[288,192]{0,1:T(8,128)(2,1)} collective-permute-done((bf16[288,192]{0,1:T(8,128)(2,1)}, bf16[288,192]{0,1:T(8,128)(2,1)}, u32[]{:S(2)}, u32[]{:S(2)}) %collective-permute-start.5) | collective-permute-done | bytes 110624 | tf_op jit(solution)/shard_map/ppermute | solution.py:404
  45.3 6.8 %collective-permute-done.7.refs_2_ = bf16[288,768]{1,0:T(8,128)(2,1)S(1)} collective-permute-done((bf16[288,768]{1,0:T(8,128)(2,1)}, bf16[288,768]{1,0:T(8,128)(2,1)S(1)}, u32[]{:S(2)}, u32[]{:S(2)}) %collective-permute-start.7) | collective-permute-done | bytes 442400 | tf_op jit(solution)/shard_map/ppermute | solution.py:404
  67.1 15.3 %collective-permute-done.1 = bf16[512,768]{0,1:T(8,128)(2,1)} collective-permute-done((bf16[512,768]{0,1:T(8,128)(2,1)S(1)}, bf16[512,768]{0,1:T(8,128)(2,1)}, u32[]{:S(2)}, u32[]{:S(2)}) %collective-permute-start.1) | collective-permute-done | bytes 786464 | tf_op jit(solution)/shard_map/ppermute | solution.py:404
  83.6 8.4 %collective-permute-done.2 = bf16[512,768]{0,1:T(8,128)(2,1)} collective-permute-done((bf16[512,768]{0,1:T(8,128)(2,1)}, bf16[512,768]{0,1:T(8,128)(2,1)}, u32[]{:S(2)}, u32[]{:S(2)}) %collective-permute-start.2) | collective-permute-done | bytes 786464 | tf_op jit(solution)/shard_map/ppermute | solution.py:404
  106.6 7.3 %project.3.ka_ref.va_ref.k_ref.v_ref = bf16[1024,1536]{1,0:T(8,128)(2,1)} custom-call(bf16[1024,768]{1,0:T(8,128)(2,1)S(1)} %copy.108.x_ref, bf16[2304,768]{1,0:T(8,128)(2,1)} %bitcast.121, f32[1024,128]{1,0:T(8,128)S(1)} %copy-done.24, f32[1024,128]{1,0:T(8,128)S(1)} %copy-done.20), custom_call_target="tpu_custom_call" | custom-call | flops 2415919104 | bytes 9437184 | tf_op jit(solution)/shard_map/project/pallas_call | solution.py:606
  127.5 19.2 %attend.3 = (bf16[1024,768]{1,0:T(8,128)(2,1)S(1)}, bf16[1024,1536]{1,0:T(8,128)(2,1)}) custom-call(s32[7]{0:T(128)S(1)} %stack.82.refs_10_.place_ref, bf16[1024,768]{1,0:T(8,128)(2,1)S(1)} %project.2.q_ref, bf16[1024,1536]{1,0:T(8,128)(2,1)} %project.3.ka_ref.va_ref.k_ref.v_ref, bf16[1024,1536]{1,0:T(8,128)(2,1)} %project.3.ka_ref.va_ref.k_ref.v_ref, ...), custom_call_target="tpu_custom_call" | custom-call | flops 17179869184 | bytes 8388608 | tf_op jit(solution)/shard_map/attend/pallas_call | solution.py:693
  146.7 19.4 %attend.4 = (bf16[1024,768]{1,0:T(8,128)(2,1)S(1)}, bf16[1024,1536]{1,0:T(8,128)(2,1)}) custom-call(s32[7]{0:T(128)S(1)} %stack.82.refs_10_.place_ref, bf16[1024,768]{1,0:T(8,128)(2,1)S(1)} %project.2.q_ref, bf16[1024,1536]{1,0:T(8,128)(2,1)} %project.3.ka_ref.va_ref.k_ref.v_ref, ...), custom_call_target="tpu_custom_call", output_to_operand_aliasing={{0}: (6, {}), {1}: (7, {})} | custom-call | flops 17179869184 | bytes 8388608 | tf_op jit(solution)/shard_map/attend/pallas_call | solution.py:693
  171.8 19.2 %attend.5 = (bf16[1024,768]{1,0:T(8,128)(2,1)S(1)}, bf16[1024,1536]{1,0:T(8,128)(2,1)}) custom-call(s32[7]{0:T(128)S(1)} %stack.82.refs_10_.place_ref, bf16[1024,768]{1,0:T(8,128)(2,1)S(1)} %project.2.q_ref, bf16[1024,1536]{1,0:T(8,128)(2,1)} %project.3.ka_ref.va_ref.k_ref.v_ref, ...), custom_call_target="tpu_custom_call", output_to_operand_aliasing={{0}: (6, {}), {1}: (7, {})} | custom-call | flops 17179869184 | bytes 8388608 | tf_op jit(solution)/shard_map/attend/pallas_call | solution.py:693
  201.5 10.6 %stack_pieces.3.w_ref.wg_ref.wu_ref.wd_ref.refs_3_ = bf16[8,1248,768]{2,1,0:T(8,128)(2,1)} custom-call(s32[1]{0:T(128)} %bitcast.9.rep_ref, bf16[1248,768]{1,0:T(8,128)(2,1)} %pad_maximum_fusion.refs_0_, bf16[1248,768]{1,0:T(8,128)(2,1)} %collective-permute-done.14.refs_1_, bf16[1248,768]{1,0:T(8,128)(2,1)} %collective-permute-done.15.refs_2_, ...), custom_call_target="tpu_custom_call" | custom-call | bytes 30670848 | tf_op jit(solution)/shard_map/stack_pieces/pallas_call | solution.py:518
  219.1 5.4 out_norm.1
  225.7 25.8 %feed_forward.1 = (bf16[1024,3072]{1,0:T(8,128)(2,1)}, bf16[2,1024,3072]{2,1,0:T(8,128)(2,1)}, bf16[1024,768]{1,0:T(8,128)(2,1)}, f32[1024,768]{1,0:T(8,128)}) custom-call(f32[1024,768]{1,0:T(8,128)} %get-tuple-element.115.hat_ref.refs_0_, f32[2,768]{1,0:T(2,128)} %refs_2_.1, f32[2,768]{1,0:T(2,128)} %biases_ref.3, ...), custom_call_target="tpu_custom_call" | custom-call | flops 14495514624 | bytes 33030144 | tf_op jit(solution)/shard_map/feed_forward/pallas_call | solution.py:950
  255.2 6.1 norm_back.1
  265.3 5.8 away_columns.1
  279.0 5.4 collective-permute-start.24
  285.8 21.7 %feed_back.2 = (bf16[2,384,1536]{2,1,0:T(8,128)(2,1)}, bf16[2,384,1536]{2,1,0:T(8,128)(2,1)}, f32[1024,768]{1,0:T(8,128)}) custom-call(s32[4]{0:T(128)} %copy-done.51, f32[1024,768]{1,0:T(8,128)} %get-tuple-element.119.grad_ref, bf16[1024,768]{1,0:T(8,128)(2,1)} %copy-done.4, bf16[2,1024,3072]{2,1,0:T(8,128)(2,1)} %get-tuple-element.121.factor_ref, ...), custom_call_target="tpu_custom_call" | custom-call | flops 12079595520 | bytes 18087936 | tf_op jit(solution)/shard_map/feed_back/pallas_call | solution.py:1147
  310.9 9.3 %collective-permute-done.25 = bf16[512,768]{0,1:T(8,128)(2,1)} collective-permute-done((bf16[512,768]{0,1:T(8,128)(2,1)}, bf16[512,768]{0,1:T(8,128)(2,1)}, u32[]{:S(2)}, u32[]{:S(2)}) %collective-permute-start.25) | collective-permute-done | bytes 786464 | tf_op jit(solution)/shard_map/ppermute | solution.py:404
  323.2 5.7 keep_columns.1
  331.0 26.3 %feed_back.3 = (bf16[2,384,1536]{2,1,0:T(8,128)(2,1)}, bf16[2,384,1536]{2,1,0:T(8,128)(2,1)}, f32[1024,768]{1,0:T(8,128)}, bf16[1024,768]{1,0:T(8,128)(2,1)}, bf...) custom-call(s32[4]{0:T(128)} %copy-done.51, f32[1024,768]{1,0:T(8,128)} %get-tuple-element.127.grad_ref, ...), custom_call_target="tpu_custom_call" | custom-call | flops 12079595520 | bytes 18087936 | tf_op jit(solution)/shard_map/feed_back/pallas_call | solution.py:1147
  375.4 18.5 %attend_back.5 = (f32[1024,256]{1,0:T(8,128)S(1)}, bf16[1024,256]{1,0:T(8,128)(2,1)S(1)}, bf16[1024,256]{1,0:T(8,128)(2,1)S(1)}) custom-call(s32[7]{0:T(128)S(1)} %stack.82.refs_10_.place_ref, bf16[1024,1536]{1,0:T(8,128)(2,1)} %get-tuple-element.111.qx_ref, bf16[1024,1536]{1,0:T(8,128)(2,1)} %collective-permute-done.13.kb_ref.vb_ref.k_ref.v_ref, ...), custom_call_target="tpu_custom_call" | custom-call | flops 10737418240 | bytes 10485760 | tf_op jit(solution)/shard_map/attend_back/pallas_call | solution.py:820
  396.7 36.5 %attend_back.6 = (f32[1024,512]{1,0:T(8,128)}, bf16[1024,512]{1,0:T(8,128)(2,1)S(1)}, bf16[1024,512]{1,0:T(8,128)(2,1)S(1)}) custom-call(s32[7]{0:T(128)S(1)} %stack.82.refs_10_.place_ref, bf16[1024,1536]{1,0:T(8,128)(2,1)} %get-tuple-element.111.qx_ref, bf16[1024,1536]{1,0:T(8,128)(2,1)} %collective-permute-done.13.kb_ref.vb_ref.k_ref.v_ref, ...), custom_call_target="tpu_custom_call" | custom-call | flops 21474836480 | bytes 20971520 | tf_op jit(solution)/shard_map/attend_back/pallas_call | solution.py:820
  437.9 10.6 %collective-permute-done.32 = bf16[192,3840]{1,0:T(8,128)(2,1)} collective-permute-done((bf16[192,3840]{1,0:T(8,128)(2,1)}, bf16[192,3840]{1,0:T(8,128)(2,1)}, u32[]{:S(2)}, u32[]{:S(2)}) %collective-permute-start.32) | collective-permute-done | bytes 1474592 | tf_op jit(solution)/shard_map/ppermute | solution.py:404
  457.1 15.7 %attend_back.7.right_ref.refs_2_ = bf16[3,1024,256]{2,1,0:T(8,128)(2,1)S(1)} custom-call(s32[7]{0:T(128)S(1)} %stack.82.refs_10_.place_ref, bf16[1024,1536]{1,0:T(8,128)(2,1)} %get-tuple-element.111.qx_ref, bf16[1024,1536]{1,0:T(8,128)(2,1)} %project.3.ka_ref.va_ref.k_ref.v_ref, bf16[1024,1536]{1,0:T(8,128)(2,1)} %project.3.ka_ref.va_ref.k_ref.v_ref, ...), custom_call_target="tpu_custom_call" | custom-call | flops 10737418240 | bytes 10485760 | tf_op jit(solution)/shard_map/attend_back/pallas_call | solution.py:820
  475.5 16.7 %attend_back.8.right_ref.refs_0_ = bf16[3,1024,256]{2,1,0:T(8,128)(2,1)S(1)} custom-call(s32[7]{0:T(128)S(1)} %stack.82.refs_10_.place_ref, bf16[1024,1536]{1,0:T(8,128)(2,1)} %get-tuple-element.111.qx_ref, bf16[1024,1536]{1,0:T(8,128)(2,1)} %project.3.ka_ref.va_ref.k_ref.v_ref, bf16[1024,1536]{1,0:T(8,128)(2,1)} %project.3.ka_ref.va_ref.k_ref.v_ref, ...), custom_call_target="tpu_custom_call" | custom-call | flops 10737418240 | bytes 10485760 | tf_op jit(solution)/shard_map/attend_back/pallas_call | solution.py:820
  508.4 9.0 %collective-permute-done.56 = f32[4,768]{1,0:T(4,128)S(1)} collective-permute-done((f32[4,768]{1,0:T(4,128)S(1)}, f32[4,768]{1,0:T(4,128)S(1)}, u32[]{:S(2)}, u32[]{:S(2)}) %collective-permute-start.56) | collective-permute-done | bytes 12320 | tf_op jit(solution)/shard_map/ppermute | solution.py:404
  525.6 15.9 %attend_back.9.right_ref.refs_1_ = bf16[3,1024,256]{2,1,0:T(8,128)(2,1)S(1)} custom-call(s32[7]{0:T(128)S(1)} %stack.82.refs_10_.place_ref, bf16[1024,1536]{1,0:T(8,128)(2,1)} %get-tuple-element.111.qx_ref, bf16[1024,1536]{1,0:T(8,128)(2,1)} %project.3.ka_ref.va_ref.k_ref.v_ref, bf16[1024,1536]{1,0:T(8,128)(2,1)} %project.3.ka_ref.va_ref.k_ref.v_ref, ...), custom_call_target="tpu_custom_call" | custom-call | flops 10737418240 | bytes 10485760 | tf_op jit(solution)/shard_map/attend_back/pallas_call | solution.py:820
  544.3 7.2 %input_rows.1 = bf16[1024,768]{1,0:T(8,128)(2,1)S(1)} custom-call(bf16[3,1024,256]{2,1,0:T(8,128)(2,1)S(1)} %copy-done.3, bf16[3,1024,256]{2,1,0:T(8,128)(2,1)S(1)} %attend_back.9.right_ref.refs_1_, bf16[3,1024,256]{2,1,0:T(8,128)(2,1)} %copy-done.1, bf16[3,768,768]{2,1,0:T(8,128)(2,1)} %bitcast.123, bf16[3,768,768]{2,1,0:T(8,128)(2,1)} %bitcast.124, ...), custom_call_target="tpu_custom_call" | custom-call | flops 3623878656 | bytes 11010048 | tf_op jit(solution)/shard_map/input_rows/pallas_call | solution.py:1309
  552.7 8.5 %merge_main.1 = (f32[192,6144]{1,0:T(8,128)}, f32[192,768]{1,0:T(8,128)S(1)}, f32[8,512]{1,0:T(8,128)S(1)}) custom-call(s32[1]{0:T(128)} %bitcast.51.owner_ref, bf16[2,192,1536]{2,1,0:T(8,128)(2,1)} %fusion.fs_ref, bf16[2,192,1536]{2,1,0:T(8,128)(2,1)} %collective-permute-done.40.ff_ref, bf16[192,3840]{1,0:T(8,128)(2,1)} %add_convert_fusion.ss_ref.os_ref, ...), custom_call_target="tpu_custom_call" | custom-call | flops 61931520 | bytes 14450688 | tf_op jit(solution)/shard_map/merge_main/pallas_call | solution.py:1379
  588.3 5.5 pull.3
  606.7 10.7 %collective-permute-done.46 = bf16[192,768]{1,0:T(8,128)(2,1)S(1)} collective-permute-done((bf16[192,768]{1,0:T(8,128)(2,1)S(1)}, bf16[192,768]{1,0:T(8,128)(2,1)S(1)}, u32[]{:S(2)}, u32[]{:S(2)}) %collective-permute-start.46) | collective-permute-done | bytes 294944 | tf_op jit(solution)/shard_map/ppermute | solution.py:404
  623.0 5.7 collective-permute-done.48.refs_4_
  649.6 7.9 %new_errors.3 = (f32[1,192,6144]{2,1,0:T(8,128)}, f32[1,192,768]{2,1,0:T(8,128)}, f32[1,768,768]{2,1,0:T(8,128)}) custom-call(f32[8,1280]{1,0:T(8,128)S(1)} %get-tuple-element.177.basis_ref, f32[8,7680]{1,0:T(8,128)S(1)} %add_multiply_fusion.refs_0_.refs_1_.refs_2_, f32[8,7680]{1,0:T(8,128)S(1)} %add_multiply_fusion.refs_0_.refs_1_.refs_2_, ...), custom_call_target="tpu_custom_call" | custom-call | flops 92012544 | bytes 15335424 | tf_op jit(solution)/shard_map/new_errors/pallas_call | solution.py:1585
  (416 shorter events, 258.1 us)
Async XLA Ops:
  7.2 89.4 %all-gather.3.cloned.1.call-start = ((), (), s32[]{:S(2)}) async-start(), calls=%async_computation | async-start | bytes 2396160 | tf_op jit(solution)/shard_map/all_gather | solution.py:1685
  14.1 23.7 %collective-permute-start.5 = (bf16[288,192]{0,1:T(8,128)(2,1)}, bf16[288,192]{0,1:T(8,128)(2,1)}, u32[]{:S(2)}, u32[]{:S(2)}) collective-permute-start(bf16[288,192]{0,1:T(8,128)(2,1)} %get-tuple-element.285), channel_id=1, source_target_pairs={{0,3},{1,0},{2,1},{3,2},{4,7},{5,4},{6,5},{7,6},{8,11},{9,8},{10,9... | collective-permute-start | bytes 331784 | tf_op jit(solution)/shard_map/ppermute | solution.py:404
  15.2 43.3 %collective-permute-start = (s32[2]{0:T(128)S(1)}, s32[2]{0:T(128)S(1)}, u32[]{:S(2)}, u32[]{:S(2)}) collective-permute-start(s32[2]{0:T(128)S(1)} %copy-done.84), channel_id=1, source_target_pairs={{0,4},{1,5},{2,6},{3,7},{4,0},{5,1},{6,2},{7,3},{8,12},{9,13},{10,... | collective-permute-start | bytes 32 | tf_op jit(solution)/shard_map/ppermute | solution.py:404
  15.6 66.8 %collective-permute-start.1 = (bf16[512,768]{0,1:T(8,128)(2,1)S(1)}, bf16[512,768]{0,1:T(8,128)(2,1)}, u32[]{:S(2)}, u32[]{:S(2)}) collective-permute-start(bf16[512,768]{0,1:T(8,128)(2,1)S(1)} %bitcast.144), channel_id=1, source_target_pairs={{2,4},{3,5},{4,2},{5,3},{10,12},{11,13},{12,10},{13,11},{18,20},{1... | collective-permute-start | bytes 2359304 | tf_op jit(solution)/shard_map/ppermute | solution.py:404
  30.7 61.3 %collective-permute-start.2 = (bf16[512,768]{0,1:T(8,128)(2,1)}, bf16[512,768]{0,1:T(8,128)(2,1)}, u32[]{:S(2)}, u32[]{:S(2)}) collective-permute-start(bf16[512,768]{0,1:T(8,128)(2,1)} %bitcast.8), channel_id=1, source_target_pairs={{0,1},{1,0},{2,5},{3,4},{4,3},{5,2},{6,7},{7,6},{8,9},{9,8},{10,13... | collective-permute-start | bytes 2359304 | tf_op jit(solution)/shard_map/ppermute | solution.py:404
  54.2 42.4 %collective-permute-start.11 = (bf16[576,768]{1,0:T(8,128)(2,1)}, bf16[576,768]{1,0:T(8,128)(2,1)}, u32[]{:S(2)}, u32[]{:S(2)}) collective-permute-start(bf16[576,768]{1,0:T(8,128)(2,1)} %pad_maximum_fusion.7), channel_id=1, source_target_pairs={{0,4},{1,5},{2,6},{3,7},{4,0},{5,1},{6,2},{7,3},{8,12},{9,13},{10,... | collective-permute-start | bytes 2654216 | tf_op jit(solution)/shard_map/ppermute | solution.py:404
  64.3 32.3 %collective-permute-start.10 = (bf16[288,768]{1,0:T(8,128)(2,1)}, bf16[288,768]{1,0:T(8,128)(2,1)}, u32[]{:S(2)}, u32[]{:S(2)}) collective-permute-start(bf16[288,768]{1,0:T(8,128)(2,1)} %pad_maximum_fusion.12.refs_0_), channel_id=1, source_target_pairs={{0,4},{1,5},{2,6},{3,7},{4,0},{5,1},{6,2},{7,3},{8,12},{9,13},{10,... | collective-permute-start | bytes 1327112 | tf_op jit(solution)/shard_map/ppermute | solution.py:404
  67.1 29.5 %collective-permute-start.12 = (bf16[288,768]{1,0:T(8,128)(2,1)}, bf16[288,768]{1,0:T(8,128)(2,1)}, u32[]{:S(2)}, u32[]{:S(2)}) collective-permute-start(bf16[288,768]{1,0:T(8,128)(2,1)} %pad_maximum_fusion.13), channel_id=1, source_target_pairs={{0,4},{1,5},{2,6},{3,7},{4,0},{5,1},{6,2},{7,3},{8,12},{9,13},{10,... | collective-permute-start | bytes 1327112 | tf_op jit(solution)/shard_map/ppermute | solution.py:404
  120.9 45.2 %collective-permute-start.14 = (bf16[1248,768]{1,0:T(8,128)(2,1)}, bf16[1248,768]{1,0:T(8,128)(2,1)}, u32[]{:S(2)}, u32[]{:S(2)}) collective-permute-start(bf16[1248,768]{1,0:T(8,128)(2,1)} %pad_maximum_fusion.refs_0_), channel_id=1, source_target_pairs={{0,8},{1,9},{2,10},{3,11},{4,12},{5,13},{6,14},{7,15},{8,0},{9,1},... | collective-permute-start | bytes 5750792 | tf_op jit(solution)/shard_map/ppermute | solution.py:404
  122.4 44.2 %collective-permute-start.15 = (bf16[1248,768]{1,0:T(8,128)(2,1)}, bf16[1248,768]{1,0:T(8,128)(2,1)}, u32[]{:S(2)}, u32[]{:S(2)}) collective-permute-start(bf16[1248,768]{1,0:T(8,128)(2,1)} %pad_maximum_fusion.refs_0_), channel_id=1, source_target_pairs={{0,16},{1,17},{2,18},{3,19},{4,20},{5,21},{6,22},{7,23},{8,24},{9,... | collective-permute-start | bytes 5750792 | tf_op jit(solution)/shard_map/ppermute | solution.py:404
  167.9 27.1 %collective-permute-start.19 = (bf16[1248,768]{1,0:T(8,128)(2,1)}, bf16[1248,768]{1,0:T(8,128)(2,1)}, u32[]{:S(2)}, u32[]{:S(2)}) collective-permute-start(bf16[1248,768]{1,0:T(8,128)(2,1)} %collective-permute-done.14.refs_1_), channel_id=1, source_target_pairs={{0,4},{1,5},{2,6},{3,7},{4,0},{5,1},{6,2},{7,3},{8,12},{9,13},{10,... | collective-permute-start | bytes 5750792 | tf_op jit(solution)/shard_map/ppermute | solution.py:404
  169.2 25.8 %collective-permute-start.20 = (bf16[1248,768]{1,0:T(8,128)(2,1)}, bf16[1248,768]{1,0:T(8,128)(2,1)}, u32[]{:S(2)}, u32[]{:S(2)}) collective-permute-start(bf16[1248,768]{1,0:T(8,128)(2,1)} %collective-permute-done.15.refs_2_), channel_id=1, source_target_pairs={{0,4},{1,5},{2,6},{3,7},{4,0},{5,1},{6,2},{7,3},{8,12},{9,13},{10,... | collective-permute-start | bytes 5750792 | tf_op jit(solution)/shard_map/ppermute | solution.py:404
  169.8 23.2 %collective-permute-start.16 = (bf16[624,768]{1,0:T(8,128)(2,1)S(1)}, bf16[624,768]{1,0:T(8,128)(2,1)S(1)}, u32[]{:S(2)}, u32[]{:S(2)}) collective-permute-start(bf16[624,768]{1,0:T(8,128)(2,1)S(1)} %slice.95), channel_id=1, source_target_pairs={{0,8},{1,9},{2,10},{3,11},{4,12},{5,13},{6,14},{7,15},{8,0},{9,1},... | collective-permute-start | bytes 2875400 | tf_op jit(solution)/shard_map/ppermute | solution.py:404
  215.8 35.8 %collective-permute-start.22 = (bf16[512,768]{0,1:T(8,128)(2,1)}, bf16[512,768]{0,1:T(8,128)(2,1)}, u32[]{:S(2)}, u32[]{:S(2)}) collective-permute-start(bf16[512,768]{0,1:T(8,128)(2,1)} %bitcast.145), channel_id=1, source_target_pairs={{2,4},{3,5},{4,2},{5,3},{10,12},{11,13},{12,10},{13,11},{18,20},{1... | collective-permute-start | bytes 2359304 | tf_op jit(solution)/shard_map/ppermute | solution.py:404
  225.3 29.8 %collective-permute-start.23 = (bf16[512,768]{1,0:T(8,128)(2,1)}, bf16[512,768]{1,0:T(8,128)(2,1)S(1)}, u32[]{:S(2)}, u32[]{:S(2)}) collective-permute-start(bf16[512,768]{1,0:T(8,128)(2,1)} %get-tuple-element.272), channel_id=1, source_target_pairs={{0,1},{1,0},{2,5},{3,4},{4,3},{5,2},{6,7},{7,6},{8,9},{9,8},{10,13... | collective-permute-start | bytes 2359304 | tf_op jit(solution)/shard_map/ppermute | solution.py:404
  271.1 52.1 %collective-permute-start.26 = (bf16[768,1536]{1,0:T(8,128)(2,1)}, bf16[768,1536]{1,0:T(8,128)(2,1)}, u32[]{:S(2)}, u32[]{:S(2)}) collective-permute-start(bf16[768,1536]{1,0:T(8,128)(2,1)} %away_columns.1), channel_id=1, source_target_pairs={{0,4},{1,5},{2,6},{3,7},{4,0},{5,1},{6,2},{7,3},{8,12},{9,13},{10,... | collective-permute-start | bytes 7077896 | tf_op jit(solution)/shard_map/ppermute | solution.py:404
  279.0 31.9 %collective-permute-start.24 = (bf16[512,768]{0,1:T(8,128)(2,1)}, bf16[512,768]{0,1:T(8,128)(2,1)}, u32[]{:S(2)}, u32[]{:S(2)}) collective-permute-start(bf16[512,768]{0,1:T(8,128)(2,1)} %get-tuple-element.270), channel_id=1, source_target_pairs={{2,4},{3,5},{4,2},{5,3},{10,12},{11,13},{12,10},{13,11},{18,20},{1... | collective-permute-start | bytes 2359304 | tf_op jit(solution)/shard_map/ppermute | solution.py:404
  284.4 35.8 %collective-permute-start.25 = (bf16[512,768]{0,1:T(8,128)(2,1)}, bf16[512,768]{0,1:T(8,128)(2,1)}, u32[]{:S(2)}, u32[]{:S(2)}) collective-permute-start(bf16[512,768]{0,1:T(8,128)(2,1)} %get-tuple-element.271), channel_id=1, source_target_pairs={{0,1},{1,0},{2,5},{3,4},{4,3},{5,2},{6,7},{7,6},{8,9},{9,8},{10,13... | collective-permute-start | bytes 2359304 | tf_op jit(solution)/shard_map/ppermute | solution.py:404
  307.5 55.8 %collective-permute-start.30 = (bf16[2,384,1536]{2,1,0:T(8,128)(2,1)}, bf16[2,384,1536]{2,1,0:T(8,128)(2,1)}, u32[]{:S(2)}, u32[]{:S(2)}) collective-permute-start(bf16[2,384,1536]{2,1,0:T(8,128)(2,1)} %get-tuple-element.140), channel_id=1, source_target_pairs={{0,4},{1,5},{2,6},{3,7},{4,0},{5,1},{6,2},{7,3},{8,12},{9,13},{10,... | collective-permute-start | bytes 7077896 | tf_op jit(solution)/shard_map/ppermute | solution.py:404
  363.4 30.6 %collective-permute-start.29 = (bf16[768,768]{1,0:T(8,128)(2,1)}, bf16[768,768]{1,0:T(8,128)(2,1)S(1)}, u32[]{:S(2)}, u32[]{:S(2)}) collective-permute-start(bf16[768,768]{1,0:T(8,128)(2,1)} %copy-done.62), channel_id=1, source_target_pairs={{0,1},{1,0},{2,3},{3,2},{4,5},{5,4},{6,7},{7,6},{8,9},{9,8},{10,11... | collective-permute-start | bytes 3538952 | tf_op jit(solution)/shard_map/ppermute | solution.py:404
  366.4 66.7 %collective-permute-start.31 = (bf16[2,192,1536]{2,1,0:T(8,128)(2,1)}, bf16[2,192,1536]{2,1,0:T(8,128)(2,1)}, u32[]{:S(2)}, u32[]{:S(2)}) collective-permute-start(bf16[2,192,1536]{2,1,0:T(8,128)(2,1)} %fusion.2), channel_id=1, source_target_pairs={{0,1},{1,0},{2,3},{3,2},{4,5},{5,4},{6,7},{7,6},{8,9},{9,8},{10,11... | collective-permute-start | bytes 3538952 | tf_op jit(solution)/shard_map/ppermute | solution.py:404
  374.3 74.1 %collective-permute-start.32 = (bf16[192,3840]{1,0:T(8,128)(2,1)}, bf16[192,3840]{1,0:T(8,128)(2,1)}, u32[]{:S(2)}, u32[]{:S(2)}) collective-permute-start(bf16[192,3840]{1,0:T(8,128)(2,1)} %pad_maximum_fusion.6), channel_id=1, source_target_pairs={{0,1},{1,0},{2,3},{3,2},{4,5},{5,4},{6,7},{7,6},{8,9},{9,8},{10,11... | collective-permute-start | bytes 4423688 | tf_op jit(solution)/shard_map/ppermute | solution.py:404
  394.4 81.1 %collective-permute-start.35 = (bf16[768,768]{1,0:T(8,128)(2,1)S(1)}, bf16[768,768]{1,0:T(8,128)(2,1)S(1)}, u32[]{:S(2)}, u32[]{:S(2)}) collective-permute-start(bf16[768,768]{1,0:T(8,128)(2,1)S(1)} %add_convert_fusion.3.s_ref), channel_id=1, source_target_pairs={{2,5},{3,4},{4,3},{5,2},{10,13},{11,12},{12,11},{13,10},{18,21},{1... | collective-permute-start | bytes 3538952 | tf_op jit(solution)/shard_map/ppermute | solution.py:404
  433.7 41.8 %collective-permute-start.36 = (bf16[1024,512]{1,0:T(8,128)(2,1)S(1)}, bf16[1024,512]{1,0:T(8,128)(2,1)S(1)}, u32[]{:S(2)}, u32[]{:S(2)}) collective-permute-start(bf16[1024,512]{1,0:T(8,128)(2,1)S(1)} %get-tuple-element.148), channel_id=1, source_target_pairs={{0,4},{1,5},{2,6},{3,7},{4,0},{5,1},{6,2},{7,3},{8,12},{9,13},{10,... | collective-permute-start | bytes 3145736 | tf_op jit(solution)/shard_map/ppermute | solution.py:404
  448.5 75.8 %collective-permute-start.40 = (bf16[2,192,1536]{2,1,0:T(8,128)(2,1)}, bf16[2,192,1536]{2,1,0:T(8,128)(2,1)}, u32[]{:S(2)}, u32[]{:S(2)}) collective-permute-start(bf16[2,192,1536]{2,1,0:T(8,128)(2,1)} %fusion.fs_ref), channel_id=1, source_target_pairs={{2,5},{3,4},{4,3},{5,2},{10,13},{11,12},{12,11},{13,10},{18,21},{1... | collective-permute-start | bytes 3538952 | tf_op jit(solution)/shard_map/ppermute | solution.py:404
  454.0 70.3 %collective-permute-start.41 = (bf16[192,3840]{1,0:T(8,128)(2,1)}, bf16[192,3840]{1,0:T(8,128)(2,1)}, u32[]{:S(2)}, u32[]{:S(2)}) collective-permute-start(bf16[192,3840]{1,0:T(8,128)(2,1)} %add_convert_fusion.ss_ref.os_ref), channel_id=1, source_target_pairs={{2,5},{3,4},{4,3},{5,2},{10,13},{11,12},{12,11},{13,10},{18,21},{1... | collective-permute-start | bytes 4423688 | tf_op jit(solution)/shard_map/ppermute | solution.py:404
  475.5 41.9 %collective-permute-start.39 = (bf16[384,768]{1,0:T(8,128)(2,1)}, bf16[384,768]{1,0:T(8,128)(2,1)}, u32[]{:S(2)}, u32[]{:S(2)}) collective-permute-start(bf16[384,768]{1,0:T(8,128)(2,1)} %away_rows.5), channel_id=1, source_target_pairs={{0,4},{1,5},{2,6},{3,7},{4,0},{5,1},{6,2},{7,3},{8,12},{9,13},{10,... | collective-permute-start | bytes 1769480 | tf_op jit(solution)/shard_map/ppermute | solution.py:404
  496.1 24.6 %collective-permute-start.38 = (bf16[384,768]{1,0:T(8,128)(2,1)}, bf16[384,768]{1,0:T(8,128)(2,1)}, u32[]{:S(2)}, u32[]{:S(2)}) collective-permute-start(bf16[384,768]{1,0:T(8,128)(2,1)} %away_rows.6), channel_id=1, source_target_pairs={{0,4},{1,5},{2,6},{3,7},{4,0},{5,1},{6,2},{7,3},{8,12},{9,13},{10,... | collective-permute-start | bytes 1769480 | tf_op jit(solution)/shard_map/ppermute | solution.py:404
  568.9 33.0 %collective-permute-start.45 = (bf16[384,768]{1,0:T(8,128)(2,1)}, bf16[384,768]{1,0:T(8,128)(2,1)}, u32[]{:S(2)}, u32[]{:S(2)}) collective-permute-start(bf16[384,768]{1,0:T(8,128)(2,1)} %copy-done.48), channel_id=1, source_target_pairs={{0,4},{1,5},{2,6},{3,7},{4,0},{5,1},{6,2},{7,3},{8,12},{9,13},{10,... | collective-permute-start | bytes 1769480 | tf_op jit(solution)/shard_map/ppermute | solution.py:404
  569.1 53.9 %collective-permute-start.47 = (bf16[192,1536]{1,0:T(8,128)(2,1)}, bf16[192,1536]{1,0:T(8,128)(2,1)}, u32[]{:S(2)}, u32[]{:S(2)}) collective-permute-start(bf16[192,1536]{1,0:T(8,128)(2,1)} %add_convert_fusion.6.refs_0_.refs_2_), channel_id=1, source_target_pairs={{2,5},{3,4},{4,3},{5,2},{10,13},{11,12},{12,11},{13,10},{18,21},{1... | collective-permute-start | bytes 1769480 | tf_op jit(solution)/shard_map/ppermute | solution.py:404
  578.5 55.3 %collective-permute-start.42 = (bf16[512,768]{0,1:T(8,128)(2,1)}, bf16[512,768]{0,1:T(8,128)(2,1)}, u32[]{:S(2)}, u32[]{:S(2)}) collective-permute-start(bf16[512,768]{0,1:T(8,128)(2,1)} %copy.132), channel_id=1, source_target_pairs={{2,4},{3,5},{4,2},{5,3},{10,12},{11,13},{12,10},{13,11},{18,20},{1... | collective-permute-start | bytes 2359304 | tf_op jit(solution)/shard_map/ppermute | solution.py:404
  584.0 49.8 %collective-permute-start.43 = (bf16[512,768]{0,1:T(8,128)(2,1)}, bf16[512,768]{0,1:T(8,128)(2,1)}, u32[]{:S(2)}, u32[]{:S(2)}) collective-permute-start(bf16[512,768]{0,1:T(8,128)(2,1)} %copy.133), channel_id=1, source_target_pairs={{0,1},{1,0},{2,5},{3,4},{4,3},{5,2},{6,7},{7,6},{8,9},{9,8},{10,13... | collective-permute-start | bytes 2359304 | tf_op jit(solution)/shard_map/ppermute | solution.py:404
  (117 other events, 989.3 us)
Sparse Core Ops, SparseCore 0:
  11.6 66.6 all-gather.2
